TPU v7x, 32 devices: a whole 2x2x4 slice. The times are simulated.
32 devices in a mesh: prow: 8 (over z, y), pcol: 4 (over x, core).
Axes of the slice: x: 2, y: 2, z: 4, core: 2. Of those that a mesh axis runs over, the one named last changes fastest.
Arguments:
- anc_inverse: float32 [2048, 2048], P('prow', 'pcol'), as said below
- factor_one: float32 [2048, 2048], P('prow', 'pcol'), may hold values from -0.1875 to 0.1875
- pivot_one: float32 [8, 256, 256], P('pcol')
- factor_two: float32 [2048, 2048], P('prow', 'pcol'), may hold values from -0.25 to 0.25
- factor_link: float32 [16, 256, 128], P('pcol'), may hold values from -0.375 to 0.375
- pivot_two: float32 [16, 128, 128], P('pcol')
- pattern_one: int32 [8, 8], replicated, may hold values 0 or 1
- pattern_two: int32 [8, 16], replicated, may hold values 0 or 1
- parent_two: int32 [16], replicated, may hold values from 0 to 7, as said below
- size_one: int32 [8], replicated, may hold values from 64 to 256
- size_two: int32 [16], replicated, may hold values from 64 to 128
Outputs:
- inverse_one: float32 [2048, 2048], P('prow', 'pcol')
- diagonal_one: float32 [8, 256, 256], P('pcol')
- inverse_two: float32 [2048, 2048], P('prow', 'pcol')
- inverse_link: float32 [16, 256, 128], P('pcol')
- diagonal_two: float32 [16, 128, 128], P('pcol')
Inputs may be any that keep to these rules, and one draw needn't show every extreme that they name: anc_inverse is exactly symmetric. `parent_two`: the parent of a level-2 supernode K in [c * 4, (c + 1) * 4) lies in [c * 2, (c + 1) * 2); every level-1 supernode has exactly two children.
All inputs are finite; a program needn't handle non-finite values.
Results may differ from a plain program's by a relative error of at most 0.000078.
Values sent between devices are 32-bit elements; how exact they have to be, the bound alone decides.
No kernel may reach another device: no remote copies, remote signals or barrier semaphores. Data moves between devices by JAX's collectives and lax.ppermute only.
A program may use at most 128 MiB of HBM per device.

v0:
```python
import jax
import jax.numpy as jnp
from jax import lax
from jax.sharding import PartitionSpec as P

PRECISE = lax.Precision.HIGHEST


def block_repeat(blocks, height, width):
    return jnp.repeat(jnp.repeat(blocks, height, axis=0), width, axis=1)


def size_mask(sizes, width):
    return (jnp.arange(width)[None, :] < sizes[:, None]).astype(jnp.float32)


def folder(row_panel, keep, piece):
    return jnp.dot(row_panel, piece * keep, precision=PRECISE)


def on_device(
    anc_inverse,
    factor_one,
    pivot_one,
    factor_two,
    factor_link,
    pivot_two,
    pattern_one,
    pattern_two,
    parent_two,
    size_one,
    size_two,
):
    row_count = anc_inverse.shape[0]
    count_one = pivot_one.shape[0]
    count_two = pivot_two.shape[0]
    block_one = pivot_one.shape[1]
    block_two = pivot_two.shape[1]
    my_row = lax.axis_index("prow")
    my_col = lax.axis_index("pcol")
    row_panel = lax.all_gather(anc_inverse, "pcol", axis=1, tiled=True)
    first_pattern = pattern_one.astype(jnp.float32)
    total_one = first_pattern.shape[1]
    selector = (parent_two[None, :] == jnp.arange(total_one)[:, None]).astype(jnp.float32)
    second_pattern = pattern_two.astype(jnp.float32) * jnp.dot(
        first_pattern, selector, precision=PRECISE
    )
    pattern_mine = lax.dynamic_slice_in_dim(first_pattern, my_col * count_one, count_one, 1)
    second_mine = lax.dynamic_slice_in_dim(second_pattern, my_col * count_two, count_two, 1)
    columns_one = size_mask(
        lax.dynamic_slice_in_dim(size_one, my_col * count_one, count_one, 0), block_one
    )
    columns_two = size_mask(
        lax.dynamic_slice_in_dim(size_two, my_col * count_two, count_two, 0), block_two
    )
    parents_mine = (
        lax.dynamic_slice_in_dim(parent_two, my_col * count_two, count_two, 0) - my_col * count_one
    )
    linker = (parents_mine[None, :] == jnp.arange(count_one)[:, None]).astype(jnp.float32)
    blocks_one = block_repeat(pattern_mine, block_one, block_one)
    keep_one = blocks_one * columns_one.reshape(1, -1)
    blocks_two = block_repeat(second_mine, block_one, block_two)
    keep_two = blocks_two * columns_two.reshape(1, -1)
    row_start = my_row * row_count
    local_one = factor_one * lax.dynamic_slice_in_dim(keep_one, row_start, row_count, 0)
    local_two = factor_two * lax.dynamic_slice_in_dim(keep_two, row_start, row_count, 0)
    product_one = folder(
        row_panel, keep_one, lax.all_gather(factor_one, "prow", axis=0, tiled=True)
    )
    inverse_one = -product_one * lax.dynamic_slice_in_dim(blocks_one, row_start, row_count, 0)
    pivots_one = pivot_one * columns_one[:, :, None] * columns_one[:, None, :]
    local_three = local_one.reshape(row_count, count_one, block_one)
    inverse_three = inverse_one.reshape(row_count, count_one, block_one)
    correction = jnp.einsum("ija,ijb->jab", local_three, inverse_three, precision=PRECISE)
    diagonal_one = pivots_one - lax.psum(correction, "prow")
    product_two = folder(
        row_panel, keep_two, lax.all_gather(factor_two, "prow", axis=0, tiled=True)
    )
    link_rows = jnp.dot(linker.T, columns_one, precision=PRECISE)
    link = factor_link * link_rows[:, :, None] * columns_two[:, None, :]
    parent_cols = jnp.einsum("rjb,jk->rkb", inverse_three, linker, precision=PRECISE)
    near = jnp.einsum("rkb,kbd->rkd", parent_cols, link, precision=PRECISE).reshape(
        row_count, count_two * block_two
    )
    inverse_two = -(near + product_two) * lax.dynamic_slice_in_dim(
        blocks_two, row_start, row_count, 0
    )
    second_three = local_two.reshape(row_count, count_two, block_two)
    inverse_four = inverse_two.reshape(row_count, count_two, block_two)
    cross = jnp.einsum("rka,rkd->kad", parent_cols, second_three, precision=PRECISE)
    energy = jnp.einsum("rkd,rke->kde", second_three, inverse_four, precision=PRECISE)
    cross, energy = lax.psum((cross, energy), "prow")
    parent_diag = jnp.einsum("jab,jk->kab", diagonal_one, linker, precision=PRECISE)
    inverse_link = -(jnp.einsum("kab,kbd->kad", parent_diag, link, precision=PRECISE) + cross)
    pivots_two = pivot_two * columns_two[:, :, None] * columns_two[:, None, :]
    diagonal_two = (
        pivots_two - jnp.einsum("kbd,kbe->kde", link, inverse_link, precision=PRECISE) - energy
    )
    return (inverse_one, diagonal_one, inverse_two, inverse_link, diagonal_two)


def solution(mesh):
    return jax.shard_map(
        on_device,
        mesh=mesh,
        in_specs=(
            P("prow", "pcol"),
            P("prow", "pcol"),
            P("pcol", None, None),
            P("prow", "pcol"),
            P("pcol", None, None),
            P("pcol", None, None),
            P(),
            P(),
            P(),
            P(),
            P(),
        ),
        out_specs=(
            P("prow", "pcol"),
            P("pcol", None, None),
            P("prow", "pcol"),
            P("pcol", None, None),
            P("pcol", None, None),
        ),
        check_vma=False,
    )
```

profile of v0, /device:TPU:1, one launch (start us, length us, event | category | flops | bytes accessed | tf_op | source)
XLA Modules:
  0.0 294.2 jit_solution(16120043471021820972)
XLA Ops:
  7.2 0.7 all-gather.6.cloned.1.call-update
  7.9 0.0 all-gather.4.cloned.1.call-start
  7.9 2.0 copy.16
  10.0 0.0 all-gather.8.cloned.1.call-start
  10.1 2.0 copy.23
  12.1 0.0 all-reduce.3.cloned.1.call-start
  12.2 0.7 dynamic_slice.28
  12.9 0.1 fusion.40
  13.0 0.7 convert_element_type.48
  13.7 0.1 constant_dynamic-slice_fusion.1
  13.8 0.1 copy.17
  13.8 0.1 broadcast_bitcast_fusion.1
  13.9 0.7 dynamic_slice.32
  14.7 0.8 fusion.27
  15.5 0.1 constant_dynamic-slice_fusion
  15.6 0.1 copy.24
  15.7 0.1 broadcast_bitcast_fusion
  15.8 2.3 bitcast_multiply_fusion.1
  18.1 0.1 fusion.41
  18.2 0.3 bitcast_multiply_fusion
  18.5 0.1 dynamic-slice_subtract_fusion
  18.6 0.2 fusion.39
  18.8 1.6 dynamic-slice_multiply_fusion.1
  20.4 0.1 copy-done
  20.5 0.1 dynamic-slice_multiply_fusion
  20.6 14.1 %all-gather.6.cloned.1.call-done = f32[256,2048]{1,0:T(8,128)} async-done(((f32[256,512]{1,0:T(8,128)}), f32[256,2048]{1,0:T(8,128)}) %all-gather.6.cloned.1.call-update) | async-done | bytes 2097168 | tf_op jit(solution)/shard_map/all_gather | solution.py:41
  34.7 76.9 %all-gather.4.cloned.1.call-done = f32[2048,512]{0,1:T(8,128)} async-done(((f32[256,512]{0,1:T(8,128)}), f32[2048,512]{0,1:T(8,128)}) %all-gather.4.cloned.1.call-update) | async-done | bytes 4194320 | tf_op jit(solution)/shard_map/all_gather | solution.py:68
  111.5 0.5 broadcast_in_dim.9
  112.0 1.7 copy-done.2
  113.7 6.4 %fusion.23 = f32[256,512]{0,1:T(8,128)S(1)} fusion(f32[256,2048]{1,0:T(8,128)} %all-gather.6.cloned.1.call-done, f32[2048,512]{0,1:T(8,128)} %all-gather.4.cloned.1.call-done, f32[2048,512]{0,1:T(8,128)S(1)} %copy-done.2, f32[2048,512]{0,1:T(8,128)S(1)} %bitcast.63, s32[]{:T(128)S(6)} %select_n.7), kind=kOutput, calls=%fused_computation.15 | convolution fusion | flops 3222536192 | bytes 11534340 | tf_op jit(solution)/shard_map/dot_general | solution.py:18
  120.1 0.2 copy.20
  120.3 2.3 convolution_bitcast_fusion
  122.6 1.6 copy.26
  124.2 1.5 fusion.51
  125.7 1.9 fusion.52
  127.5 1.2 fusion.31
  128.7 58.6 %all-gather.8.cloned.1.call-done = f32[2048,512]{0,1:T(8,128)} async-done(((f32[256,512]{0,1:T(8,128)}), f32[2048,512]{0,1:T(8,128)}) %all-gather.8.cloned.1.call-update) | async-done | bytes 4194320 | tf_op jit(solution)/shard_map/all_gather | solution.py:77
  187.4 0.5 broadcast_in_dim.11
  187.9 1.7 copy-done.1
  189.6 6.6 %fusion.20 = f32[256,512]{0,1:T(8,128)S(1)} fusion(f32[256,512]{0,1:T(8,128)S(1)} %bitcast.67, f32[256,2048]{1,0:T(8,128)} %all-gather.6.cloned.1.call-done, f32[2048,512]{0,1:T(8,128)} %all-gather.8.cloned.1.call-done, f32[2048,512]{0,1:T(8,128)S(1)} %copy-done.1, f32[2048,512]{0,1:T(8,128)S(1)} %bitcast.62, s32[]{:T(128)S(6)} %select_n.7), kind=kOutput, calls=%fused_computation.14 | convolution fusion | flops 3222667264 | bytes 12058628 | tf_op jit(solution)/shard_map/dot_general | solution.py:18
  196.1 1.3 fusion.53
  197.5 1.0 copy.30
  198.5 1.0 copy.31
  199.5 81.2 %all-reduce.3.cloned.1.call-done = (f32[2,256,256]{2,1,0:T(8,128)}, f32[4,256,128]{2,1,0:T(8,128)}, f32[4,128,128]{2,1,0:T(8,128)}) async-done(((f32[2,256,256]{2,1,0:T(8,128)}, f32[4,256,128]{2,1,0:T(8,128)}, f32[4,128,128]{2,1,0:T(8,128)}), (f32[2,256,256]{2,1,0:T(8,128)}, f32[4,256,128]{2,1,0:T(8,128)}, f32[4,128,128]{2,1,0:T(8,128)})) %all-reduce.3.cloned.1.call-update) | async-done | bytes 1310736 | tf_op jit(solution)/shard_map/psum | solution.py:75
  280.7 1.2 multiply_subtract_fusion
  282.0 1.5 fusion.29
  283.5 2.3 fusion.4
  285.8 1.9 fusion.26
  (28 shorter events, 0.2 us)
Async XLA Ops:
  7.2 27.5 %all-gather.6.cloned.1.call-start = ((), (), s32[]{:S(2)}) async-start(), calls=%async_computation.1 | async-start | bytes 2621440 | tf_op jit(solution)/shard_map/all_gather | solution.py:41
  7.9 103.6 %all-gather.4.cloned.1.call-start = ((), (), s32[]{:S(2)}) async-start(), calls=%async_computation | async-start | bytes 4718592 | tf_op jit(solution)/shard_map/all_gather | solution.py:68
  10.0 177.4 %all-gather.8.cloned.1.call-start = ((), (), s32[]{:S(2)}) async-start(), calls=%async_computation.2 | async-start | bytes 4718592 | tf_op jit(solution)/shard_map/all_gather | solution.py:77
  12.1 268.6 %all-reduce.3.cloned.1.call-start = ((), (), s32[]{:S(2)}) async-start(), calls=%async_computation.3 | async-start | bytes 2621440 | tf_op jit(solution)/shard_map/psum | solution.py:75
  15.8 2.7 copy-start.11
  15.8 3.0 %copy-start.4 = (f32[256,512]{0,1:T(8,128)S(1)}, f32[256,512]{0,1:T(8,128)}, u32[]{:S(2)}) copy-start(f32[256,512]{0,1:T(8,128)} %copy.16) | copy-start | bytes 1572868
  15.8 4.7 %copy-start.3 = (f32[256,512]{0,1:T(8,128)S(1)}, f32[256,512]{0,1:T(8,128)}, u32[]{:S(2)}) copy-start(f32[256,512]{0,1:T(8,128)} %copy.23) | copy-start | bytes 1572868
  18.5 2.0 copy-start
  111.5 2.2 copy-start.2
  120.1 7.5 %copy-start.5 = (f32[4,256,128]{2,1,0:T(8,128)S(1)}, f32[4,256,128]{2,1,0:T(8,128)}, u32[]{:S(2)}) copy-start(f32[4,256,128]{2,1,0:T(8,128)} %param.15) | copy-start | bytes 1572868
  187.4 2.2 copy-start.1
  196.1 84.6 %copy-start.8 = (f32[2,256,256]{2,1,0:T(8,128)S(1)}, f32[2,256,256]{2,1,0:T(8,128)}, u32[]{:S(2)}) copy-start(f32[2,256,256]{2,1,0:T(8,128)} %param.13) | copy-start | bytes 1572868
  197.5 88.2 %copy-start.9 = (f32[4,128,128]{2,1,0:T(8,128)S(1)}, f32[4,128,128]{2,1,0:T(8,128)}, u32[]{:S(2)}) copy-start(f32[4,128,128]{2,1,0:T(8,128)} %param.16) | copy-start | bytes 786436
  280.7 5.1 %copy-start.10 = (f32[4,128,128]{2,1,0:T(8,128)S(1)}, f32[4,128,128]{2,1,0:T(8,128)}, u32[]{:S(2)}) copy-start(f32[4,128,128]{2,1,0:T(8,128)} %get-tuple-element.12) | copy-start | bytes 786436
  281.9 5.7 %copy-start.6 = (f32[2,256,256]{2,1,0:T(8,128)}, f32[2,256,256]{2,1,0:T(8,128)S(1)}, u32[]{:S(2)}) copy-start(f32[2,256,256]{2,1,0:T(8,128)S(1)} %multiply_subtract_fusion) | copy-start | bytes 1572868
  285.7 1.9 copy-start.7
Sparse Core Ops, SparseCore 0:
  9.6 25.0 all-gather.5
  37.3 74.1 all-gather.3
  114.1 73.1 all-gather.7
  197.6 83.0 all-reduce.2
where the time goes:
time: 295 us; the launch traced here: 294 us
  waiting for transfers between devices  231 us (78%)
  matrix products  27.8 us (9%)
  local copies, waits for them, and re-layouts  14.4 us (5%)
  between operations  14 us (5%)
  other arithmetic  6.41 us (2%)
    psum x1, waiting for transfers between devices, on_device(): diagonal_one = pivots_one - lax.psum(correction, 'prow')  81.2 us
    all_gather x1, waiting for transfers between devices, on_device(): lax.all_gather(factor_one, 'prow', axis=0, tiled=True)  76.9 us
    all_gather x1, waiting for transfers between devices, on_device(): lax.all_gather(factor_two, 'prow', axis=0, tiled=True)  58.6 us
    all_gather x1, waiting for transfers between devices, on_device(): row_panel = lax.all_gather(anc_inverse, 'pcol', axis=1, tiled=True)  14.1 us
    dot_general x2, matrix products, folder(): return jnp.dot(row_panel, piece * keep, precision=PRECISE)  12.9 us
    unnamed x33, local copies, waits for them, and re-layouts  9.83 us
  transfers between devices with their start and end apart: 4, of which 4 were waited for; matrix products, arithmetic and copies ran while one was open for 10% of the time, Pallas kernels for 0%

commit v1 on v0

v1 whole, which is shorter than its diff:
```python
import jax
import jax.numpy as jnp
from jax import lax
from jax.sharding import PartitionSpec as P

PRECISE = lax.Precision.HIGH
AXES = ("prow", "pcol")
CHUNKS = 1


def matmul(left, right, dims):
    return lax.dot_general(left, right, (dims, ((), ())), precision=PRECISE)


def size_mask(size, width):
    return (jnp.arange(width) < size).astype(jnp.float32)


def solution(mesh):
    rows_of, cols_of = mesh.shape["prow"], mesh.shape["pcol"]
    depth, wide = rows_of // 2, cols_of // 2

    def pairs(move):
        out = []
        for z in range(depth):
            for y in range(2):
                for x in range(wide):
                    for k in range(2):
                        to = move(z, y, x, k)
                        if to is not None:
                            a, b, c, d = to
                            out.append(
                                ((z * 2 + y) * cols_of + x * 2 + k, (a * 2 + b) * cols_of + c * 2 + d)
                            )
        return out

    to_worker = pairs(lambda z, y, x, k: (z, y, x, 1 - k) if k == y else (z, 1 - y, x, k))
    to_home = pairs(lambda z, y, x, k: (z, 1 - y, x, k) if k == y else (z, y, x, 1 - k))
    across = pairs(lambda z, y, x, k: None if k == y else (z, 1 - y, x, 1 - k))
    other_y = pairs(lambda z, y, x, k: (z, 1 - y, x, k))
    other_core = pairs(lambda z, y, x, k: (z, y, x, 1 - k))
    up = pairs(lambda z, y, x, k: (z + 1, y, x, k) if z + 1 < depth else None)
    down = pairs(lambda z, y, x, k: (z - 1, y, x, k) if z > 0 else None)

    def send(value, perm):
        return lax.ppermute(value, AXES, perm)

    def on_device(
        anc_inverse,
        factor_one,
        pivot_one,
        factor_two,
        factor_link,
        pivot_two,
        pattern_one,
        pattern_two,
        parent_two,
        size_one,
        size_two,
    ):
        rows, tile = anc_inverse.shape
        b1, b2 = pivot_one.shape[1], pivot_two.shape[1]
        my_row, my_col = lax.axis_index("prow"), lax.axis_index("pcol")
        z, y = my_row // 2, my_row % 2
        x, k = my_col // 2, my_col % 2
        stays = k == y
        base_one, base_two = my_col * 2, my_col * 4
        parents = [parent_two[base_two + i] - base_one for i in range(4)]
        place = [
            2 * parents[i] + sum([(parents[j] == parents[i]).astype(jnp.int32) for j in range(i)], 0)
            for i in range(4)
        ]
        order = [
            sum([jnp.where(place[i] == j, i, 0) for i in range(1, 4)], 0).astype(jnp.int32) for j in range(4)
        ]
        on_one = [pattern_one[my_row, base_one + f].astype(jnp.float32) for f in range(2)]
        on_two = [
            pattern_two[my_row, base_two + order[j]].astype(jnp.float32) * on_one[j // 2] for j in range(4)
        ]
        live_one = [size_mask(size_one[base_one + f], b1) for f in range(2)]
        live_two = [size_mask(size_two[base_two + order[j]], b2) for j in range(4)]
        first = [factor_one[:, f * b1 : (f + 1) * b1] * (on_one[f] * live_one[f])[None, :] for f in range(2)]
        second = [
            jnp.concatenate(
                [
                    lax.dynamic_slice_in_dim(factor_two, order[j] * b2, b2, 1) * (on_two[j] * live_two[j])[None, :]
                    for j in (2 * f, 2 * f + 1)
                ],
                axis=1,
            )
            for f in range(2)
        ]

        def fetch(mine):
            kept = jnp.where(y == 0, mine[0], mine[1])
            near = send(jnp.where(y == 0, mine[1], mine[0]), to_worker)
            far = send(kept, across)
            same = jnp.where(stays, kept, near)
            other = jnp.where(stays, near, far)
            return jnp.concatenate([jnp.where(y == 0, same, other), jnp.where(y == 0, other, same)], axis=0)

        w1 = fetch(first)
        beside = send(anc_inverse, other_y)

        def stacked(own, received):
            return jnp.concatenate(
                [jnp.where(y == 0, own, received), jnp.where(y == 0, received, own)], axis=0
            )

        tiles = [(x, stacked(anc_inverse, beside))]
        for s in range(1, wide):
            turn = pairs(lambda z, y, x, k: (z, y, (x + s) % wide, k))
            tiles.append(((x + wide - s) % wide, stacked(send(anc_inverse, turn), send(beside, turn))))
        panel = jnp.zeros((2 * rows, tile * cols_of), jnp.float32)
        for at, value in tiles:
            panel = lax.dynamic_update_slice(panel, value, (0, (at * 2 + k) * tile))
        for at, value in tiles:
            panel = lax.dynamic_update_slice(panel, send(value, other_core), (0, (at * 2 + 1 - k) * tile))
        w2 = fetch(second)
        span = 2 * rows
        parts = matmul(panel, w2, ((0,), (0,)))

        def part(d):
            d = jnp.clip(d, 0, depth - 1)
            return lax.dynamic_slice_in_dim(parts, d * span, span, 0)

        held = jnp.zeros(((3 * depth - 2) * span, b1), jnp.float32)
        held = lax.dynamic_update_slice(held, w1, ((z + depth - 1) * span, 0))
        from_below = from_above = w1
        for s in range(1, depth + 1):
            go_up, go_down = from_below, from_above
            if s > 1:
                go_up = go_up + jnp.where(z <= s - 2, part(z + 1 + depth - s), 0.0)
                back = depth - 1 - z
                go_down = go_down + jnp.where(back <= s - 2, part(z - 1 - depth + s), 0.0)
            from_below, from_above = send(go_up, up), send(go_down, down)
            if s < depth:
                held = lax.dynamic_update_slice(held, from_below, ((z - s + depth - 1) * span, 0))
                held = lax.dynamic_update_slice(held, from_above, ((z + s + depth - 1) * span, 0))
        whole = held[(depth - 1) * span : (2 * depth - 1) * span]
        y1 = matmul(panel, whole, ((1,), (0,)))
        y2 = part(z) + from_below + from_above
        grams = jnp.concatenate([matmul(w1, y1, ((0,), (0,))), matmul(y1, w2, ((0,), (0,)))], axis=1)
        energy = jnp.concatenate(
            [matmul(w2[:, j * b2 : (j + 1) * b2], y2[:, j * b2 : (j + 1) * b2], ((0,), (0,))) for j in range(2)],
            axis=1,
        )

        def total(value):
            step = 1
            while step < depth:
                value = value + send(value, pairs(lambda z, y, x, k: (z ^ step, y, x, k)))
                step *= 2
            return value

        def deliver(same, other):
            near = send(jnp.where(stays, other, same), to_home)
            far = send(other, across)
            mine = jnp.where(stays, same, far)
            return [jnp.where(y == 0, mine, near), jnp.where(y == 0, near, mine)]

        def split(value):
            lower, upper = value[:rows], value[rows:]
            return jnp.where(y == 0, lower, upper), jnp.where(y == 0, upper, lower)

        home_one = deliver(*split(y1))
        home_two = deliver(*split(y2))
        grams = total(grams)
        grams = deliver(grams, grams)
        energy = total(energy)
        energy = deliver(energy, energy)
        out_one, out_diag, out_two, out_link, out_last = [], [], [None] * 4, [None] * 4, [None] * 4
        for f in range(2):
            out_one.append(-home_one[f] * on_one[f])
            diag = pivot_one[f] * live_one[f][:, None] * live_one[f][None, :] + grams[f][:, :b1]
            out_diag.append(diag)
            for j in (2 * f, 2 * f + 1):
                cut = slice((j - 2 * f) * b2, (j - 2 * f + 1) * b2)
                link = (
                    lax.dynamic_index_in_dim(factor_link, order[j], 0, keepdims=False)
                    * live_one[f][:, None]
                    * live_two[j][None, :]
                )
                near = matmul(home_one[f], link, ((1,), (0,)))
                out_two[j] = on_two[j] * (near - home_two[f][:, cut])
                cross = grams[f][:, b1:][:, cut]
                down_link = cross - matmul(diag, link, ((1,), (0,)))
                out_link[j] = down_link
                pivot = (
                    lax.dynamic_index_in_dim(pivot_two, order[j], 0, keepdims=False)
                    * live_two[j][:, None]
                    * live_two[j][None, :]
                )
                out_last[j] = (
                    pivot
                    - matmul(link, down_link, ((0,), (0,)))
                    - matmul(cross, link, ((0,), (0,)))
                    + energy[f][:, cut]
                )

        def unsorted(values):
            stack = jnp.stack(values)
            return [lax.dynamic_index_in_dim(stack, place[i], 0, keepdims=False) for i in range(4)]

        return (
            jnp.concatenate(out_one, axis=1),
            jnp.stack(out_diag),
            jnp.concatenate(unsorted(out_two), axis=1),
            jnp.stack(unsorted(out_link)),
            jnp.stack(unsorted(out_last)),
        )

    return jax.shard_map(
        on_device,
        mesh=mesh,
        in_specs=(
            P("prow", "pcol"),
            P("prow", "pcol"),
            P("pcol", None, None),
            P("prow", "pcol"),
            P("pcol", None, None),
            P("pcol", None, None),
            P(),
            P(),
            P(),
            P(),
            P(),
        ),
        out_specs=(
            P("prow", "pcol"),
            P("pcol", None, None),
            P("prow", "pcol"),
            P("pcol", None, None),
            P("pcol", None, None),
        ),
        check_vma=False,
    )
```

time: 295 us -> 205 us (0.69)
  waiting for transfers between devices: 231 us -> 58.3 us
  starting transfers between devices: 0.16 us -> 54.6 us
  other arithmetic: 6.41 us -> 32.8 us
  local copies, waits for them, and re-layouts: 14.4 us -> 32.3 us
  matrix products: 27.8 us -> 16.9 us
  between operations: 14 us -> 8.37 us
    all_gather x3 -> x0, waiting for transfers between devices: 150 us -> none  [the longest x1 76.9 us: on_device(): lax.all_gather(factor_one, 'prow', axis=0, tiled=True)]
    psum x1 -> x0, waiting for transfers between devices: 81.2 us -> none  [on_device(): diagonal_one = pivots_one - lax.psum(correction, 'prow')]
    ppermute x0 -> x29, waiting for transfers between devices: none -> 58.3 us  [send(): return lax.ppermute(value, AXES, perm)]
    ppermute x0 -> x29, starting transfers between devices: none -> 54.6 us  [send(): return lax.ppermute(value, AXES, perm)]
    dot_general x12 -> x22, matrix products: 27.8 us -> 16.9 us  [matmul(): return lax.dot_general(left, right, (dims, ((), ())), precision=PRECISE)]
    add x0 -> x8, other arithmetic: none -> 8.89 us  [the longest x2 3.71 us: on_device(): go_down = go_down + jnp.where(back <= s - 2, part(z - 1 - depth + s), 0.0)]
    dynamic_update_slice x0 -> x5, local copies, waits for them, and re-layouts: none -> 7.94 us  [the longest x2 3.81 us: on_device(): lax.dynamic_update_slice(held, from_above, ((z + s + depth - 1) * span, 0))]
    concatenate x0 -> x7, other arithmetic: none -> 6.64 us  [the longest x2 3.22 us: stacked(): jnp.concatenate([jnp.where(y == 0, own, received), jnp.where(y == 0, rece...]
  transfers between devices with their start and end apart: 4 -> 29, of which waited for: 4 -> 12; matrix products, arithmetic and copies ran while one was open for 10% -> 29% of each run, Pallas kernels for 0% -> 0%
where the time goes in v1:
time: 205 us; the launch traced here: 203 us
  waiting for transfers between devices  58.3 us (28%)
  starting transfers between devices  54.6 us (27%)
  other arithmetic  32.8 us (16%)
  local copies, waits for them, and re-layouts  32.3 us (16%)
  matrix products  16.9 us (8%)
  between operations  8.37 us (4%)
    ppermute x29, waiting for transfers between devices, send(): return lax.ppermute(value, AXES, perm)  58.3 us
    ppermute x29, starting transfers between devices, send(): return lax.ppermute(value, AXES, perm)  54.6 us
    dot_general x22, matrix products, matmul(): return lax.dot_general(left, right, (dims, ((), ())), precision=PRECISE)  16.9 us
    unnamed x48, local copies, waits for them, and re-layouts  10.5 us
    convert_element_type x6, other arithmetic, size_mask(): return (jnp.arange(width) < size).astype(jnp.float32)  4.87 us
  transfers between devices with their start and end apart: 29, of which 12 were waited for; matrix products, arithmetic and copies ran while one was open for 29% of the time, Pallas kernels for 0%

profile of v1, /device:TPU:1, one launch (start us, length us, event | category | flops | bytes accessed | tf_op | source)
XLA Modules:
  0.0 203.3 jit_solution(7196832901463957606)
XLA Ops:
  0.7 1.3 copy.38
  2.0 2.1 %collective-permute-start = (f32[256,512]{0,1:T(8,128)S(1)}, f32[256,512]{0,1:T(8,128)S(1)}, u32[]{:S(2)}, u32[]{:S(2)}) collective-permute-start(f32[256,512]{0,1:T(8,128)S(1)} %copy.38), channel_id=1, source_target_pairs={{0,4},{1,5},{2,6},{3,7},{4,0},{5,1},{6,2},{7,3},{8,12},{9,13},{10,... | collective-permute-start | bytes 1572872 | tf_op jit(solution)/shard_map/ppermute | solution.py:46
  5.3 1.4 fusion.108
  9.4 1.5 fusion.105
  12.2 1.4 fusion.109
  17.2 4.5 %collective-permute-start.6 = (f32[256,256]{0,1:T(8,128)S(1)}, f32[256,256]{0,1:T(8,128)}, u32[]{:S(2)}, u32[]{:S(2)}) collective-permute-start(f32[256,256]{0,1:T(8,128)S(1)} %get-tuple-element.48), channel_id=1, source_target_pairs={{1,4},{3,6},{4,1},{6,3},{9,12},{11,14},{12,9},{14,11},{17,20},{19,... | collective-permute-start | bytes 786440 | tf_op jit(solution)/shard_map/ppermute | solution.py:46
  29.0 2.6 %broadcast_in_dim.13 = f32[512,2048]{0,1:T(8,128)} broadcast(f32[]{:T(128)} %constant.150.clone.1), dimensions={} | broadcast | bytes 4194308 | tf_op jit(solution)/shard_map/broadcast_in_dim | solution.py:114
  31.5 1.6 pad_maximum_fusion
  33.1 6.7 %collective-permute-done.2 = f32[256,512]{0,1:T(8,128)S(1)} collective-permute-done((f32[256,512]{0,1:T(8,128)S(1)}, f32[256,512]{0,1:T(8,128)S(1)}, u32[]{:S(2)}, u32[]{:S(2)}) %collective-permute-start.2) | collective-permute-done | bytes 524320 | tf_op jit(solution)/shard_map/ppermute | solution.py:46
  39.9 1.6 pad_maximum_fusion.1
  42.4 2.3 %collective-permute-start.10 = (f32[256,256]{0,1:T(8,128)S(1)}, f32[256,256]{0,1:T(8,128)S(1)}, u32[]{:S(2)}, u32[]{:S(2)}) collective-permute-start(f32[256,256]{0,1:T(8,128)S(1)} %get-tuple-element.63), channel_id=1, source_target_pairs={{1,4},{3,6},{4,1},{6,3},{9,12},{11,14},{12,9},{14,11},{17,20},{19,... | collective-permute-start | bytes 786440 | tf_op jit(solution)/shard_map/ppermute | solution.py:46
  45.9 3.0 %broadcast_in_dim.14 = f32[5120,256]{0,1:T(8,128)} broadcast(f32[]{:T(128)} %constant.150.clone.1), dimensions={} | broadcast | bytes 5242884 | tf_op jit(solution)/shard_map/broadcast_in_dim | solution.py:127
  49.8 3.2 %collective-permute-start.7 = (f32[512,256]{0,1:T(8,128)S(1)}, f32[512,256]{0,1:T(8,128)S(1)}, u32[]{:S(2)}, u32[]{:S(2)}) collective-permute-start(f32[512,256]{0,1:T(8,128)S(1)} %get-tuple-element.68), channel_id=1, source_target_pairs={{0,8},{1,9},{2,10},{3,11},{4,12},{5,13},{6,14},{7,15},{8,16},{9,17... | collective-permute-start | bytes 1572872 | tf_op jit(solution)/shard_map/ppermute | solution.py:46
  53.0 1.3 collective-permute-start.8
  57.6 4.0 %fusion.11 = f32[2048,256]{0,1:T(8,128)S(1)} fusion(f32[512,2048]{0,1:T(8,128)} %constant_dynamic-update-slice_fusion.7, f32[256,256]{0,1:T(8,128)S(1)} %get-tuple-element.44, f32[256,256]{0,1:T(8,128)S(1)} %get-tuple-element.43), kind=kOutput, calls=%fused_computation.45 | convolution fusion | flops 1610743808 | bytes 6815744 | tf_op jit(solution)/shard_map/dot_general | solution.py:12
  61.6 2.2 %collective-permute-done.7 = f32[512,256]{0,1:T(8,128)S(1)} collective-permute-done((f32[512,256]{0,1:T(8,128)S(1)}, f32[512,256]{0,1:T(8,128)S(1)}, u32[]{:S(2)}, u32[]{:S(2)}) %collective-permute-start.7) | collective-permute-done | bytes 524320 | tf_op jit(solution)/shard_map/ppermute | solution.py:46
  63.8 3.8 %collective-permute-done.8 = f32[512,256]{0,1:T(8,128)S(1)} collective-permute-done((f32[512,256]{0,1:T(8,128)S(1)}, f32[512,256]{0,1:T(8,128)S(1)}, u32[]{:S(2)}, u32[]{:S(2)}) %collective-permute-start.8) | collective-permute-done | bytes 524320 | tf_op jit(solution)/shard_map/ppermute | solution.py:46
  69.7 4.0 %collective-permute-start.11 = (f32[512,256]{0,1:T(8,128)}, f32[512,256]{0,1:T(8,128)}, u32[]{:S(2)}, u32[]{:S(2)}) collective-permute-start(f32[512,256]{0,1:T(8,128)} %get-tuple-element.28), channel_id=1, source_target_pairs={{0,8},{1,9},{2,10},{3,11},{4,12},{5,13},{6,14},{7,15},{8,16},{9,17... | collective-permute-start | bytes 1572872 | tf_op jit(solution)/shard_map/ppermute | solution.py:46
  73.7 1.3 collective-permute-start.12
  76.4 1.9 fusion.103
  78.2 1.9 constant_dynamic-update-slice_fusion.4
  80.1 2.7 %collective-permute-done.11 = f32[512,256]{0,1:T(8,128)} collective-permute-done((f32[512,256]{0,1:T(8,128)}, f32[512,256]{0,1:T(8,128)}, u32[]{:S(2)}, u32[]{:S(2)}) %collective-permute-start.11) | collective-permute-done | bytes 524320 | tf_op jit(solution)/shard_map/ppermute | solution.py:46
  82.9 4.6 %collective-permute-done.12 = f32[512,256]{0,1:T(8,128)} collective-permute-done((f32[512,256]{0,1:T(8,128)}, f32[512,256]{0,1:T(8,128)}, u32[]{:S(2)}, u32[]{:S(2)}) %collective-permute-start.12) | collective-permute-done | bytes 524320 | tf_op jit(solution)/shard_map/ppermute | solution.py:46
  87.5 2.5 %select_add_fusion.2 = (f32[512,256]{0,1:T(8,128)}, f32[512,256]{0,1:T(8,128)}, f32[5120,256]{0,1:T(8,128)}) fusion(f32[512,256]{0,1:T(8,128)} %collective-permute-done.12, f32[2048,256]{0,1:T(8,128)S(1)} %fusion.11, s32[]{:T(128)S(6)} %select_n.474, pred[]{:T(512)S(6)} %le.21, f32[512,256]{0,1:T(8,128)} %collective-permute-done.11, s32[]{:T(128)S(6)} %select_n.470, ...), kind=kLoop, calls=%fused_computation.40 | loop fusion | flops 524288 | bytes 3670030 | tf_op jit(solution)/shard_map/add | solution.py:135
  89.9 3.2 %collective-permute-start.13 = (f32[512,256]{0,1:T(8,128)}, f32[512,256]{0,1:T(8,128)}, u32[]{:S(2)}, u32[]{:S(2)}) collective-permute-start(f32[512,256]{0,1:T(8,128)} %get-tuple-element.26), channel_id=1, source_target_pairs={{0,8},{1,9},{2,10},{3,11},{4,12},{5,13},{6,14},{7,15},{8,16},{9,17... | collective-permute-start | bytes 1572872 | tf_op jit(solution)/shard_map/ppermute | solution.py:46
  94.3 1.3 collective-permute-start.14
  97.8 1.8 copy.75
  100.9 1.9 constant_dynamic-update-slice_fusion.2
  102.8 1.9 constant_dynamic-update-slice_fusion.1
  104.7 2.2 %collective-permute-done.14 = f32[512,256]{0,1:T(8,128)} collective-permute-done((f32[512,256]{0,1:T(8,128)}, f32[512,256]{0,1:T(8,128)}, u32[]{:S(2)}, u32[]{:S(2)}) %collective-permute-start.14) | collective-permute-done | bytes 524320 | tf_op jit(solution)/shard_map/ppermute | solution.py:46
  106.9 2.5 %select_add_fusion.1 = (f32[512,256]{0,1:T(8,128)}, f32[512,256]{0,1:T(8,128)}, f32[5120,256]{0,1:T(8,128)}) fusion(f32[512,256]{0,1:T(8,128)} %collective-permute-done.13, f32[2048,256]{0,1:T(8,128)S(1)} %fusion.11, s32[]{:T(128)S(6)} %select_n.490, pred[]{:T(512)S(6)} %le.22, f32[512,256]{0,1:T(8,128)} %collective-permute-done.14, s32[]{:T(128)S(6)} %select_n.493, ...), kind=kLoop, calls=%fused_computation.39 | loop fusion | flops 524288 | bytes 3670030 | tf_op jit(solution)/shard_map/add | solution.py:133
  109.4 4.7 %fusion = f32[512,256]{0,1:T(8,128)S(1)} fusion(f32[512,2048]{0,1:T(8,128)} %constant_dynamic-update-slice_fusion.7, f32[5120,256]{0,1:T(8,128)} %get-tuple-element.51), kind=kOutput, calls=%fused_computation | convolution fusion | flops 1610612736 | bytes 6815744 | tf_op jit(solution)/shard_map/dot_general | solution.py:12
  114.6 2.6 %collective-permute-start.21 = (f32[512,256]{0,1:T(8,128)}, f32[512,256]{0,1:T(8,128)}, u32[]{:S(2)}, u32[]{:S(2)}) collective-permute-start(f32[512,256]{0,1:T(8,128)} %get-tuple-element.23), channel_id=1, source_target_pairs={{0,8},{1,9},{2,10},{3,11},{4,12},{5,13},{6,14},{7,15},{8,16},{9,17... | collective-permute-start | bytes 1572872 | tf_op jit(solution)/shard_map/ppermute | solution.py:46
  117.2 1.3 collective-permute-start.22
  118.5 7.8 %collective-permute-start.15 = (f32[256,256]{0,1:T(8,128)S(1)}, f32[256,256]{0,1:T(8,128)S(1)}, u32[]{:S(2)}, u32[]{:S(2)}) collective-permute-start(f32[256,256]{0,1:T(8,128)S(1)} %get-tuple-element.22), channel_id=1, source_target_pairs={{1,4},{3,6},{4,1},{6,3},{9,12},{11,14},{12,9},{14,11},{17,20},{19,... | collective-permute-start | bytes 786440 | tf_op jit(solution)/shard_map/ppermute | solution.py:46
  127.6 2.4 %collective-permute-start.17 = (f32[256,512]{0,1:T(8,128)}, f32[256,512]{0,1:T(8,128)}, u32[]{:S(2)}, u32[]{:S(2)}) collective-permute-start(f32[256,512]{0,1:T(8,128)} %pad_maximum_fusion.5), channel_id=1, source_target_pairs={{0,8},{1,9},{2,10},{3,11},{4,12},{5,13},{6,14},{7,15},{8,0},{9,1},... | collective-permute-start | bytes 1572872 | tf_op jit(solution)/shard_map/ppermute | solution.py:46
  130.0 2.3 %collective-permute-done.15 = f32[256,256]{0,1:T(8,128)S(1)} collective-permute-done((f32[256,256]{0,1:T(8,128)S(1)}, f32[256,256]{0,1:T(8,128)S(1)}, u32[]{:S(2)}, u32[]{:S(2)}) %collective-permute-start.15) | collective-permute-done | bytes 262176 | tf_op jit(solution)/shard_map/ppermute | solution.py:46
  135.2 2.0 %copy.59 = f32[256,512]{1,0:T(8,128)} copy(f32[256,512]{0,1:T(8,128)} %pad_maximum_fusion.4) | data formatting | bytes 1048576
  137.3 1.4 add_add_fusion
  139.3 2.4 %collective-permute-start.25 = (f32[128,256]{1,0:T(8,128)S(1)}, f32[128,256]{1,0:T(8,128)S(1)}, u32[]{:S(2)}, u32[]{:S(2)}) collective-permute-start(f32[128,256]{1,0:T(8,128)S(1)} %pad_maximum_fusion.17), channel_id=1, source_target_pairs={{0,8},{1,9},{2,10},{3,11},{4,12},{5,13},{6,14},{7,15},{8,0},{9,1},... | collective-permute-start | bytes 393224 | tf_op jit(solution)/shard_map/ppermute | solution.py:46
  141.8 3.5 %collective-permute-start.23 = (f32[256,256]{0,1:T(8,128)S(1)}, f32[256,256]{0,1:T(8,128)S(1)}, u32[]{:S(2)}, u32[]{:S(2)}) collective-permute-start(f32[256,256]{0,1:T(8,128)S(1)} %get-tuple-element.16), channel_id=1, source_target_pairs={{1,4},{3,6},{4,1},{6,3},{9,12},{11,14},{12,9},{14,11},{17,20},{19,... | collective-permute-start | bytes 786440 | tf_op jit(solution)/shard_map/ppermute | solution.py:46
  147.6 2.1 %collective-permute-start.18 = (f32[256,512]{0,1:T(8,128)S(1)}, f32[256,512]{0,1:T(8,128)S(1)}, u32[]{:S(2)}, u32[]{:S(2)}) collective-permute-start(f32[256,512]{0,1:T(8,128)S(1)} %fusion.101), channel_id=1, source_target_pairs={{0,16},{1,17},{2,18},{3,19},{4,20},{5,21},{6,22},{7,23},{8,24},{9,... | collective-permute-start | bytes 1572872 | tf_op jit(solution)/shard_map/ppermute | solution.py:46
  149.7 16.2 %collective-permute-done.26 = f32[128,256]{1,0:T(8,128)S(1)} collective-permute-done((f32[128,256]{1,0:T(8,128)S(1)}, f32[128,256]{1,0:T(8,128)S(1)}, u32[]{:S(2)}, u32[]{:S(2)}) %collective-permute-start.26) | collective-permute-done | bytes 131104 | tf_op jit(solution)/shard_map/ppermute | solution.py:46
  165.9 3.8 %collective-permute-start.27 = (f32[128,256]{1,0:T(8,128)S(1)}, f32[128,256]{1,0:T(8,128)S(1)}, u32[]{:S(2)}, u32[]{:S(2)}) collective-permute-start(f32[128,256]{1,0:T(8,128)S(1)} %add.474), channel_id=1, source_target_pairs={{1,4},{3,6},{4,1},{6,3},{9,12},{11,14},{12,9},{14,11},{17,20},{19,... | collective-permute-start | bytes 393224 | tf_op jit(solution)/shard_map/ppermute | solution.py:46
  171.4 5.7 %collective-permute-done.18 = f32[256,512]{0,1:T(8,128)S(1)} collective-permute-done((f32[256,512]{0,1:T(8,128)S(1)}, f32[256,512]{0,1:T(8,128)S(1)}, u32[]{:S(2)}, u32[]{:S(2)}) %collective-permute-start.18) | collective-permute-done | bytes 524320 | tf_op jit(solution)/shard_map/ppermute | solution.py:46
  177.2 3.2 %collective-permute-start.19 = (f32[256,512]{0,1:T(8,128)S(1)}, f32[256,512]{0,1:T(8,128)S(1)}, u32[]{:S(2)}, u32[]{:S(2)}) collective-permute-start(f32[256,512]{0,1:T(8,128)S(1)} %add.454), channel_id=1, source_target_pairs={{1,4},{3,6},{4,1},{6,3},{9,12},{11,14},{12,9},{14,11},{17,20},{19,... | collective-permute-start | bytes 1572872 | tf_op jit(solution)/shard_map/ppermute | solution.py:46
  182.7 9.9 %collective-permute-done.19 = f32[256,512]{0,1:T(8,128)S(1)} collective-permute-done((f32[256,512]{0,1:T(8,128)S(1)}, f32[256,512]{0,1:T(8,128)S(1)}, u32[]{:S(2)}, u32[]{:S(2)}) %collective-permute-start.19) | collective-permute-done | bytes 524320 | tf_op jit(solution)/shard_map/ppermute | solution.py:46
  193.4 1.3 broadcast_select_fusion.2
  (152 shorter events, 44.1 us)
Async XLA Ops:
  0.6 21.2 %copy-start.10 = (f32[256,512]{1,0:T(8,128)S(1)}, f32[256,512]{1,0:T(8,128)}, u32[]{:S(2)}) copy-start(f32[256,512]{1,0:T(8,128)} %param.14) | copy-start | bytes 1572868
  0.6 21.4 %copy-start.13 = (s32[16]{0:T(128)S(1)}, s32[16]{0:T(128)}, u32[]{:S(2)}) copy-start(s32[16]{0:T(128)} %param.21) | copy-start | bytes 196
  2.0 26.0 %collective-permute-start = (f32[256,512]{0,1:T(8,128)S(1)}, f32[256,512]{0,1:T(8,128)S(1)}, u32[]{:S(2)}, u32[]{:S(2)}) collective-permute-start(f32[256,512]{0,1:T(8,128)S(1)} %copy.38), channel_id=1, source_target_pairs={{0,4},{1,5},{2,6},{3,7},{4,0},{5,1},{6,2},{7,3},{8,12},{9,13},{10,... | collective-permute-start | bytes 1572872 | tf_op jit(solution)/shard_map/ppermute | solution.py:46
  4.1 29.0 %collective-permute-start.1 = (f32[256,512]{0,1:T(8,128)S(1)}, f32[256,512]{0,1:T(8,128)S(1)}, u32[]{:S(2)}, u32[]{:S(2)}) collective-permute-start(f32[256,512]{0,1:T(8,128)S(1)} %copy.38), channel_id=1, source_target_pairs={{0,2},{1,3},{2,0},{3,1},{4,6},{5,7},{6,4},{7,5},{8,10},{9,11},{10,... | collective-permute-start | bytes 1572872 | tf_op jit(solution)/shard_map/ppermute | solution.py:46
  17.0 27.8 %collective-permute-start.5 = (f32[256,256]{0,1:T(8,128)}, f32[256,256]{0,1:T(8,128)}, u32[]{:S(2)}, u32[]{:S(2)}) collective-permute-start(f32[256,256]{0,1:T(8,128)} %get-tuple-element.47), channel_id=1, source_target_pairs={{0,1},{1,5},{2,3},{3,7},{4,0},{5,4},{6,2},{7,6},{8,9},{9,13},{10,1... | collective-permute-start | bytes 786440 | tf_op jit(solution)/shard_map/ppermute | solution.py:46
  17.2 27.6 %collective-permute-start.6 = (f32[256,256]{0,1:T(8,128)S(1)}, f32[256,256]{0,1:T(8,128)}, u32[]{:S(2)}, u32[]{:S(2)}) collective-permute-start(f32[256,256]{0,1:T(8,128)S(1)} %get-tuple-element.48), channel_id=1, source_target_pairs={{1,4},{3,6},{4,1},{6,3},{9,12},{11,14},{12,9},{14,11},{17,20},{19,... | collective-permute-start | bytes 786440 | tf_op jit(solution)/shard_map/ppermute | solution.py:46
  27.9 11.9 %collective-permute-start.2 = (f32[256,512]{0,1:T(8,128)S(1)}, f32[256,512]{0,1:T(8,128)S(1)}, u32[]{:S(2)}, u32[]{:S(2)}) collective-permute-start(f32[256,512]{0,1:T(8,128)S(1)} %collective-permute-done), channel_id=1, source_target_pairs={{0,2},{1,3},{2,0},{3,1},{4,6},{5,7},{6,4},{7,5},{8,10},{9,11},{10,... | collective-permute-start | bytes 1572872 | tf_op jit(solution)/shard_map/ppermute | solution.py:46
  33.1 22.3 %collective-permute-start.3 = (f32[512,512]{0,1:T(8,128)}, f32[512,512]{0,1:T(8,128)S(1)}, u32[]{:S(2)}, u32[]{:S(2)}) collective-permute-start(f32[512,512]{0,1:T(8,128)} %get-tuple-element.37), channel_id=1, source_target_pairs={{0,1},{1,0},{2,3},{3,2},{4,5},{5,4},{6,7},{7,6},{8,9},{9,8},{10,11... | collective-permute-start | bytes 3145736 | tf_op jit(solution)/shard_map/ppermute | solution.py:46
  41.5 14.9 %collective-permute-start.4 = (f32[512,512]{0,1:T(8,128)}, f32[512,512]{0,1:T(8,128)S(1)}, u32[]{:S(2)}, u32[]{:S(2)}) collective-permute-start(f32[512,512]{0,1:T(8,128)} %get-tuple-element.35), channel_id=1, source_target_pairs={{0,1},{1,0},{2,3},{3,2},{4,5},{5,4},{6,7},{7,6},{8,9},{9,8},{10,11... | collective-permute-start | bytes 3145736 | tf_op jit(solution)/shard_map/ppermute | solution.py:46
  42.4 12.0 %copy-start.8 = (f32[256,256]{0,1:T(8,128)}, f32[256,256]{0,1:T(8,128)S(1)}, u32[]{:S(2)}) copy-start(f32[256,256]{0,1:T(8,128)S(1)} %get-tuple-element.63) | copy-start | bytes 786436
  42.4 10.6 %collective-permute-start.10 = (f32[256,256]{0,1:T(8,128)S(1)}, f32[256,256]{0,1:T(8,128)S(1)}, u32[]{:S(2)}, u32[]{:S(2)}) collective-permute-start(f32[256,256]{0,1:T(8,128)S(1)} %get-tuple-element.63), channel_id=1, source_target_pairs={{1,4},{3,6},{4,1},{6,3},{9,12},{11,14},{12,9},{14,11},{17,20},{19,... | collective-permute-start | bytes 786440 | tf_op jit(solution)/shard_map/ppermute | solution.py:46
  44.8 9.6 %collective-permute-start.9 = (f32[256,256]{0,1:T(8,128)}, f32[256,256]{0,1:T(8,128)S(1)}, u32[]{:S(2)}, u32[]{:S(2)}) collective-permute-start(f32[256,256]{0,1:T(8,128)} %get-tuple-element.62), channel_id=1, source_target_pairs={{0,1},{1,5},{2,3},{3,7},{4,0},{5,4},{6,2},{7,6},{8,9},{9,13},{10,1... | collective-permute-start | bytes 786440 | tf_op jit(solution)/shard_map/ppermute | solution.py:46
  49.8 14.1 %collective-permute-start.7 = (f32[512,256]{0,1:T(8,128)S(1)}, f32[512,256]{0,1:T(8,128)S(1)}, u32[]{:S(2)}, u32[]{:S(2)}) collective-permute-start(f32[512,256]{0,1:T(8,128)S(1)} %get-tuple-element.68), channel_id=1, source_target_pairs={{0,8},{1,9},{2,10},{3,11},{4,12},{5,13},{6,14},{7,15},{8,16},{9,17... | collective-permute-start | bytes 1572872 | tf_op jit(solution)/shard_map/ppermute | solution.py:46
  53.0 1.3 copy-start.12
  53.0 14.7 %collective-permute-start.8 = (f32[512,256]{0,1:T(8,128)S(1)}, f32[512,256]{0,1:T(8,128)S(1)}, u32[]{:S(2)}, u32[]{:S(2)}) collective-permute-start(f32[512,256]{0,1:T(8,128)S(1)} %get-tuple-element.68), channel_id=1, source_target_pairs={{8,0},{9,1},{10,2},{11,3},{12,4},{13,5},{14,6},{15,7},{16,8},{17,9... | collective-permute-start | bytes 1572872 | tf_op jit(solution)/shard_map/ppermute | solution.py:46
  67.7 0.8 copy-start.7
  69.7 13.1 %collective-permute-start.11 = (f32[512,256]{0,1:T(8,128)}, f32[512,256]{0,1:T(8,128)}, u32[]{:S(2)}, u32[]{:S(2)}) collective-permute-start(f32[512,256]{0,1:T(8,128)} %get-tuple-element.28), channel_id=1, source_target_pairs={{0,8},{1,9},{2,10},{3,11},{4,12},{5,13},{6,14},{7,15},{8,16},{9,17... | collective-permute-start | bytes 1572872 | tf_op jit(solution)/shard_map/ppermute | solution.py:46
  73.7 13.8 %collective-permute-start.12 = (f32[512,256]{0,1:T(8,128)}, f32[512,256]{0,1:T(8,128)}, u32[]{:S(2)}, u32[]{:S(2)}) collective-permute-start(f32[512,256]{0,1:T(8,128)} %get-tuple-element.27), channel_id=1, source_target_pairs={{8,0},{9,1},{10,2},{11,3},{12,4},{13,5},{14,6},{15,7},{16,8},{17,9... | collective-permute-start | bytes 1572872 | tf_op jit(solution)/shard_map/ppermute | solution.py:46
  89.9 12.9 %collective-permute-start.13 = (f32[512,256]{0,1:T(8,128)}, f32[512,256]{0,1:T(8,128)}, u32[]{:S(2)}, u32[]{:S(2)}) collective-permute-start(f32[512,256]{0,1:T(8,128)} %get-tuple-element.26), channel_id=1, source_target_pairs={{0,8},{1,9},{2,10},{3,11},{4,12},{5,13},{6,14},{7,15},{8,16},{9,17... | collective-permute-start | bytes 1572872 | tf_op jit(solution)/shard_map/ppermute | solution.py:46
  94.3 12.6 %collective-permute-start.14 = (f32[512,256]{0,1:T(8,128)}, f32[512,256]{0,1:T(8,128)}, u32[]{:S(2)}, u32[]{:S(2)}) collective-permute-start(f32[512,256]{0,1:T(8,128)} %get-tuple-element.25), channel_id=1, source_target_pairs={{8,0},{9,1},{10,2},{11,3},{12,4},{13,5},{14,6},{15,7},{16,8},{17,9... | collective-permute-start | bytes 1572872 | tf_op jit(solution)/shard_map/ppermute | solution.py:46
  114.5 12.2 %copy-start.4 = (f32[256,256]{0,1:T(8,128)}, f32[256,256]{0,1:T(8,128)S(1)}, u32[]{:S(2)}) copy-start(f32[256,256]{0,1:T(8,128)S(1)} %fusion.102) | copy-start | bytes 786436
  114.6 22.7 %collective-permute-start.21 = (f32[512,256]{0,1:T(8,128)}, f32[512,256]{0,1:T(8,128)}, u32[]{:S(2)}, u32[]{:S(2)}) collective-permute-start(f32[512,256]{0,1:T(8,128)} %get-tuple-element.23), channel_id=1, source_target_pairs={{0,8},{1,9},{2,10},{3,11},{4,12},{5,13},{6,14},{7,15},{8,16},{9,17... | collective-permute-start | bytes 1572872 | tf_op jit(solution)/shard_map/ppermute | solution.py:46
  117.2 20.1 %collective-permute-start.22 = (f32[512,256]{0,1:T(8,128)}, f32[512,256]{0,1:T(8,128)}, u32[]{:S(2)}, u32[]{:S(2)}) collective-permute-start(f32[512,256]{0,1:T(8,128)} %get-tuple-element.24), channel_id=1, source_target_pairs={{8,0},{9,1},{10,2},{11,3},{12,4},{13,5},{14,6},{15,7},{16,8},{17,9... | collective-permute-start | bytes 1572872 | tf_op jit(solution)/shard_map/ppermute | solution.py:46
  118.5 13.8 %collective-permute-start.15 = (f32[256,256]{0,1:T(8,128)S(1)}, f32[256,256]{0,1:T(8,128)S(1)}, u32[]{:S(2)}, u32[]{:S(2)}) collective-permute-start(f32[256,256]{0,1:T(8,128)S(1)} %get-tuple-element.22), channel_id=1, source_target_pairs={{1,4},{3,6},{4,1},{6,3},{9,12},{11,14},{12,9},{14,11},{17,20},{19,... | collective-permute-start | bytes 786440 | tf_op jit(solution)/shard_map/ppermute | solution.py:46
  126.3 7.2 %collective-permute-start.16 = (f32[256,256]{0,1:T(8,128)S(1)}, f32[256,256]{0,1:T(8,128)S(1)}, u32[]{:S(2)}, u32[]{:S(2)}) collective-permute-start(f32[256,256]{0,1:T(8,128)S(1)} %get-tuple-element.21), channel_id=1, source_target_pairs={{0,4},{1,0},{2,6},{3,2},{4,5},{5,1},{6,7},{7,3},{8,12},{9,8},{10,1... | collective-permute-start | bytes 786440 | tf_op jit(solution)/shard_map/ppermute | solution.py:46
  126.7 8.5 %copy-start.5 = (f32[256,256]{0,1:T(8,128)}, f32[256,256]{0,1:T(8,128)S(1)}, u32[]{:S(2)}) copy-start(f32[256,256]{0,1:T(8,128)S(1)} %fusion.10) | copy-start | bytes 786436
  127.6 18.8 %collective-permute-start.17 = (f32[256,512]{0,1:T(8,128)}, f32[256,512]{0,1:T(8,128)}, u32[]{:S(2)}, u32[]{:S(2)}) collective-permute-start(f32[256,512]{0,1:T(8,128)} %pad_maximum_fusion.5), channel_id=1, source_target_pairs={{0,8},{1,9},{2,10},{3,11},{4,12},{5,13},{6,14},{7,15},{8,0},{9,1},... | collective-permute-start | bytes 1572872 | tf_op jit(solution)/shard_map/ppermute | solution.py:46
  137.3 9.1 %copy-start.6 = (f32[256,256]{0,1:T(8,128)S(1)}, f32[256,256]{0,1:T(8,128)}, u32[]{:S(2)}) copy-start(f32[256,256]{0,1:T(8,128)} %copy-done.5) | copy-start | bytes 786436
  137.3 32.6 %copy-start = (f32[4,256,128]{2,1,0:T(8,128)S(1)}, f32[4,256,128]{2,1,0:T(8,128)}, u32[]{:S(2)}) copy-start(f32[4,256,128]{2,1,0:T(8,128)} %param.15) | copy-start | bytes 1572868
  137.3 32.6 %copy-start.3 = (f32[256,256]{0,1:T(8,128)S(1)}, f32[256,256]{0,1:T(8,128)}, u32[]{:S(2)}) copy-start(f32[256,256]{0,1:T(8,128)} %get-tuple-element.18) | copy-start | bytes 786436
  138.7 31.9 %copy-start.2 = (f32[256,256]{0,1:T(8,128)S(1)}, f32[256,256]{0,1:T(8,128)}, u32[]{:S(2)}) copy-start(f32[256,256]{0,1:T(8,128)} %get-tuple-element.34) | copy-start | bytes 786436
  138.7 31.9 %copy-start.14 = (f32[128]{0:T(128)S(1)}, f32[128]{0:T(128)}, u32[]{:S(2)}) copy-start(f32[128]{0:T(128)} %compare_convert_fusion.1) | copy-start | bytes 1540
  139.0 32.0 %copy-start.16 = (f32[128]{0:T(128)S(1)}, f32[128]{0:T(128)}, u32[]{:S(2)}) copy-start(f32[128]{0:T(128)} %compare_convert_fusion) | copy-start | bytes 1540
  139.3 6.6 %collective-permute-start.25 = (f32[128,256]{1,0:T(8,128)S(1)}, f32[128,256]{1,0:T(8,128)S(1)}, u32[]{:S(2)}, u32[]{:S(2)}) collective-permute-start(f32[128,256]{1,0:T(8,128)S(1)} %pad_maximum_fusion.17), channel_id=1, source_target_pairs={{0,8},{1,9},{2,10},{3,11},{4,12},{5,13},{6,14},{7,15},{8,0},{9,1},... | collective-permute-start | bytes 393224 | tf_op jit(solution)/shard_map/ppermute | solution.py:46
  141.8 27.9 %collective-permute-start.23 = (f32[256,256]{0,1:T(8,128)S(1)}, f32[256,256]{0,1:T(8,128)S(1)}, u32[]{:S(2)}, u32[]{:S(2)}) collective-permute-start(f32[256,256]{0,1:T(8,128)S(1)} %get-tuple-element.16), channel_id=1, source_target_pairs={{1,4},{3,6},{4,1},{6,3},{9,12},{11,14},{12,9},{14,11},{17,20},{19,... | collective-permute-start | bytes 786440 | tf_op jit(solution)/shard_map/ppermute | solution.py:46
  145.3 24.4 %collective-permute-start.24 = (f32[256,256]{0,1:T(8,128)S(1)}, f32[256,256]{0,1:T(8,128)S(1)}, u32[]{:S(2)}, u32[]{:S(2)}) collective-permute-start(f32[256,256]{0,1:T(8,128)S(1)} %get-tuple-element.15), channel_id=1, source_target_pairs={{0,4},{1,0},{2,6},{3,2},{4,5},{5,1},{6,7},{7,3},{8,12},{9,8},{10,1... | collective-permute-start | bytes 786440 | tf_op jit(solution)/shard_map/ppermute | solution.py:46
  146.0 19.9 %collective-permute-start.26 = (f32[128,256]{1,0:T(8,128)S(1)}, f32[128,256]{1,0:T(8,128)S(1)}, u32[]{:S(2)}, u32[]{:S(2)}) collective-permute-start(f32[128,256]{1,0:T(8,128)S(1)} %fusion.84), channel_id=1, source_target_pairs={{0,16},{1,17},{2,18},{3,19},{4,20},{5,21},{6,22},{7,23},{8,24},{9,... | collective-permute-start | bytes 393224 | tf_op jit(solution)/shard_map/ppermute | solution.py:46
  147.6 29.5 %collective-permute-start.18 = (f32[256,512]{0,1:T(8,128)S(1)}, f32[256,512]{0,1:T(8,128)S(1)}, u32[]{:S(2)}, u32[]{:S(2)}) collective-permute-start(f32[256,512]{0,1:T(8,128)S(1)} %fusion.101), channel_id=1, source_target_pairs={{0,16},{1,17},{2,18},{3,19},{4,20},{5,21},{6,22},{7,23},{8,24},{9,... | collective-permute-start | bytes 1572872 | tf_op jit(solution)/shard_map/ppermute | solution.py:46
  165.9 15.8 %collective-permute-start.27 = (f32[128,256]{1,0:T(8,128)S(1)}, f32[128,256]{1,0:T(8,128)S(1)}, u32[]{:S(2)}, u32[]{:S(2)}) collective-permute-start(f32[128,256]{1,0:T(8,128)S(1)} %add.474), channel_id=1, source_target_pairs={{1,4},{3,6},{4,1},{6,3},{9,12},{11,14},{12,9},{14,11},{17,20},{19,... | collective-permute-start | bytes 393224 | tf_op jit(solution)/shard_map/ppermute | solution.py:46
  169.7 12.0 %collective-permute-start.28 = (f32[128,256]{1,0:T(8,128)S(1)}, f32[128,256]{1,0:T(8,128)}, u32[]{:S(2)}, u32[]{:S(2)}) collective-permute-start(f32[128,256]{1,0:T(8,128)S(1)} %add.474), channel_id=1, source_target_pairs={{0,4},{1,0},{2,6},{3,2},{4,5},{5,1},{6,7},{7,3},{8,12},{9,8},{10,1... | collective-permute-start | bytes 393224 | tf_op jit(solution)/shard_map/ppermute | solution.py:46
  177.2 15.4 %collective-permute-start.19 = (f32[256,512]{0,1:T(8,128)S(1)}, f32[256,512]{0,1:T(8,128)S(1)}, u32[]{:S(2)}, u32[]{:S(2)}) collective-permute-start(f32[256,512]{0,1:T(8,128)S(1)} %add.454), channel_id=1, source_target_pairs={{1,4},{3,6},{4,1},{6,3},{9,12},{11,14},{12,9},{14,11},{17,20},{19,... | collective-permute-start | bytes 1572872 | tf_op jit(solution)/shard_map/ppermute | solution.py:46
  180.3 13.1 %collective-permute-start.20 = (f32[256,512]{0,1:T(8,128)S(1)}, f32[256,512]{0,1:T(8,128)}, u32[]{:S(2)}, u32[]{:S(2)}) collective-permute-start(f32[256,512]{0,1:T(8,128)S(1)} %add.454), channel_id=1, source_target_pairs={{0,4},{1,0},{2,6},{3,2},{4,5},{5,1},{6,7},{7,3},{8,12},{9,8},{10,1... | collective-permute-start | bytes 1572872 | tf_op jit(solution)/shard_map/ppermute | solution.py:46
  180.4 15.1 %copy-start.1 = (f32[1,256,256]{1,2,0:T(8,128)S(1)}, f32[1,256,256]{1,2,0:T(8,128)}, u32[]{:S(2)}) copy-start(f32[1,256,256]{1,2,0:T(8,128)} %copy.75) | copy-start | bytes 786436
  181.7 16.0 %copy-start.11 = (f32[4,128,128]{2,1,0:T(8,128)S(1)}, f32[4,128,128]{2,1,0:T(8,128)}, u32[]{:S(2)}) copy-start(f32[4,128,128]{2,1,0:T(8,128)} %param.16) | copy-start | bytes 786436
  182.7 16.3 %copy-start.15 = (f32[128]{0:T(128)S(1)}, f32[128]{0:T(128)}, u32[]{:S(2)}) copy-start(f32[128]{0:T(128)} %compare_convert_fusion.1) | copy-start | bytes 1540
  182.7 16.7 %copy-start.17 = (f32[128]{0:T(128)S(1)}, f32[128]{0:T(128)}, u32[]{:S(2)}) copy-start(f32[128]{0:T(128)} %compare_convert_fusion) | copy-start | bytes 1540
  192.6 0.8 copy-start.9

commit v2 on v0

v2 whole, which is shorter than its diff:
```python
import functools

import jax
import jax.numpy as jnp
from jax import lax
from jax.experimental import pallas as pl
from jax.experimental.pallas import tpu as pltpu
from jax.sharding import PartitionSpec as P

AXES = ("prow", "pcol")
F32 = jnp.float32
VMEM = pl.BlockSpec(memory_space=pltpu.VMEM)
SMEM = pl.BlockSpec(memory_space=pltpu.SMEM)
NN = ((1,), (0,))
NT = ((1,), (1,))
TN = ((0,), (0,))


def halves(value):
    high = value.astype(jnp.bfloat16)
    return high, (value - high.astype(F32)).astype(jnp.bfloat16)


def dot3(left, right, dims):
    def one(a, b):
        return lax.dot_general(a, b, (dims, ((), ())), preferred_element_type=F32)

    return one(left[0], right[0]) + (one(left[0], right[1]) + one(left[1], right[0]))


def place_of():
    my_row, my_col = lax.axis_index("prow"), lax.axis_index("pcol")
    return my_row // 2, my_row % 2, my_col // 2, my_col % 2


def family_order(parent_ref, my_col):
    parents = [parent_ref[my_col * 4 + i] - my_col * 2 for i in range(4)]
    place = []
    for i in range(4):
        seen = jnp.int32(0)
        for j in range(i):
            seen += jnp.where(parents[j] == parents[i], 1, 0)
        place.append(2 * parents[i] + seen)
    order = []
    for j in range(4):
        found = jnp.int32(0)
        for i in range(1, 4):
            found += jnp.where(place[i] == j, i, 0)
        order.append(found)
    return order


def below(size, shape, axis):
    return (lax.broadcasted_iota(jnp.int32, shape, axis) < size).astype(F32)


def pick(values, index):
    out = values[0]
    for i in range(1, len(values)):
        out = jnp.where(index == i, values[i], out)
    return out


def pack_one(block, factor_ref, pattern_ref, size_ref, kept_ref, give_ref):
    my_row, my_col = lax.axis_index("prow"), lax.axis_index("pcol")
    y = my_row % 2
    for out_ref, f in ((kept_ref, y), (give_ref, 1 - y)):
        values = factor_ref[:, pl.ds(pl.multiple_of(f * block, 128), block)]
        on = pattern_ref[my_row, my_col * 2 + f].astype(F32)
        keep = below(size_ref[my_col * 2 + f], values.shape, 1) * on
        out_ref[...] = (values * keep).T


def pack_two(
    block, factor_ref, first_ref, second_ref, parent_ref, size_ref, kept_ref, give_ref
):
    my_row, my_col = lax.axis_index("prow"), lax.axis_index("pcol")
    y = my_row % 2
    order = family_order(parent_ref, my_col)
    for out_ref, f in ((kept_ref, y), (give_ref, 1 - y)):
        for i in range(2):
            child = pick([order[i], order[2 + i]], f)
            values = factor_ref[:, pl.ds(pl.multiple_of(child * block, 128), block)]
            on = first_ref[my_row, my_col * 2 + f] * second_ref[my_row, my_col * 4 + child]
            keep = below(size_ref[my_col * 4 + child], values.shape, 1) * on.astype(F32)
            out_ref[i * block : (i + 1) * block, :] = (values * keep).T


def join(kept_ref, near_ref, far_ref, out_ref):
    _, y, _, k = place_of()
    rows = kept_ref.shape[1]

    @pl.when(k == y)
    def _():
        out_ref[:, :rows] = kept_ref[...]
        out_ref[:, rows:] = near_ref[...]

    @pl.when(k != y)
    def _():
        out_ref[:, :rows] = near_ref[...]
        out_ref[:, rows:] = far_ref[...]


def partial_products(wide, w2_ref, *refs):
    tiles, (parts_ref, high_ref, low_ref) = refs[:-3], refs[-3:]
    _, y, x, k = place_of()
    rows, tile = tiles[0].shape
    w2 = halves(w2_ref[...])
    same = (w2[0][:, :rows], w2[1][:, :rows])
    other = (w2[0][:, rows:], w2[1][:, rows:])
    for s in range(wide):
        for c in range(2):
            top, bottom = tiles[(s * 2 + c) * 2], tiles[(s * 2 + c) * 2 + 1]
            first = (lax.rem(x + wide - s, wide) * 2 + (k if c == 0 else 1 - k)) * (tile // rows)
            for b in range(tile // rows):
                block = first + b
                block = block - lax.rem(block, 2) + jnp.where(y == 0, lax.rem(block, 2), 1 - lax.rem(block, 2))
                at = pl.ds(pl.multiple_of(block * rows, 128), rows)
                cut = slice(b * rows, (b + 1) * rows)
                a = halves(top[:, cut])
                high_ref[:rows, at], low_ref[:rows, at] = a
                done = dot3(same, a, NN)
                a = halves(bottom[:, cut])
                high_ref[rows:, at], low_ref[rows:, at] = a
                parts_ref[:, at] = done + dot3(other, a, NN)


def combine(depth, s, up_ref, down_ref, part_up_ref, part_down_ref, go_up_ref, go_down_ref):
    z = lax.axis_index("prow") // 2

    @pl.when(z <= s - 2)
    def _():
        go_up_ref[...] = up_ref[...] + part_up_ref[...]

    @pl.when(z > s - 2)
    def _():
        go_up_ref[...] = up_ref[...]

    @pl.when(depth - 1 - z <= s - 2)
    def _():
        go_down_ref[...] = down_ref[...] + part_down_ref[...]

    @pl.when(depth - 1 - z > s - 2)
    def _():
        go_down_ref[...] = down_ref[...]


def gram_products(depth, high_ref, low_ref, w1_ref, w2_ref, *refs):
    taken = refs[: 2 * (depth - 1)]
    same_ref, other_ref, give_ref, mine_ref, theirs_ref, total_ref = refs[2 * (depth - 1) :]
    z, y, _, k = place_of()
    span = w1_ref.shape[1]
    rows = span // 2

    def product(ref, at):
        columns = pl.ds(pl.multiple_of(at * span, 128), span)
        return dot3(halves(ref[...]), (high_ref[:, columns], low_ref[:, columns]), NT)

    total_ref[...] = product(w1_ref, z)
    for s in range(1, depth):

        @pl.when(z >= s)
        def _():
            total_ref[...] += product(taken[2 * s - 2], z - s)

        @pl.when(z + s < depth)
        def _():
            total_ref[...] += product(taken[2 * s - 1], z + s)

    same_ref[...] = total_ref[:, :rows]
    other_ref[...] = total_ref[:, rows:]
    give_ref[...] = jnp.where(k == y, total_ref[:, rows:], total_ref[:, :rows])
    y1 = halves(total_ref[...])
    w1, w2 = halves(w1_ref[...]), halves(w2_ref[...])
    half, wide = mine_ref.shape[0], w1_ref.shape[0]
    for out_ref, start in ((mine_ref, z % 2), (theirs_ref, 1 - z % 2)):
        cut = pl.ds(pl.multiple_of(start * half, 8), half)
        out_ref[:, :wide] = dot3(halves(w1_ref[cut, :]), y1, NT)
        out_ref[:, wide:] = dot3(halves(total_ref[cut, :]), w2, NT)


def energy_products(part_ref, up_ref, down_ref, w2_ref, same_ref, other_ref, give_ref, energy_ref):
    _, y, _, k = place_of()
    rows = same_ref.shape[1]
    y2 = part_ref[...] + up_ref[...] + down_ref[...]
    same_ref[...] = y2[:, :rows]
    other_ref[...] = y2[:, rows:]
    give_ref[...] = jnp.where(k == y, y2[:, rows:], y2[:, :rows])
    y2, w2 = halves(y2), halves(w2_ref[...])
    block = energy_ref.shape[0]
    for i in range(2):
        cut = slice(i * block, (i + 1) * block)
        energy_ref[:, cut] = dot3((w2[0][cut], w2[1][cut]), (y2[0][cut], y2[1][cut]), NT)


def finish_rows(
    own1, near1, far1, own2, near2, far2, link_ref, first_ref, second_ref, parent_ref, one_ref, two_ref, out1, out2
):
    my_row, my_col = lax.axis_index("prow"), lax.axis_index("pcol")
    y, k = my_row % 2, my_col % 2
    b1, b2 = link_ref.shape[1:]
    order = family_order(parent_ref, my_col)
    for f, y1, y2 in (
        (1 - y, near1[...], near2[...]),
        (y, jnp.where(k == y, own1[...], far1[...]), jnp.where(k == y, own2[...], far2[...])),
    ):
        y1, y2 = y1.T, y2.T
        on = first_ref[my_row, my_col * 2 + f]
        out1[:, pl.ds(pl.multiple_of(f * b1, 128), b1)] = -y1 * on.astype(F32)
        y1 = halves(y1)
        for i in range(2):
            child = pick([order[i], order[2 + i]], f)
            link = (
                link_ref[child]
                * below(one_ref[my_col * 2 + f], (b1, b2), 0)
                * below(two_ref[my_col * 4 + child], (b1, b2), 1)
            )
            both = (on * second_ref[my_row, my_col * 4 + child]).astype(F32)
            near = dot3(y1, halves(link), NN)
            out2[:, pl.ds(pl.multiple_of(child * b2, 128), b2)] = (near - y2[:, i * b2 : (i + 1) * b2]) * both


def finish_blocks(
    half,
    grams,
    own_e,
    near_e,
    far_e,
    pivot1_ref,
    link_ref,
    pivot2_ref,
    parent_ref,
    one_ref,
    two_ref,
    out_diag,
    out_link,
    out_last,
    d_ref,
):
    own_a, near_a, far_a, own_b, near_b, far_b = grams
    my_row, my_col = lax.axis_index("prow"), lax.axis_index("pcol")
    y, k = my_row % 2, my_col % 2
    stays = k == y
    b1, b2 = link_ref.shape[1:]
    order = family_order(parent_ref, my_col)
    low = (my_row // 2) % 2
    for f, g_a, g_b, energy in (
        (1 - y, near_a[...], near_b[...], near_e[...]),
        (
            y,
            jnp.where(stays, own_a[...], far_a[...]),
            jnp.where(stays, own_b[...], far_b[...]),
            jnp.where(stays, own_e[...], far_e[...]),
        ),
    ):
        d_ref[pl.ds(pl.multiple_of(low * half, 8), half), :] = g_a
        d_ref[pl.ds(pl.multiple_of((1 - low) * half, 8), half), :] = g_b
        size = one_ref[my_col * 2 + f]
        diag = pivot1_ref[f] * below(size, (b1, b1), 0) * below(size, (b1, b1), 1) + d_ref[:, :b1]
        out_diag[f] = diag
        diag = halves(diag)
        for i in range(2):
            child = pick([order[i], order[2 + i]], f)
            width = two_ref[my_col * 4 + child]
            link = halves(link_ref[child] * below(size, (b1, b2), 0) * below(width, (b1, b2), 1))
            cross = d_ref[:, b1 + i * b2 : b1 + (i + 1) * b2]
            down = cross - dot3(diag, link, NN)
            out_link[child] = down
            pivot = pivot2_ref[child] * below(width, (b2, b2), 0) * below(width, (b2, b2), 1)
            out_last[child] = (
                pivot
                - dot3(link, halves(down), TN)
                - dot3(halves(cross), link, TN)
                + energy[:, i * b2 : (i + 1) * b2]
            )


def call(body, outs, ins, scratch=(), scalars=0, name=None, flops=0):
    specs = [VMEM] * (len(ins) - scalars) + [SMEM] * scalars
    moved = 4 * sum(v.size for v in ins) + sum(v.size * v.dtype.itemsize for v in outs)
    return pl.pallas_call(
        body,
        out_shape=outs,
        in_specs=specs,
        out_specs=[VMEM] * len(outs),
        scratch_shapes=list(scratch),
        name=name,
        compiler_params=pltpu.CompilerParams(vmem_limit_bytes=40 * 2**20),
        cost_estimate=pl.CostEstimate(flops=flops, bytes_accessed=moved, transcendentals=0),
    )(*ins)


def array(*shape, dtype=F32):
    return jax.ShapeDtypeStruct(shape, dtype)


def solution(mesh):
    rows_of, cols_of = mesh.shape["prow"], mesh.shape["pcol"]
    depth, wide = rows_of // 2, cols_of // 2

    def pairs(move):
        out = []
        for z in range(depth):
            for y in range(2):
                for x in range(wide):
                    for k in range(2):
                        to = move(z, y, x, k)
                        if to is not None:
                            a, b, c, d = to
                            out.append(((z * 2 + y) * cols_of + x * 2 + k, (a * 2 + b) * cols_of + c * 2 + d))
        return out

    to_worker = pairs(lambda z, y, x, k: (z, y, x, 1 - k) if k == y else (z, 1 - y, x, k))
    to_home = pairs(lambda z, y, x, k: (z, 1 - y, x, k) if k == y else (z, y, x, 1 - k))
    across = pairs(lambda z, y, x, k: None if k == y else (z, 1 - y, x, 1 - k))
    other_y = pairs(lambda z, y, x, k: (z, 1 - y, x, k))
    other_core = pairs(lambda z, y, x, k: (z, y, x, 1 - k))
    up = pairs(lambda z, y, x, k: (z + 1, y, x, k) if z + 1 < depth else None)
    down = pairs(lambda z, y, x, k: (z - 1, y, x, k) if z > 0 else None)

    def send(value, perm):
        return lax.ppermute(value, AXES, perm)

    def on_device(
        anc_inverse,
        factor_one,
        pivot_one,
        factor_two,
        factor_link,
        pivot_two,
        pattern_one,
        pattern_two,
        parent_two,
        size_one,
        size_two,
    ):
        rows, tile = anc_inverse.shape
        total = tile * cols_of
        span = 2 * rows
        b1, b2 = pivot_one.shape[1], pivot_two.shape[1]
        z = lax.axis_index("prow") // 2
        block = array(b1, rows)
        kept1, give1 = call(
            functools.partial(pack_one, b1), [block] * 2, [factor_one, pattern_one, size_one], scalars=2, name="pack_one"
        )
        near1, far1 = send(give1, to_worker), send(kept1, across)
        beside = send(anc_inverse, other_y)
        tiles = [[anc_inverse, beside]]
        for s in range(1, wide):
            turn = pairs(lambda z, y, x, k: (z, y, (x + s) % wide, k))
            tiles.append([send(anc_inverse, turn), send(beside, turn)])
        kept2, give2 = call(
            functools.partial(pack_two, b2),
            [block] * 2,
            [factor_two, pattern_one, pattern_two, parent_two, size_two],
            scalars=4,
            name="pack_two",
        )
        near2, far2 = send(give2, to_worker), send(kept2, across)
        (w1,) = call(join, [array(b1, span)], [kept1, near1, far1], name="join_one")
        (w2,) = call(join, [array(b1, span)], [kept2, near2, far2], name="join_two")
        panel = []
        for mine in tiles:
            panel += mine + [send(v, other_core) for v in mine]
        parts, high, low = call(
            functools.partial(partial_products, wide),
            [array(b1, total), array(span, total, dtype=jnp.bfloat16), array(span, total, dtype=jnp.bfloat16)],
            [w2] + panel,
            name="partial_products",
            flops=6 * b1 * span * total,
        )

        def combined(s, from_below, from_above):
            whole = pl.BlockSpec((b1, span), lambda i, at: (0, 0))
            spec = pltpu.PrefetchScalarGridSpec(
                num_scalar_prefetch=1,
                grid=(1,),
                in_specs=[
                    whole,
                    whole,
                    pl.BlockSpec((b1, span), lambda i, at: (0, jnp.minimum(at[0] + 1 + depth - s, depth - 1))),
                    pl.BlockSpec((b1, span), lambda i, at: (0, jnp.maximum(at[0] - 1 - depth + s, 0))),
                ],
                out_specs=[whole, whole],
            )

            def body(at_ref, *refs):
                combine(depth, s, *refs)

            return pl.pallas_call(body, grid_spec=spec, out_shape=[array(b1, span)] * 2, name="combine")(
                z[None], from_below, from_above, parts, parts
            )

        from_below = from_above = w1
        taken = []
        for s in range(1, depth + 1):
            go_up, go_down = (w1, w1) if s == 1 else combined(s, from_below, from_above)
            from_below, from_above = send(go_up, up), send(go_down, down)
            if s < depth:
                taken += [from_below, from_above]
        half = b1 // 2
        same1, other1, give1, mine, theirs = call(
            functools.partial(gram_products, depth),
            [block] * 3 + [array(half, 2 * b1)] * 2,
            [high, low, w1, w2] + taken,
            scratch=[pltpu.VMEM((b1, span), F32)],
            name="gram_products",
            flops=6 * b1 * span * total,
        )
        home1 = [same1, send(give1, to_home), send(other1, across)]

        def swap(value, step):
            return send(value, pairs(lambda z, y, x, k: (z ^ step, y, x, k)))

        def deliver(value):
            return [value, send(value, to_home), send(value, across)]

        grams = mine + swap(theirs, 1)
        step = 2
        while step < depth:
            grams = grams + swap(grams, step)
            step *= 2
        grams_a = deliver(grams)
        grams_b = deliver(swap(grams, 1))

        def last_part():
            whole = pl.BlockSpec((b1, span), lambda i, at: (0, 0))
            small = pl.BlockSpec((b1, rows), lambda i, at: (0, 0))
            spec = pltpu.PrefetchScalarGridSpec(
                num_scalar_prefetch=1,
                grid=(1,),
                in_specs=[pl.BlockSpec((b1, span), lambda i, at: (0, at[0])), whole, whole, whole],
                out_specs=[small] * 3 + [pl.BlockSpec((b2, 2 * b2), lambda i, at: (0, 0))],
            )

            def body(at_ref, *refs):
                energy_products(*refs)

            return pl.pallas_call(body, grid_spec=spec, out_shape=[block] * 3 + [array(b2, 2 * b2)], name="energy")(
                z[None], parts, from_below, from_above, w2
            )

        same2, other2, give2, energy = last_part()
        home2 = [same2, send(give2, to_home), send(other2, across)]
        step = 1
        while step < depth:
            energy = energy + swap(energy, step)
            step *= 2
        energies = deliver(energy)
        scalars = [pattern_one, pattern_two, parent_two, size_one, size_two]
        inverse_one, inverse_two = call(
            finish_rows,
            [array(rows, 2 * b1), array(rows, 4 * b2)],
            home1 + home2 + [factor_link] + scalars,
            scalars=5,
            name="finish_rows",
        )

        def blocks_body(*refs):
            finish_blocks(half, refs[:6], *refs[6:])

        diagonal_one, inverse_link, diagonal_two = call(
            blocks_body,
            [array(*pivot_one.shape), array(*factor_link.shape), array(*pivot_two.shape)],
            grams_a + grams_b + energies + [pivot_one, factor_link, pivot_two] + scalars[2:],
            scratch=[pltpu.VMEM((b1, 2 * b1), F32)],
            scalars=3,
            name="finish_blocks",
        )
        return inverse_one, diagonal_one, inverse_two, inverse_link, diagonal_two

    return jax.shard_map(
        on_device,
        mesh=mesh,
        in_specs=(
            P("prow", "pcol"),
            P("prow", "pcol"),
            P("pcol", None, None),
            P("prow", "pcol"),
            P("pcol", None, None),
            P("pcol", None, None),
            P(),
            P(),
            P(),
            P(),
            P(),
        ),
        out_specs=(
            P("prow", "pcol"),
            P("pcol", None, None),
            P("prow", "pcol"),
            P("pcol", None, None),
            P("pcol", None, None),
        ),
        check_vma=False,
    )
```

time: 295 us -> 160 us (0.54)
  waiting for transfers between devices: 231 us -> 53.9 us
  starting transfers between devices: 0.16 us -> 58.4 us
  matrix products: 27.8 us -> 0 us
  Pallas kernels: 0 us -> 27.3 us
  between operations: 14 us -> 1.12 us
  other arithmetic: 6.41 us -> 1.01 us
  local copies, waits for them, and re-layouts: 14.4 us -> 17.5 us
    all_gather x3 -> x0, waiting for transfers between devices: 150 us -> none  [the longest x1 76.9 us: on_device(): lax.all_gather(factor_one, 'prow', axis=0, tiled=True)]
    psum x1 -> x0, waiting for transfers between devices: 81.2 us -> none  [on_device(): diagonal_one = pivots_one - lax.psum(correction, 'prow')]
    ppermute x0 -> x34, starting transfers between devices: none -> 58.4 us  [send(): return lax.ppermute(value, AXES, perm)]
    ppermute x0 -> x34, waiting for transfers between devices: none -> 53.9 us  [send(): return lax.ppermute(value, AXES, perm)]
    dot_general x12 -> x0, matrix products: 27.8 us -> none  [the longest x2 12.9 us: folder(): return jnp.dot(row_panel, piece * keep, precision=PRECISE)]
    pallas_call x0 -> x12, Pallas kernels: none -> 27.3 us  [the longest x8 16.9 us: call(): pl.pallas_call(body, out_shape=outs, in_specs=specs, out_specs=[VMEM] * l...]
    unnamed x33 -> x60, local copies, waits for them, and re-layouts: 9.83 us -> 17.5 us
    mul x4 -> x0, other arithmetic: 4.28 us -> none  [the longest x1 2.28 us: on_device(): keep_one = blocks_one * columns_one.reshape(1, -1)]
  transfers between devices with their start and end apart: 4 -> 34, of which waited for: 4 -> 14; matrix products, arithmetic and copies ran while one was open for 10% -> 1% of each run, Pallas kernels for 0% -> 10%
where the time goes in v2:
time: 160 us; the launch traced here: 159 us
  starting transfers between devices  58.4 us (36%)
  waiting for transfers between devices  53.9 us (34%)
  Pallas kernels  27.3 us (17%)
  local copies, waits for them, and re-layouts  17.5 us (11%)
    ppermute x34, starting transfers between devices, send(): return lax.ppermute(value, AXES, perm)  58.4 us
    ppermute x34, waiting for transfers between devices, send(): return lax.ppermute(value, AXES, perm)  53.9 us
    unnamed x60, local copies, waits for them, and re-layouts  17.5 us
    pallas_call x8, Pallas kernels, call(): pl.pallas_call(body, out_shape=outs, in_specs=specs, out_specs=[VMEM] * l...  16.9 us
    pallas_call x3, Pallas kernels, combined(): pl.pallas_call(body, grid_spec=spec, out_shape=[array(b1, span)] * 2, nam...  7.74 us
  transfers between devices with their start and end apart: 34, of which 14 were waited for; matrix products, arithmetic and copies ran while one was open for 1% of the time, Pallas kernels for 10%

profile of v2, /device:TPU:1, one launch (start us, length us, event | category | flops | bytes accessed | tf_op | source)
XLA Modules:
  0.0 159.2 jit_solution(8060388641718696913)
XLA Ops:
  0.6 2.1 %collective-permute-start.2 = (f32[256,512]{1,0:T(8,128)}, f32[256,512]{1,0:T(8,128)S(1)}, u32[]{:S(2)}, u32[]{:S(2)}) collective-permute-start(f32[256,512]{1,0:T(8,128)} %refs_0_.1), channel_id=1, source_target_pairs={{0,4},{1,5},{2,6},{3,7},{4,0},{5,1},{6,2},{7,3},{8,12},{9,13},{10,... | collective-permute-start | bytes 1572872 | tf_op jit(solution)/shard_map/ppermute | solution.py:322
  2.8 1.0 copy-done.7
  7.5 1.4 collective-permute-start.5
  8.9 5.7 %collective-permute-done.2.refs_1_ = f32[256,512]{1,0:T(8,128)S(1)} collective-permute-done((f32[256,512]{1,0:T(8,128)}, f32[256,512]{1,0:T(8,128)S(1)}, u32[]{:S(2)}, u32[]{:S(2)}) %collective-permute-start.2) | collective-permute-done | bytes 524320 | tf_op jit(solution)/shard_map/ppermute | solution.py:322
  14.6 1.1 collective-permute-start.6
  18.9 1.3 collective-permute-start.9
  21.2 4.3 %collective-permute-start.10 = (f32[256,256]{1,0:T(8,128)S(1)}, f32[256,256]{1,0:T(8,128)S(1)}, u32[]{:S(2)}, u32[]{:S(2)}) collective-permute-start(f32[256,256]{1,0:T(8,128)S(1)} %get-tuple-element.36.kept_ref), channel_id=1, source_target_pairs={{1,4},{3,6},{4,1},{6,3},{9,12},{11,14},{12,9},{14,11},{17,20},{19,... | collective-permute-start | bytes 786440 | tf_op jit(solution)/shard_map/ppermute | solution.py:322
  25.5 3.4 %collective-permute-start.1 = (f32[256,256]{1,0:T(8,128)S(1)}, f32[256,256]{1,0:T(8,128)S(1)}, u32[]{:S(2)}, u32[]{:S(2)}) collective-permute-start(f32[256,256]{1,0:T(8,128)S(1)} %get-tuple-element.32.kept_ref), channel_id=1, source_target_pairs={{1,4},{3,6},{4,1},{6,3},{9,12},{11,14},{12,9},{14,11},{17,20},{19,... | collective-permute-start | bytes 786440 | tf_op jit(solution)/shard_map/ppermute | solution.py:322
  28.9 1.4 collective-permute-done.10.far_ref
  31.4 1.9 %collective-permute-start.8 = (f32[256,512]{1,0:T(8,128)S(1)}, f32[256,512]{1,0:T(8,128)}, u32[]{:S(2)}, u32[]{:S(2)}) collective-permute-start(f32[256,512]{1,0:T(8,128)S(1)} %collective-permute-done.6.refs_5_), channel_id=1, source_target_pairs={{0,1},{1,0},{2,3},{3,2},{4,5},{5,4},{6,7},{7,6},{8,9},{9,8},{10,11... | collective-permute-start | bytes 1572872 | tf_op jit(solution)/shard_map/ppermute | solution.py:322
  33.4 4.1 %collective-permute-start.11 = (f32[256,512]{1,0:T(8,128)S(1)}, f32[256,512]{1,0:T(8,128)}, u32[]{:S(2)}, u32[]{:S(2)}) collective-permute-start(f32[256,512]{1,0:T(8,128)S(1)} %join_one.1.w1_ref), channel_id=1, source_target_pairs={{0,8},{1,9},{2,10},{3,11},{4,12},{5,13},{6,14},{7,15},{8,16},{9,17... | collective-permute-start | bytes 1572872 | tf_op jit(solution)/shard_map/ppermute | solution.py:322
  38.3 1.3 collective-permute-start.12
  39.7 1.2 copy-done.21
  45.1 3.8 %partial_products.1 = (f32[256,2048]{1,0:T(8,128)S(1)}, bf16[512,2048]{1,0:T(8,128)(2,1)S(1)}, bf16[512,2048]{1,0:T(8,128)(2,1)S(1)}) custom-call(f32[256,512]{1,0:T(8,128)S(1)} %join_two.1.w2_ref.refs_3_, f32[256,512]{1,0:T(8,128)S(1)} %copy-done.21, f32[256,512]{1,0:T(8,128)S(1)} %copy-done.23, f32[256,512]{1,0:T(8,128)S(1)} %copy-done.29, ...), custom_call_target="tpu_custom_call" | custom-call | flops 1610612736 | bytes 11010048 | tf_op jit(solution)/shard_map/partial_products/pallas_call | solution.py:281
  48.9 1.3 copy-done
  50.2 1.3 copy-done.3
  51.5 2.0 %collective-permute-done.12.refs_1_ = f32[256,512]{1,0:T(8,128)} collective-permute-done((f32[256,512]{1,0:T(8,128)S(1)}, f32[256,512]{1,0:T(8,128)}, u32[]{:S(2)}, u32[]{:S(2)}) %collective-permute-start.12) | collective-permute-done | bytes 524320 | tf_op jit(solution)/shard_map/ppermute | solution.py:322
  53.5 2.6 %combine.3 = (f32[256,512]{1,0:T(8,128)}, f32[256,512]{1,0:T(8,128)}) custom-call(s32[1]{0:T(128)} %bitcast.at_ref, f32[256,512]{1,0:T(8,128)} %collective-permute-done.11.refs_0_, f32[256,512]{1,0:T(8,128)} %collective-permute-done.12.refs_1_, f32[256,2048]{1,0:T(8,128)} %copy-done, f32[256,2048]{1,0:T(8,128)} %copy-done), custom_call_target="tpu_custom_call" | custom-call | tf_op jit(solution)/shard_map/combine/pallas_call | solution.py:390
  56.1 3.2 %collective-permute-start.13 = (f32[256,512]{1,0:T(8,128)}, f32[256,512]{1,0:T(8,128)}, u32[]{:S(2)}, u32[]{:S(2)}) collective-permute-start(f32[256,512]{1,0:T(8,128)} %get-tuple-element.39), channel_id=1, source_target_pairs={{0,8},{1,9},{2,10},{3,11},{4,12},{5,13},{6,14},{7,15},{8,16},{9,17... | collective-permute-start | bytes 1572872 | tf_op jit(solution)/shard_map/ppermute | solution.py:322
  59.3 1.3 collective-permute-start.14
  60.6 8.3 %collective-permute-done.13.refs_0_.refs_2_ = f32[256,512]{1,0:T(8,128)} collective-permute-done((f32[256,512]{1,0:T(8,128)}, f32[256,512]{1,0:T(8,128)}, u32[]{:S(2)}, u32[]{:S(2)}) %collective-permute-start.13) | collective-permute-done | bytes 524320 | tf_op jit(solution)/shard_map/ppermute | solution.py:322
  68.9 4.7 %collective-permute-done.14.refs_1_.refs_3_ = f32[256,512]{1,0:T(8,128)} collective-permute-done((f32[256,512]{1,0:T(8,128)}, f32[256,512]{1,0:T(8,128)}, u32[]{:S(2)}, u32[]{:S(2)}) %collective-permute-start.14) | collective-permute-done | bytes 524320 | tf_op jit(solution)/shard_map/ppermute | solution.py:322
  73.6 2.6 %combine.4 = (f32[256,512]{1,0:T(8,128)}, f32[256,512]{1,0:T(8,128)}) custom-call(s32[1]{0:T(128)} %bitcast.at_ref, f32[256,512]{1,0:T(8,128)} %collective-permute-done.13.refs_0_.refs_2_, f32[256,512]{1,0:T(8,128)} %collective-permute-done.14.refs_1_.refs_3_, f32[256,2048]{1,0:T(8,128)} %copy-done, f32[256,2048]{1,0:T(8,128)} %copy-done), custom_call_target="tpu_custom_call" | custom-call | tf_op jit(solution)/shard_map/combine/pallas_call | solution.py:390
  76.2 3.2 %collective-permute-start.15 = (f32[256,512]{1,0:T(8,128)}, f32[256,512]{1,0:T(8,128)}, u32[]{:S(2)}, u32[]{:S(2)}) collective-permute-start(f32[256,512]{1,0:T(8,128)} %get-tuple-element.41), channel_id=1, source_target_pairs={{0,8},{1,9},{2,10},{3,11},{4,12},{5,13},{6,14},{7,15},{8,16},{9,17... | collective-permute-start | bytes 1572872 | tf_op jit(solution)/shard_map/ppermute | solution.py:322
  79.4 1.3 collective-permute-start.16
  80.7 7.1 %collective-permute-done.15.refs_4_.refs_0_ = f32[256,512]{1,0:T(8,128)} collective-permute-done((f32[256,512]{1,0:T(8,128)}, f32[256,512]{1,0:T(8,128)}, u32[]{:S(2)}, u32[]{:S(2)}) %collective-permute-start.15) | collective-permute-done | bytes 524320 | tf_op jit(solution)/shard_map/ppermute | solution.py:322
  87.7 4.7 %collective-permute-done.16.refs_5_.refs_1_ = f32[256,512]{1,0:T(8,128)} collective-permute-done((f32[256,512]{1,0:T(8,128)}, f32[256,512]{1,0:T(8,128)}, u32[]{:S(2)}, u32[]{:S(2)}) %collective-permute-start.16) | collective-permute-done | bytes 524320 | tf_op jit(solution)/shard_map/ppermute | solution.py:322
  92.4 2.6 %combine.5 = (f32[256,512]{1,0:T(8,128)}, f32[256,512]{1,0:T(8,128)}) custom-call(s32[1]{0:T(128)} %bitcast.at_ref, f32[256,512]{1,0:T(8,128)} %collective-permute-done.15.refs_4_.refs_0_, f32[256,512]{1,0:T(8,128)} %collective-permute-done.16.refs_5_.refs_1_, f32[256,2048]{1,0:T(8,128)} %copy-done, f32[256,2048]{1,0:T(8,128)} %copy-done), custom_call_target="tpu_custom_call" | custom-call | tf_op jit(solution)/shard_map/combine/pallas_call | solution.py:390
  95.0 4.0 %collective-permute-start.19 = (f32[256,512]{1,0:T(8,128)}, f32[256,512]{1,0:T(8,128)}, u32[]{:S(2)}, u32[]{:S(2)}) collective-permute-start(f32[256,512]{1,0:T(8,128)} %get-tuple-element.46), channel_id=1, source_target_pairs={{0,8},{1,9},{2,10},{3,11},{4,12},{5,13},{6,14},{7,15},{8,16},{9,17... | collective-permute-start | bytes 1572872 | tf_op jit(solution)/shard_map/ppermute | solution.py:322
  99.0 1.3 collective-permute-start.20
  100.3 1.6 copy-done.4
  101.9 6.1 %gram_products.1 = (f32[256,256]{1,0:T(8,128)S(1)}, f32[256,256]{1,0:T(8,128)}, f32[256,256]{1,0:T(8,128)}, f32[128,512]{1,0:T(8,128)S(1)}, f32[128,512]{1,0:T(8,128)S(1)}) custom-call(bf16[512,2048]{1,0:T(8,128)(2,1)S(1)} %get-tuple-element.34.high_ref, bf16[512,2048]{1,0:T(8,128)(2,1)S(1)} %copy-done.4, f32[256,512]{1,0:T(8,128)S(1)} %join_one.1.w1_ref, ...), custom_call_target="tpu_custom_call" | custom-call | flops 1610612736 | bytes 13893632 | tf_op jit(solution)/shard_map/gram_products/pallas_call | solution.py:281
  108.0 2.1 %collective-permute-start.23 = (f32[128,512]{1,0:T(8,128)S(1)}, f32[128,512]{1,0:T(8,128)S(1)}, u32[]{:S(2)}, u32[]{:S(2)}) collective-permute-start(f32[128,512]{1,0:T(8,128)S(1)} %get-tuple-element.53), channel_id=1, source_target_pairs={{0,8},{1,9},{2,10},{3,11},{4,12},{5,13},{6,14},{7,15},{8,0},{9,1},... | collective-permute-start | bytes 786440 | tf_op jit(solution)/shard_map/ppermute | solution.py:322
  110.1 7.0 %collective-permute-done.23 = f32[128,512]{1,0:T(8,128)S(1)} collective-permute-done((f32[128,512]{1,0:T(8,128)S(1)}, f32[128,512]{1,0:T(8,128)S(1)}, u32[]{:S(2)}, u32[]{:S(2)}) %collective-permute-start.23) | collective-permute-done | bytes 262176 | tf_op jit(solution)/shard_map/ppermute | solution.py:322
  117.8 3.4 %collective-permute-start.17 = (f32[256,256]{1,0:T(8,128)}, f32[256,256]{1,0:T(8,128)S(1)}, u32[]{:S(2)}, u32[]{:S(2)}) collective-permute-start(f32[256,256]{1,0:T(8,128)} %get-tuple-element.44), channel_id=1, source_target_pairs={{0,4},{1,0},{2,6},{3,2},{4,5},{5,1},{6,7},{7,3},{8,12},{9,8},{10,1... | collective-permute-start | bytes 786440 | tf_op jit(solution)/shard_map/ppermute | solution.py:322
  121.2 2.2 %collective-permute-start.18 = (f32[256,256]{1,0:T(8,128)}, f32[256,256]{1,0:T(8,128)S(1)}, u32[]{:S(2)}, u32[]{:S(2)}) collective-permute-start(f32[256,256]{1,0:T(8,128)} %get-tuple-element.45), channel_id=1, source_target_pairs={{1,4},{3,6},{4,1},{6,3},{9,12},{11,14},{12,9},{14,11},{17,20},{19,... | collective-permute-start | bytes 786440 | tf_op jit(solution)/shard_map/ppermute | solution.py:322
  123.5 2.6 %energy.1 = (f32[256,256]{1,0:T(8,128)}, f32[256,256]{1,0:T(8,128)}, f32[256,256]{1,0:T(8,128)}, f32[128,256]{1,0:T(8,128)}) custom-call(s32[1]{0:T(128)} %bitcast.at_ref, f32[256,2048]{1,0:T(8,128)} %copy-done, f32[256,512]{1,0:T(8,128)} %collective-permute-done.19.refs_1_, f32[256,512]{1,0:T(8,128)} %collective-permute-done.20.refs_2_, f32[256,512]{1,0:T(8,128)} %copy-done.1), custom_call_target="tpu_custom_call" | custom-call | tf_op jit(solution)/shard_map/energy/pallas_call | solution.py:439
  126.1 3.0 %collective-permute-done.24 = f32[128,512]{1,0:T(8,128)S(1)} collective-permute-done((f32[128,512]{1,0:T(8,128)S(1)}, f32[128,512]{1,0:T(8,128)S(1)}, u32[]{:S(2)}, u32[]{:S(2)}) %collective-permute-start.24) | collective-permute-done | bytes 262176 | tf_op jit(solution)/shard_map/ppermute | solution.py:322
  129.2 4.5 %collective-permute-done.30 = f32[128,256]{1,0:T(8,128)S(1)} collective-permute-done((f32[128,256]{1,0:T(8,128)}, f32[128,256]{1,0:T(8,128)S(1)}, u32[]{:S(2)}, u32[]{:S(2)}) %collective-permute-start.30) | collective-permute-done | bytes 131104 | tf_op jit(solution)/shard_map/ppermute | solution.py:322
  133.7 1.9 %collective-permute-start.22 = (f32[256,256]{1,0:T(8,128)}, f32[256,256]{1,0:T(8,128)S(1)}, u32[]{:S(2)}, u32[]{:S(2)}) collective-permute-start(f32[256,256]{1,0:T(8,128)} %get-tuple-element.50), channel_id=1, source_target_pairs={{1,4},{3,6},{4,1},{6,3},{9,12},{11,14},{12,9},{14,11},{17,20},{19,... | collective-permute-start | bytes 786440 | tf_op jit(solution)/shard_map/ppermute | solution.py:322
  136.6 3.1 %collective-permute-start.31 = (f32[128,256]{1,0:T(8,128)S(1)}, f32[128,256]{1,0:T(8,128)S(1)}, u32[]{:S(2)}, u32[]{:S(2)}) collective-permute-start(f32[128,256]{1,0:T(8,128)S(1)} %add.15), channel_id=1, source_target_pairs={{0,16},{1,17},{2,18},{3,19},{4,20},{5,21},{6,22},{7,23},{8,24},{9,... | collective-permute-start | bytes 393224 | tf_op jit(solution)/shard_map/ppermute | solution.py:322
  139.7 2.2 %collective-permute-start.26 = (f32[128,512]{1,0:T(8,128)S(1)}, f32[128,512]{1,0:T(8,128)S(1)}, u32[]{:S(2)}, u32[]{:S(2)}) collective-permute-start(f32[128,512]{1,0:T(8,128)S(1)} %add.14.refs_0_), channel_id=1, source_target_pairs={{1,4},{3,6},{4,1},{6,3},{9,12},{11,14},{12,9},{14,11},{17,20},{19,... | collective-permute-start | bytes 786440 | tf_op jit(solution)/shard_map/ppermute | solution.py:322
  142.0 3.2 %collective-permute-done.31 = f32[128,256]{1,0:T(8,128)S(1)} collective-permute-done((f32[128,256]{1,0:T(8,128)S(1)}, f32[128,256]{1,0:T(8,128)S(1)}, u32[]{:S(2)}, u32[]{:S(2)}) %collective-permute-start.31) | collective-permute-done | bytes 131104 | tf_op jit(solution)/shard_map/ppermute | solution.py:322
  145.2 4.1 %collective-permute-start.29 = (f32[128,512]{1,0:T(8,128)S(1)}, f32[128,512]{1,0:T(8,128)S(1)}, u32[]{:S(2)}, u32[]{:S(2)}) collective-permute-start(f32[128,512]{1,0:T(8,128)S(1)} %collective-permute-done.27.refs_3_), channel_id=1, source_target_pairs={{1,4},{3,6},{4,1},{6,3},{9,12},{11,14},{12,9},{14,11},{17,20},{19,... | collective-permute-start | bytes 786440 | tf_op jit(solution)/shard_map/ppermute | solution.py:322
  149.3 1.9 %collective-permute-start.33 = (f32[128,256]{1,0:T(8,128)S(1)}, f32[128,256]{1,0:T(8,128)S(1)}, u32[]{:S(2)}, u32[]{:S(2)}) collective-permute-start(f32[128,256]{1,0:T(8,128)S(1)} %add.16.refs_6_), channel_id=1, source_target_pairs={{1,4},{3,6},{4,1},{6,3},{9,12},{11,14},{12,9},{14,11},{17,20},{19,... | collective-permute-start | bytes 393224 | tf_op jit(solution)/shard_map/ppermute | solution.py:322
  152.3 2.1 %finish_rows.1 = (f32[256,512]{1,0:T(8,128)}, f32[256,512]{1,0:T(8,128)}) custom-call(f32[256,256]{1,0:T(8,128)S(1)} %get-tuple-element.43.own1, f32[256,256]{1,0:T(8,128)S(1)} %collective-permute-done.17.near1, f32[256,256]{1,0:T(8,128)S(1)} %collective-permute-done.18.far1, f32[256,256]{1,0:T(8,128)S(1)} %copy-done.9, ...), custom_call_target="tpu_custom_call" | custom-call | bytes 3146656 | tf_op jit(solution)/shard_map/finish_rows/pallas_call | solution.py:281
  154.5 1.5 collective-permute-done.33.refs_8_
  156.1 3.1 %finish_blocks.1 = (f32[2,256,256]{2,1,0:T(8,128)}, f32[4,256,128]{2,1,0:T(8,128)}, f32[4,128,128]{2,1,0:T(8,128)}) custom-call(f32[128,512]{1,0:T(8,128)S(1)} %add.14.refs_0_, f32[128,512]{1,0:T(8,128)S(1)} %collective-permute-done.25.refs_1_, f32[128,512]{1,0:T(8,128)S(1)} %collective-permute-done.26.refs_2_, ...), custom_call_target="tpu_custom_call" | custom-call | bytes 4587680 | tf_op jit(solution)/shard_map/finish_blocks/pallas_call | solution.py:281
  (96 shorter events, 17.1 us)
Async XLA Ops:
  0.6 14.0 %collective-permute-start.2 = (f32[256,512]{1,0:T(8,128)}, f32[256,512]{1,0:T(8,128)S(1)}, u32[]{:S(2)}, u32[]{:S(2)}) collective-permute-start(f32[256,512]{1,0:T(8,128)} %refs_0_.1), channel_id=1, source_target_pairs={{0,4},{1,5},{2,6},{3,7},{4,0},{5,1},{6,2},{7,3},{8,12},{9,13},{10,... | collective-permute-start | bytes 1572872 | tf_op jit(solution)/shard_map/ppermute | solution.py:322
  7.4 13.7 %collective-permute-start = (f32[256,256]{1,0:T(8,128)S(1)}, f32[256,256]{1,0:T(8,128)S(1)}, u32[]{:S(2)}, u32[]{:S(2)}) collective-permute-start(f32[256,256]{1,0:T(8,128)S(1)} %get-tuple-element.33), channel_id=1, source_target_pairs={{0,1},{1,5},{2,3},{3,7},{4,0},{5,4},{6,2},{7,6},{8,9},{9,13},{10,1... | collective-permute-start | bytes 786440 | tf_op jit(solution)/shard_map/ppermute | solution.py:322
  7.5 22.8 %collective-permute-start.5 = (f32[256,512]{1,0:T(8,128)}, f32[256,512]{1,0:T(8,128)S(1)}, u32[]{:S(2)}, u32[]{:S(2)}) collective-permute-start(f32[256,512]{1,0:T(8,128)} %refs_0_.1), channel_id=1, source_target_pairs={{0,2},{1,3},{2,0},{3,1},{4,6},{5,7},{6,4},{7,5},{8,10},{9,11},{10,... | collective-permute-start | bytes 1572872 | tf_op jit(solution)/shard_map/ppermute | solution.py:322
  14.6 25.1 %copy-start.22 = (f32[256,512]{1,0:T(8,128)}, f32[256,512]{1,0:T(8,128)S(1)}, u32[]{:S(2)}) copy-start(f32[256,512]{1,0:T(8,128)S(1)} %collective-permute-done.2.refs_1_) | copy-start | bytes 1572868
  14.6 16.8 %collective-permute-start.6 = (f32[256,512]{1,0:T(8,128)S(1)}, f32[256,512]{1,0:T(8,128)S(1)}, u32[]{:S(2)}, u32[]{:S(2)}) collective-permute-start(f32[256,512]{1,0:T(8,128)S(1)} %collective-permute-done.2.refs_1_), channel_id=1, source_target_pairs={{0,2},{1,3},{2,0},{3,1},{4,6},{5,7},{6,4},{7,5},{8,10},{9,11},{10,... | collective-permute-start | bytes 1572872 | tf_op jit(solution)/shard_map/ppermute | solution.py:322
  18.9 6.5 %collective-permute-start.9 = (f32[256,256]{1,0:T(8,128)S(1)}, f32[256,256]{1,0:T(8,128)S(1)}, u32[]{:S(2)}, u32[]{:S(2)}) collective-permute-start(f32[256,256]{1,0:T(8,128)S(1)} %get-tuple-element.37), channel_id=1, source_target_pairs={{0,1},{1,5},{2,3},{3,7},{4,0},{5,4},{6,2},{7,6},{8,9},{9,13},{10,1... | collective-permute-start | bytes 786440 | tf_op jit(solution)/shard_map/ppermute | solution.py:322
  20.2 17.3 %collective-permute-start.3 = (f32[256,512]{1,0:T(8,128)}, f32[256,512]{1,0:T(8,128)S(1)}, u32[]{:S(2)}, u32[]{:S(2)}) collective-permute-start(f32[256,512]{1,0:T(8,128)} %refs_0_.1), channel_id=1, source_target_pairs={{0,1},{1,0},{2,3},{3,2},{4,5},{5,4},{6,7},{7,6},{8,9},{9,8},{10,11... | collective-permute-start | bytes 1572872 | tf_op jit(solution)/shard_map/ppermute | solution.py:322
  21.2 9.1 %collective-permute-start.10 = (f32[256,256]{1,0:T(8,128)S(1)}, f32[256,256]{1,0:T(8,128)S(1)}, u32[]{:S(2)}, u32[]{:S(2)}) collective-permute-start(f32[256,256]{1,0:T(8,128)S(1)} %get-tuple-element.36.kept_ref), channel_id=1, source_target_pairs={{1,4},{3,6},{4,1},{6,3},{9,12},{11,14},{12,9},{14,11},{17,20},{19,... | collective-permute-start | bytes 786440 | tf_op jit(solution)/shard_map/ppermute | solution.py:322
  25.5 7.9 %collective-permute-start.1 = (f32[256,256]{1,0:T(8,128)S(1)}, f32[256,256]{1,0:T(8,128)S(1)}, u32[]{:S(2)}, u32[]{:S(2)}) collective-permute-start(f32[256,256]{1,0:T(8,128)S(1)} %get-tuple-element.32.kept_ref), channel_id=1, source_target_pairs={{1,4},{3,6},{4,1},{6,3},{9,12},{11,14},{12,9},{14,11},{17,20},{19,... | collective-permute-start | bytes 786440 | tf_op jit(solution)/shard_map/ppermute | solution.py:322
  30.2 9.4 %collective-permute-start.4 = (f32[256,512]{1,0:T(8,128)S(1)}, f32[256,512]{1,0:T(8,128)}, u32[]{:S(2)}, u32[]{:S(2)}) collective-permute-start(f32[256,512]{1,0:T(8,128)S(1)} %collective-permute-done.2.refs_1_), channel_id=1, source_target_pairs={{0,1},{1,0},{2,3},{3,2},{4,5},{5,4},{6,7},{7,6},{8,9},{9,8},{10,11... | collective-permute-start | bytes 1572872 | tf_op jit(solution)/shard_map/ppermute | solution.py:322
  30.2 9.5 %copy-start.24 = (f32[256,512]{1,0:T(8,128)}, f32[256,512]{1,0:T(8,128)S(1)}, u32[]{:S(2)}) copy-start(f32[256,512]{1,0:T(8,128)S(1)} %collective-permute-done.5.refs_4_) | copy-start | bytes 1572868
  30.2 9.4 %collective-permute-start.7 = (f32[256,512]{1,0:T(8,128)S(1)}, f32[256,512]{1,0:T(8,128)}, u32[]{:S(2)}, u32[]{:S(2)}) collective-permute-start(f32[256,512]{1,0:T(8,128)S(1)} %collective-permute-done.5.refs_4_), channel_id=1, source_target_pairs={{0,1},{1,0},{2,3},{3,2},{4,5},{5,4},{6,7},{7,6},{8,9},{9,8},{10,11... | collective-permute-start | bytes 1572872 | tf_op jit(solution)/shard_map/ppermute | solution.py:322
  31.4 8.3 %copy-start.26 = (f32[256,512]{1,0:T(8,128)}, f32[256,512]{1,0:T(8,128)S(1)}, u32[]{:S(2)}) copy-start(f32[256,512]{1,0:T(8,128)S(1)} %collective-permute-done.6.refs_5_) | copy-start | bytes 1572868
  31.4 8.3 %collective-permute-start.8 = (f32[256,512]{1,0:T(8,128)S(1)}, f32[256,512]{1,0:T(8,128)}, u32[]{:S(2)}, u32[]{:S(2)}) collective-permute-start(f32[256,512]{1,0:T(8,128)S(1)} %collective-permute-done.6.refs_5_), channel_id=1, source_target_pairs={{0,1},{1,0},{2,3},{3,2},{4,5},{5,4},{6,7},{7,6},{8,9},{9,8},{10,11... | collective-permute-start | bytes 1572872 | tf_op jit(solution)/shard_map/ppermute | solution.py:322
  33.4 18.2 %collective-permute-start.11 = (f32[256,512]{1,0:T(8,128)S(1)}, f32[256,512]{1,0:T(8,128)}, u32[]{:S(2)}, u32[]{:S(2)}) collective-permute-start(f32[256,512]{1,0:T(8,128)S(1)} %join_one.1.w1_ref), channel_id=1, source_target_pairs={{0,8},{1,9},{2,10},{3,11},{4,12},{5,13},{6,14},{7,15},{8,16},{9,17... | collective-permute-start | bytes 1572872 | tf_op jit(solution)/shard_map/ppermute | solution.py:322
  38.3 15.2 %collective-permute-start.12 = (f32[256,512]{1,0:T(8,128)S(1)}, f32[256,512]{1,0:T(8,128)}, u32[]{:S(2)}, u32[]{:S(2)}) collective-permute-start(f32[256,512]{1,0:T(8,128)S(1)} %join_one.1.w1_ref), channel_id=1, source_target_pairs={{8,0},{9,1},{10,2},{11,3},{12,4},{13,5},{14,6},{15,7},{16,8},{17,9... | collective-permute-start | bytes 1572872 | tf_op jit(solution)/shard_map/ppermute | solution.py:322
  39.7 60.6 %copy-start.1 = (f32[256,512]{1,0:T(8,128)}, f32[256,512]{1,0:T(8,128)S(1)}, u32[]{:S(2)}) copy-start(f32[256,512]{1,0:T(8,128)S(1)} %join_two.1.w2_ref.refs_3_) | copy-start | bytes 1572868
  50.2 1.3 copy-start.3
  56.1 12.8 %collective-permute-start.13 = (f32[256,512]{1,0:T(8,128)}, f32[256,512]{1,0:T(8,128)}, u32[]{:S(2)}, u32[]{:S(2)}) collective-permute-start(f32[256,512]{1,0:T(8,128)} %get-tuple-element.39), channel_id=1, source_target_pairs={{0,8},{1,9},{2,10},{3,11},{4,12},{5,13},{6,14},{7,15},{8,16},{9,17... | collective-permute-start | bytes 1572872 | tf_op jit(solution)/shard_map/ppermute | solution.py:322
  59.3 14.2 %collective-permute-start.14 = (f32[256,512]{1,0:T(8,128)}, f32[256,512]{1,0:T(8,128)}, u32[]{:S(2)}, u32[]{:S(2)}) collective-permute-start(f32[256,512]{1,0:T(8,128)} %get-tuple-element.40), channel_id=1, source_target_pairs={{8,0},{9,1},{10,2},{11,3},{12,4},{13,5},{14,6},{15,7},{16,8},{17,9... | collective-permute-start | bytes 1572872 | tf_op jit(solution)/shard_map/ppermute | solution.py:322
  76.2 11.6 %collective-permute-start.15 = (f32[256,512]{1,0:T(8,128)}, f32[256,512]{1,0:T(8,128)}, u32[]{:S(2)}, u32[]{:S(2)}) collective-permute-start(f32[256,512]{1,0:T(8,128)} %get-tuple-element.41), channel_id=1, source_target_pairs={{0,8},{1,9},{2,10},{3,11},{4,12},{5,13},{6,14},{7,15},{8,16},{9,17... | collective-permute-start | bytes 1572872 | tf_op jit(solution)/shard_map/ppermute | solution.py:322
  79.4 13.0 %collective-permute-start.16 = (f32[256,512]{1,0:T(8,128)}, f32[256,512]{1,0:T(8,128)}, u32[]{:S(2)}, u32[]{:S(2)}) collective-permute-start(f32[256,512]{1,0:T(8,128)} %get-tuple-element.42), channel_id=1, source_target_pairs={{8,0},{9,1},{10,2},{11,3},{12,4},{13,5},{14,6},{15,7},{16,8},{17,9... | collective-permute-start | bytes 1572872 | tf_op jit(solution)/shard_map/ppermute | solution.py:322
  95.0 28.5 %collective-permute-start.19 = (f32[256,512]{1,0:T(8,128)}, f32[256,512]{1,0:T(8,128)}, u32[]{:S(2)}, u32[]{:S(2)}) collective-permute-start(f32[256,512]{1,0:T(8,128)} %get-tuple-element.46), channel_id=1, source_target_pairs={{0,8},{1,9},{2,10},{3,11},{4,12},{5,13},{6,14},{7,15},{8,16},{9,17... | collective-permute-start | bytes 1572872 | tf_op jit(solution)/shard_map/ppermute | solution.py:322
  99.0 24.5 %collective-permute-start.20 = (f32[256,512]{1,0:T(8,128)}, f32[256,512]{1,0:T(8,128)}, u32[]{:S(2)}, u32[]{:S(2)}) collective-permute-start(f32[256,512]{1,0:T(8,128)} %get-tuple-element.47), channel_id=1, source_target_pairs={{8,0},{9,1},{10,2},{11,3},{12,4},{13,5},{14,6},{15,7},{16,8},{17,9... | collective-permute-start | bytes 1572872 | tf_op jit(solution)/shard_map/ppermute | solution.py:322
  100.3 1.6 %copy-start.4 = (bf16[512,2048]{1,0:T(8,128)(2,1)S(1)}, bf16[512,2048]{1,0:T(8,128)(2,1)}, u32[]{:S(2)}) copy-start(bf16[512,2048]{1,0:T(8,128)(2,1)} %copy-done.3) | copy-start | bytes 6291460
  108.0 9.1 %collective-permute-start.23 = (f32[128,512]{1,0:T(8,128)S(1)}, f32[128,512]{1,0:T(8,128)S(1)}, u32[]{:S(2)}, u32[]{:S(2)}) collective-permute-start(f32[128,512]{1,0:T(8,128)S(1)} %get-tuple-element.53), channel_id=1, source_target_pairs={{0,8},{1,9},{2,10},{3,11},{4,12},{5,13},{6,14},{7,15},{8,0},{9,1},... | collective-permute-start | bytes 786440 | tf_op jit(solution)/shard_map/ppermute | solution.py:322
  117.1 11.9 %collective-permute-start.24 = (f32[128,512]{1,0:T(8,128)S(1)}, f32[128,512]{1,0:T(8,128)S(1)}, u32[]{:S(2)}, u32[]{:S(2)}) collective-permute-start(f32[128,512]{1,0:T(8,128)S(1)} %add.13), channel_id=1, source_target_pairs={{0,16},{1,17},{2,18},{3,19},{4,20},{5,21},{6,22},{7,23},{8,24},{9,... | collective-permute-start | bytes 786440 | tf_op jit(solution)/shard_map/ppermute | solution.py:322
  117.8 18.7 %collective-permute-start.17 = (f32[256,256]{1,0:T(8,128)}, f32[256,256]{1,0:T(8,128)S(1)}, u32[]{:S(2)}, u32[]{:S(2)}) collective-permute-start(f32[256,256]{1,0:T(8,128)} %get-tuple-element.44), channel_id=1, source_target_pairs={{0,4},{1,0},{2,6},{3,2},{4,5},{5,1},{6,7},{7,3},{8,12},{9,8},{10,1... | collective-permute-start | bytes 786440 | tf_op jit(solution)/shard_map/ppermute | solution.py:322
  121.2 30.1 %copy-start.2 = (f32[4,256,128]{2,1,0:T(8,128)S(1)}, f32[4,256,128]{2,1,0:T(8,128)}, u32[]{:S(2)}) copy-start(f32[4,256,128]{2,1,0:T(8,128)} %refs_10_.1) | copy-start | bytes 1572868
  121.2 30.1 %copy-start.12 = (s32[8,8]{1,0:T(8,128)S(1)}, s32[8,8]{1,0:T(8,128)}, u32[]{:S(2)}) copy-start(s32[8,8]{1,0:T(8,128)} %first_ref.3) | copy-start | bytes 772
  121.2 30.1 %copy-start.14 = (s32[8,16]{1,0:T(8,128)S(1)}, s32[8,16]{1,0:T(8,128)}, u32[]{:S(2)}) copy-start(s32[8,16]{1,0:T(8,128)} %second_ref.3) | copy-start | bytes 1540
  121.2 30.1 %copy-start.16 = (s32[8]{0:T(128)S(1)}, s32[8]{0:T(128)}, u32[]{:S(2)}) copy-start(s32[8]{0:T(128)} %refs_13_.1) | copy-start | bytes 100
  121.2 30.1 %copy-start.18 = (s32[16]{0:T(128)S(1)}, s32[16]{0:T(128)}, u32[]{:S(2)}) copy-start(s32[16]{0:T(128)} %refs_12_.1) | copy-start | bytes 196
  121.2 30.1 %copy-start.20 = (s32[16]{0:T(128)S(1)}, s32[16]{0:T(128)}, u32[]{:S(2)}) copy-start(s32[16]{0:T(128)} %refs_14_.1) | copy-start | bytes 196
  121.2 15.4 %collective-permute-start.18 = (f32[256,256]{1,0:T(8,128)}, f32[256,256]{1,0:T(8,128)S(1)}, u32[]{:S(2)}, u32[]{:S(2)}) collective-permute-start(f32[256,256]{1,0:T(8,128)} %get-tuple-element.45), channel_id=1, source_target_pairs={{1,4},{3,6},{4,1},{6,3},{9,12},{11,14},{12,9},{14,11},{17,20},{19,... | collective-permute-start | bytes 786440 | tf_op jit(solution)/shard_map/ppermute | solution.py:322
  126.1 30.0 %copy-start.5 = (f32[2,256,256]{2,1,0:T(8,128)S(1)}, f32[2,256,256]{2,1,0:T(8,128)}, u32[]{:S(2)}) copy-start(f32[2,256,256]{2,1,0:T(8,128)} %refs_9_.1) | copy-start | bytes 1572868
  126.1 30.0 %copy-start.8 = (f32[4,128,128]{2,1,0:T(8,128)S(1)}, f32[4,128,128]{2,1,0:T(8,128)}, u32[]{:S(2)}) copy-start(f32[4,128,128]{2,1,0:T(8,128)} %refs_11_.1) | copy-start | bytes 786436
  126.1 7.6 %collective-permute-start.30 = (f32[128,256]{1,0:T(8,128)}, f32[128,256]{1,0:T(8,128)S(1)}, u32[]{:S(2)}, u32[]{:S(2)}) collective-permute-start(f32[128,256]{1,0:T(8,128)} %get-tuple-element.54), channel_id=1, source_target_pairs={{0,8},{1,9},{2,10},{3,11},{4,12},{5,13},{6,14},{7,15},{8,0},{9,1},... | collective-permute-start | bytes 393224 | tf_op jit(solution)/shard_map/ppermute | solution.py:322
  126.1 13.7 %collective-permute-start.21 = (f32[256,256]{1,0:T(8,128)}, f32[256,256]{1,0:T(8,128)S(1)}, u32[]{:S(2)}, u32[]{:S(2)}) collective-permute-start(f32[256,256]{1,0:T(8,128)} %get-tuple-element.49), channel_id=1, source_target_pairs={{0,4},{1,0},{2,6},{3,2},{4,5},{5,1},{6,7},{7,3},{8,12},{9,8},{10,1... | collective-permute-start | bytes 786440 | tf_op jit(solution)/shard_map/ppermute | solution.py:322
  129.1 12.8 %collective-permute-start.27 = (f32[128,512]{1,0:T(8,128)S(1)}, f32[128,512]{1,0:T(8,128)S(1)}, u32[]{:S(2)}, u32[]{:S(2)}) collective-permute-start(f32[128,512]{1,0:T(8,128)S(1)} %add.14.refs_0_), channel_id=1, source_target_pairs={{0,8},{1,9},{2,10},{3,11},{4,12},{5,13},{6,14},{7,15},{8,0},{9,1},... | collective-permute-start | bytes 786440 | tf_op jit(solution)/shard_map/ppermute | solution.py:322
  133.7 15.6 %collective-permute-start.22 = (f32[256,256]{1,0:T(8,128)}, f32[256,256]{1,0:T(8,128)S(1)}, u32[]{:S(2)}, u32[]{:S(2)}) collective-permute-start(f32[256,256]{1,0:T(8,128)} %get-tuple-element.50), channel_id=1, source_target_pairs={{1,4},{3,6},{4,1},{6,3},{9,12},{11,14},{12,9},{14,11},{17,20},{19,... | collective-permute-start | bytes 786440 | tf_op jit(solution)/shard_map/ppermute | solution.py:322
  136.5 12.8 %collective-permute-start.25 = (f32[128,512]{1,0:T(8,128)S(1)}, f32[128,512]{1,0:T(8,128)S(1)}, u32[]{:S(2)}, u32[]{:S(2)}) collective-permute-start(f32[128,512]{1,0:T(8,128)S(1)} %add.14.refs_0_), channel_id=1, source_target_pairs={{0,4},{1,0},{2,6},{3,2},{4,5},{5,1},{6,7},{7,3},{8,12},{9,8},{10,1... | collective-permute-start | bytes 786440 | tf_op jit(solution)/shard_map/ppermute | solution.py:322
  136.6 8.6 %collective-permute-start.31 = (f32[128,256]{1,0:T(8,128)S(1)}, f32[128,256]{1,0:T(8,128)S(1)}, u32[]{:S(2)}, u32[]{:S(2)}) collective-permute-start(f32[128,256]{1,0:T(8,128)S(1)} %add.15), channel_id=1, source_target_pairs={{0,16},{1,17},{2,18},{3,19},{4,20},{5,21},{6,22},{7,23},{8,24},{9,... | collective-permute-start | bytes 393224 | tf_op jit(solution)/shard_map/ppermute | solution.py:322
  139.7 14.7 %collective-permute-start.26 = (f32[128,512]{1,0:T(8,128)S(1)}, f32[128,512]{1,0:T(8,128)S(1)}, u32[]{:S(2)}, u32[]{:S(2)}) collective-permute-start(f32[128,512]{1,0:T(8,128)S(1)} %add.14.refs_0_), channel_id=1, source_target_pairs={{1,4},{3,6},{4,1},{6,3},{9,12},{11,14},{12,9},{14,11},{17,20},{19,... | collective-permute-start | bytes 786440 | tf_op jit(solution)/shard_map/ppermute | solution.py:322
  141.9 14.2 %collective-permute-start.28 = (f32[128,512]{1,0:T(8,128)S(1)}, f32[128,512]{1,0:T(8,128)S(1)}, u32[]{:S(2)}, u32[]{:S(2)}) collective-permute-start(f32[128,512]{1,0:T(8,128)S(1)} %collective-permute-done.27.refs_3_), channel_id=1, source_target_pairs={{0,4},{1,0},{2,6},{3,2},{4,5},{5,1},{6,7},{7,3},{8,12},{9,8},{10,1... | collective-permute-start | bytes 786440 | tf_op jit(solution)/shard_map/ppermute | solution.py:322
  145.2 10.9 %collective-permute-start.29 = (f32[128,512]{1,0:T(8,128)S(1)}, f32[128,512]{1,0:T(8,128)S(1)}, u32[]{:S(2)}, u32[]{:S(2)}) collective-permute-start(f32[128,512]{1,0:T(8,128)S(1)} %collective-permute-done.27.refs_3_), channel_id=1, source_target_pairs={{1,4},{3,6},{4,1},{6,3},{9,12},{11,14},{12,9},{14,11},{17,20},{19,... | collective-permute-start | bytes 786440 | tf_op jit(solution)/shard_map/ppermute | solution.py:322
  149.3 5.3 %collective-permute-start.32 = (f32[128,256]{1,0:T(8,128)S(1)}, f32[128,256]{1,0:T(8,128)S(1)}, u32[]{:S(2)}, u32[]{:S(2)}) collective-permute-start(f32[128,256]{1,0:T(8,128)S(1)} %add.16.refs_6_), channel_id=1, source_target_pairs={{0,4},{1,0},{2,6},{3,2},{4,5},{5,1},{6,7},{7,3},{8,12},{9,8},{10,1... | collective-permute-start | bytes 393224 | tf_op jit(solution)/shard_map/ppermute | solution.py:322
  149.3 6.8 %collective-permute-start.33 = (f32[128,256]{1,0:T(8,128)S(1)}, f32[128,256]{1,0:T(8,128)S(1)}, u32[]{:S(2)}, u32[]{:S(2)}) collective-permute-start(f32[128,256]{1,0:T(8,128)S(1)} %add.16.refs_6_), channel_id=1, source_target_pairs={{1,4},{3,6},{4,1},{6,3},{9,12},{11,14},{12,9},{14,11},{17,20},{19,... | collective-permute-start | bytes 393224 | tf_op jit(solution)/shard_map/ppermute | solution.py:322
  (16 other events, 14.5 us)

commit v3 on v2

v3 whole, which is shorter than its diff:
```python
import functools

import jax
import jax.numpy as jnp
from jax import lax
from jax.experimental import pallas as pl
from jax.experimental.pallas import tpu as pltpu
from jax.sharding import PartitionSpec as P

AXES = ("prow", "pcol")
CHUNKS = 2
LAG = 0
OPT = {'CHUNKS': 2, 'LAG': 0, 'merge': 1, 'w2': 3, 'wtie': 1, 'relay': 4, 'half': 1, 'one': 1, 'gram': 0, 'early': 1, 'ztwo': 1, 'zone': 2, 'home': 0}
FREE = pl.CostEstimate(flops=0, bytes_accessed=0, transcendentals=0)
F32 = jnp.float32
VMEM = pl.BlockSpec(memory_space=pltpu.VMEM)
SMEM = pl.BlockSpec(memory_space=pltpu.SMEM)
NN = ((1,), (0,))
NT = ((1,), (1,))
TN = ((0,), (0,))


def halves(value):
    high = value.astype(jnp.bfloat16)
    return high, (value - high.astype(F32)).astype(jnp.bfloat16)


def dot3(left, right, dims):
    def one(a, b):
        return lax.dot_general(a, b, (dims, ((), ())), preferred_element_type=F32)

    return one(left[0], right[0]) + (one(left[0], right[1]) + one(left[1], right[0]))


def place_of():
    my_row, my_col = lax.axis_index("prow"), lax.axis_index("pcol")
    return my_row // 2, my_row % 2, my_col // 2, my_col % 2


def family_order(parent_ref, my_col):
    parents = [parent_ref[my_col * 4 + i] - my_col * 2 for i in range(4)]
    place = []
    for i in range(4):
        seen = jnp.int32(0)
        for j in range(i):
            seen += jnp.where(parents[j] == parents[i], 1, 0)
        place.append(2 * parents[i] + seen)
    order = []
    for j in range(4):
        found = jnp.int32(0)
        for i in range(1, 4):
            found += jnp.where(place[i] == j, i, 0)
        order.append(found)
    return order


def below(size, shape, axis):
    return (lax.broadcasted_iota(jnp.int32, shape, axis) < size).astype(F32)


def pick(values, index):
    out = values[0]
    for i in range(1, len(values)):
        out = jnp.where(index == i, values[i], out)
    return out


def pack_one(factor_ref, first_ref, size_ref, kept_ref, give_ref):
    my_row, my_col = lax.axis_index("prow"), lax.axis_index("pcol")
    y = my_row % 2
    for out_ref, f in ((kept_ref, y), (give_ref, 1 - y)):
        block = out_ref.shape[0]
        values = factor_ref[:, pl.ds(pl.multiple_of(f * block, 128), block)]
        on = first_ref[my_row, my_col * 2 + f].astype(F32)
        keep = below(size_ref[my_col * 2 + f], values.shape, 1) * on
        out_ref[...] = (values * keep).T


def pack_two(factor_ref, first_ref, second_ref, parent_ref, size_ref, kept_ref, give_ref):
    my_row, my_col = lax.axis_index("prow"), lax.axis_index("pcol")
    y = my_row % 2
    order = family_order(parent_ref, my_col)
    for out_ref, f in ((kept_ref, y), (give_ref, 1 - y)):
        block = out_ref.shape[0] // 2
        for i in range(2):
            child = pick([order[i], order[2 + i]], f)
            values = factor_ref[:, pl.ds(pl.multiple_of(child * block, 128), block)]
            on = first_ref[my_row, my_col * 2 + f] * second_ref[my_row, my_col * 4 + child]
            keep = below(size_ref[my_col * 4 + child], values.shape, 1) * on.astype(F32)
            out_ref[i * block : (i + 1) * block, :] = (values * keep).T


def pack(one_ref, two_ref, first_ref, second_ref, parent_ref, size1_ref, size2_ref, kept_ref, give_ref):
    my_row, my_col = lax.axis_index("prow"), lax.axis_index("pcol")
    y = my_row % 2
    order = family_order(parent_ref, my_col)
    wide = kept_ref.shape[0] // 2
    block = wide // 2
    for out_ref, f in ((kept_ref, y), (give_ref, 1 - y)):
        values = one_ref[:, pl.ds(pl.multiple_of(f * wide, 128), wide)]
        on = first_ref[my_row, my_col * 2 + f]
        keep = below(size1_ref[my_col * 2 + f], values.shape, 1) * on.astype(F32)
        out_ref[:wide] = (values * keep).T
        for i in range(2):
            child = pick([order[i], order[2 + i]], f)
            values = two_ref[:, pl.ds(pl.multiple_of(child * block, 128), block)]
            both = (on * second_ref[my_row, my_col * 4 + child]).astype(F32)
            keep = below(size2_ref[my_col * 4 + child], values.shape, 1) * both
            out_ref[wide + i * block : wide + (i + 1) * block] = (values * keep).T


def join(kept_ref, near_ref, far_ref, *outs):
    _, y, _, k = place_of()
    rows = kept_ref.shape[1]
    for c, out_ref in enumerate(outs):
        cut = slice(c * out_ref.shape[0], (c + 1) * out_ref.shape[0])

        @pl.when(k == y)
        def _():
            out_ref[:, :rows] = kept_ref[cut, :]
            out_ref[:, rows:] = near_ref[cut, :]

        @pl.when(k != y)
        def _():
            out_ref[:, :rows] = near_ref[cut, :]
            out_ref[:, rows:] = far_ref[cut, :]


def partial_products(wide, counts, w2_ref, *refs):
    parts_ref, high_ref, low_ref = refs[-3:]
    _, y, x, k = place_of()
    rows, tile = refs[0].shape
    tiles, start = [], 0
    for count in counts:
        tiles.append(refs[start : start + count])
        start += count
    w2 = halves(w2_ref[...])
    same = (w2[0][:, :rows], w2[1][:, :rows])
    other = (w2[0][:, rows:], w2[1][:, rows:])
    for s in range(wide):
        for c in range(2):
            top, bottom = tiles[0][0], tiles[0][1:]
            del tiles[0]
            first = (lax.rem(x + wide - s, wide) * 2 + (k if c == 0 else 1 - k)) * (tile // rows)
            for b in range(tile // rows):
                block = first + b
                block = block - lax.rem(block, 2) + jnp.where(y == 0, lax.rem(block, 2), 1 - lax.rem(block, 2))
                at = pl.ds(pl.multiple_of(block * rows, 128), rows)
                cut = slice(b * rows, (b + 1) * rows)
                a = halves(top[:, cut])
                high_ref[:rows, at], low_ref[:rows, at] = a
                done = dot3(same, a, NN)
                a = halves(jnp.concatenate([ref[:, cut] for ref in bottom], axis=0))
                high_ref[rows:, at], low_ref[rows:, at] = a
                parts_ref[:, at] = done + dot3(other, a, NN)


def combine(depth, s, up_ref, down_ref, part_up_ref, part_down_ref, go_up_ref, go_down_ref):
    z = lax.axis_index("prow") // 2

    @pl.when(z <= s - 2 - LAG)
    def _():
        go_up_ref[...] = up_ref[...] + part_up_ref[...]

    @pl.when(z > s - 2 - LAG)
    def _():
        go_up_ref[...] = up_ref[...]

    @pl.when(depth - 1 - z <= s - 2 - LAG)
    def _():
        go_down_ref[...] = down_ref[...] + part_down_ref[...]

    @pl.when(depth - 1 - z > s - 2 - LAG)
    def _():
        go_down_ref[...] = down_ref[...]


def line_of(value):
    shape = value.shape
    same = lax.broadcasted_iota(jnp.int32, shape, 0) == lax.broadcasted_iota(jnp.int32, shape, 1)
    return jnp.sum(jnp.where(same, value, 0.0), axis=0, keepdims=True)


def fold(upper, lower):
    shape = upper.shape
    row, column = lax.broadcasted_iota(jnp.int32, shape, 0), lax.broadcasted_iota(jnp.int32, shape, 1)
    return jnp.where(row <= column, 0.5 * (upper + upper.T), 0.5 * (lower + lower.T))


def unfold(folded, line):
    shape = folded.shape
    row, column = lax.broadcasted_iota(jnp.int32, shape, 0), lax.broadcasted_iota(jnp.int32, shape, 1)
    turned = folded.T
    upper = jnp.where(row <= column, folded, turned)
    lower = jnp.where(row > column, folded, jnp.where(row < column, turned, line))
    return upper, lower


def all_rows(refs):
    return jnp.concatenate([ref[...] for ref in refs], axis=0)


def panel_product(high_ref, low_ref, value, at):
    span = value.shape[1]
    columns = pl.ds(pl.multiple_of(at * span, 128), span)
    return dot3(halves(value), (high_ref[:, columns], low_ref[:, columns]), NT)


def own_product(high_ref, low_ref, *refs):
    refs[-1][...] = panel_product(high_ref, low_ref, all_rows(refs[:-1]), lax.axis_index("prow") // 2)


def add_products(depth, s, out_ref, total, high_ref, low_ref, from_below, from_above):
    z = lax.axis_index("prow") // 2
    out_ref[...] = total

    @pl.when(z >= s)
    def _():
        out_ref[...] += panel_product(high_ref, low_ref, all_rows(from_below), z - s)

    @pl.when(z + s < depth)
    def _():
        out_ref[...] += panel_product(high_ref, low_ref, all_rows(from_above), z + s)


def next_product(depth, s, chunks, high_ref, low_ref, total_ref, *refs):
    add_products(depth, s, refs[-1], total_ref[...], high_ref, low_ref, refs[:chunks], refs[chunks : 2 * chunks])


def gram_products(depth, s, chunks, high_ref, low_ref, before_ref, *refs):
    taken = refs[: 2 * chunks]
    w1_ref, w2_ref, y1_ref, mine_ref, theirs_ref, total_ref = refs[2 * chunks :]
    z = lax.axis_index("prow") // 2
    add_products(depth, s, total_ref, before_ref[...], high_ref, low_ref, taken[:chunks], taken[chunks:])
    y1_ref[...] = total_ref[...]
    y1, w1, w2 = halves(total_ref[...]), halves(w1_ref[...]), halves(w2_ref[...])
    half = mine_ref.shape[1] // 3
    cross = dot3(y1, w2, NT)
    gram = dot3(w1, y1, NT)
    first = jnp.concatenate([cross[:half], fold(gram[:half, :half], gram[half:, half:])], axis=1)
    middle = 0.5 * (gram[:half, half:] + gram[half:, :half].T)
    second = jnp.concatenate([cross[half:], middle], axis=1)
    low = z % 2 == 0
    line = jnp.concatenate([jnp.zeros((8, 2 * half), F32), jnp.broadcast_to(line_of(gram[half:, half:]), (8, half))], axis=1)
    mine_ref[:half] = jnp.where(low, first, second)
    theirs_ref[:half] = jnp.where(low, second, first)
    mine_ref[half:] = line
    theirs_ref[half:] = line


def energy_products(chunks, part_ref, *refs):
    from_below, from_above, (w2_ref, y1_ref) = refs[:chunks], refs[chunks : 2 * chunks], refs[2 * chunks : 2 * chunks + 2]
    same_ref, other_ref, give_ref, energy_ref = refs[2 * chunks + 2 :]
    _, y, _, k = place_of()
    wide, rows = y1_ref.shape[0], y1_ref.shape[1] // 2
    y2 = part_ref[...] + (all_rows(from_below) + all_rows(from_above))
    for start, values in ((0, y1_ref[...]), (wide, y2)):
        same_ref[start : start + wide] = values[:, :rows]
        other_ref[start : start + wide] = values[:, rows:]
        give_ref[start : start + wide] = jnp.where(k == y, values[:, rows:], values[:, :rows])
    y2, w2 = halves(y2), halves(w2_ref[...])
    block = energy_ref.shape[1]
    own = []
    for i in range(2):
        cut = slice(i * block, (i + 1) * block)
        own.append(dot3((w2[0][cut], w2[1][cut]), (y2[0][cut], y2[1][cut]), NT))
    energy_ref[:block] = fold(*own)
    energy_ref[block:] = jnp.broadcast_to(line_of(own[1]), (8, block))


def collect(depth, grams_ref, other_ref, *refs):
    out_ref = refs[-1]
    half = grams_ref.shape[1]
    low = (lax.axis_index("prow") // 2) % 2 == 0
    out_ref[:, :half] = jnp.where(low, grams_ref[...], other_ref[...])
    out_ref[:, half : 2 * half] = jnp.where(low, other_ref[...], grams_ref[...])
    total = refs[0][...]
    for ref in refs[1:-1]:
        total = total + ref[...]
    out_ref[:, 2 * half :] = total


def finish_rows(
    own, near, far, link_ref, first_ref, second_ref, parent_ref, one_ref, two_ref, out1, out2
):
    my_row, my_col = lax.axis_index("prow"), lax.axis_index("pcol")
    y, k = my_row % 2, my_col % 2
    b1, b2 = link_ref.shape[1:]
    order = family_order(parent_ref, my_col)
    for f, both in ((1 - y, near[...]), (y, jnp.where(k == y, own[...], far[...]))):
        y1, y2 = both[:b1].T, both[b1:].T
        on = first_ref[my_row, my_col * 2 + f]
        out1[:, pl.ds(pl.multiple_of(f * b1, 128), b1)] = -y1 * on.astype(F32)
        y1 = halves(y1)
        for i in range(2):
            child = pick([order[i], order[2 + i]], f)
            link = (
                link_ref[child]
                * below(one_ref[my_col * 2 + f], (b1, b2), 0)
                * below(two_ref[my_col * 4 + child], (b1, b2), 1)
            )
            both = (on * second_ref[my_row, my_col * 4 + child]).astype(F32)
            near = dot3(y1, halves(link), NN)
            out2[:, pl.ds(pl.multiple_of(child * b2, 128), b2)] = (near - y2[:, i * b2 : (i + 1) * b2]) * both


def finish_blocks(
    own, near, far, pivot1_ref, link_ref, pivot2_ref, parent_ref, one_ref, two_ref, out_diag, out_link, out_last, d_ref
):
    my_row, my_col = lax.axis_index("prow"), lax.axis_index("pcol")
    y, k = my_row % 2, my_col % 2
    b1, b2 = link_ref.shape[1:]
    order = family_order(parent_ref, my_col)
    for f, sums in ((1 - y, near[...]), (y, jnp.where(k == y, own[...], far[...]))):
        line = sums[b2 : b2 + 1]
        sums = sums[:b2]
        upper, lower = unfold(sums[:, 2 * b2 : 3 * b2], line[:, 2 * b2 : 3 * b2])
        d_ref[:b2, :b2] = upper
        d_ref[:b2, b2:] = sums[:, 5 * b2 : 6 * b2]
        d_ref[b2:, :b2] = sums[:, 5 * b2 : 6 * b2].T
        d_ref[b2:, b2:] = lower
        energy = unfold(sums[:, 6 * b2 :], line[:, 6 * b2 :])
        crosses = jnp.concatenate([sums[:, : 2 * b2], sums[:, 3 * b2 : 5 * b2]], axis=0)
        size = one_ref[my_col * 2 + f]
        diag = pivot1_ref[f] * below(size, (b1, b1), 0) * below(size, (b1, b1), 1) + d_ref[...]
        out_diag[f] = diag
        diag = halves(diag)
        for i in range(2):
            child = pick([order[i], order[2 + i]], f)
            width = two_ref[my_col * 4 + child]
            link = halves(link_ref[child] * below(size, (b1, b2), 0) * below(width, (b1, b2), 1))
            cross = crosses[:, i * b2 : (i + 1) * b2]
            down = cross - dot3(diag, link, NN)
            out_link[child] = down
            pivot = pivot2_ref[child] * below(width, (b2, b2), 0) * below(width, (b2, b2), 1)
            out_last[child] = pivot - dot3(link, halves(down), TN) - dot3(halves(cross), link, TN) + energy[i]


def call(body, outs, ins, scratch=(), scalars=0, name=None, room=8):
    specs = [VMEM] * (len(ins) - scalars) + [SMEM] * scalars
    return pl.pallas_call(
        body,
        out_shape=outs,
        in_specs=specs,
        out_specs=[VMEM] * len(outs),
        scratch_shapes=list(scratch),
        name=name,
        compiler_params=pltpu.CompilerParams(vmem_limit_bytes=room * 2**20),
        cost_estimate=FREE,
    )(*ins)


def array(*shape, dtype=F32):
    return jax.ShapeDtypeStruct(shape, dtype)


def solution(mesh):
    rows_of, cols_of = mesh.shape["prow"], mesh.shape["pcol"]
    depth, wide = rows_of // 2, cols_of // 2

    def pairs(move):
        out = []
        for z in range(depth):
            for y in range(2):
                for x in range(wide):
                    for k in range(2):
                        to = move(z, y, x, k)
                        if to is not None:
                            a, b, c, d = to
                            out.append(((z * 2 + y) * cols_of + x * 2 + k, (a * 2 + b) * cols_of + c * 2 + d))
        return out

    to_worker = pairs(lambda z, y, x, k: (z, y, x, 1 - k) if k == y else (z, 1 - y, x, k))
    to_home = pairs(lambda z, y, x, k: (z, 1 - y, x, k) if k == y else (z, y, x, 1 - k))
    across = pairs(lambda z, y, x, k: None if k == y else (z, 1 - y, x, 1 - k))
    other_y = pairs(lambda z, y, x, k: (z, 1 - y, x, k))
    other_core = pairs(lambda z, y, x, k: (z, y, x, 1 - k))
    up = pairs(lambda z, y, x, k: (z + 1, y, x, k) if z + 1 < depth else None)
    down = pairs(lambda z, y, x, k: (z - 1, y, x, k) if z > 0 else None)

    def send(value, perm):
        return lax.ppermute(value, AXES, perm)

    def on_device(
        anc_inverse,
        factor_one,
        pivot_one,
        factor_two,
        factor_link,
        pivot_two,
        pattern_one,
        pattern_two,
        parent_two,
        size_one,
        size_two,
    ):
        rows, tile = anc_inverse.shape
        total = tile * cols_of
        span = 2 * rows
        b1, b2 = pivot_one.shape[1], pivot_two.shape[1]
        z = lax.axis_index("prow") // 2
        block = array(b1, rows)
        scalars = [pattern_one, pattern_two, parent_two, size_one, size_two]
        def tie(*values):
            return lax.optimization_barrier(values)

        piece = array(b1 // CHUNKS, span)
        beside = send(anc_inverse, other_y)
        turns = [pairs(lambda z, y, x, k: (z, y, (x + s) % wide, k)) for s in range(1, wide)]
        tops = [send(anc_inverse, turn) for turn in turns]
        if OPT["merge"]:
            kept, give = call(
                pack, [array(2 * b1, rows)] * 2, [factor_one, factor_two] + scalars, scalars=5, name="pack"
            )
            near, far = send(give, to_worker), send(kept, across)
            if OPT["wtie"]:
                near, far, beside = tie(near, far, beside)
            w1, w2 = call(join, [array(b1, span)] * 2, [kept, near, far], name="join")
            give1 = give
        else:
            kept1, give1 = call(pack_one, [block] * 2, [factor_one, pattern_one, size_one], scalars=2, name="pack_one")
            near1, far1 = send(give1, to_worker), send(kept1, across)
            if OPT["w2"] == 1:
                factor_two, _ = tie(factor_two, give1)
            if OPT["w2"] == 2:
                factor_two, near1, far1 = tie(factor_two, near1, far1)
            if OPT["w2"] == 3:
                factor_two, near1, far1, beside = tie(factor_two, near1, far1, beside)
            kept2, give2 = call(
                pack_two,
                [block] * 2,
                [factor_two, pattern_one, pattern_two, parent_two, size_two],
                scalars=4,
                name="pack_two",
            )
            if OPT["wtie"] == 1:
                near1, far1, kept2, give2 = tie(near1, far1, kept2, give2)
            if OPT["wtie"] == 2:
                near1, far1, beside = tie(near1, far1, beside)
            (w1,) = call(join, [array(b1, span)], [kept1, near1, far1], name="join_one")
            if OPT["wtie"] == 3:
                w1, kept2, give2 = tie(w1, kept2, give2)
            near2, far2 = send(give2, to_worker), send(kept2, across)
            if OPT["wtie"] == 4:
                near1, far1, near2, far2 = tie(near1, far1, near2, far2)
            (w2,) = call(join, [array(b1, span)], [kept2, near2, far2], name="join_two")
        passed = beside
        if OPT["relay"] == 1:
            passed, _ = tie(beside, give1)
        if OPT["relay"] == 2:
            passed, w1 = tie(beside, w1)
        if OPT["relay"] == 3:
            passed, _ = tie(beside, w1)
        if OPT["relay"] == 4:
            passed, w1, *tops = tie(beside, w1, *tops)
        middle = rows // 2
        tiles = [[anc_inverse, beside]]
        for turn, top in zip(turns, tops):
            if OPT["half"]:
                tiles.append([top, send(passed[:middle], turn), send(top[middle:], other_y)])
            else:
                tiles.append([top, send(passed, turn)])
        from_below, from_above = [send(w1, up)], [send(w1, down)]
        if OPT["one"] == 1:
            w2, from_below, from_above = tie(w2, from_below, from_above)
        if OPT["one"] == 2:
            tiles[1:], from_below, from_above = tie(tiles[1:], from_below, from_above)
        if OPT["one"] == 3:
            tiles[1][1], from_below, from_above = tie(tiles[1][1], from_below, from_above)
        panel = []
        for mine in tiles:
            panel += mine + [send(v, other_core) for v in mine]
        parts, high, low = call(
            functools.partial(partial_products, wide, [len(m) for m in tiles for _ in range(2)]),
            [array(b1, total), array(span, total, dtype=jnp.bfloat16), array(span, total, dtype=jnp.bfloat16)],
            [w2] + panel,
            name="partial_products",
            room=20,
        )

        def combined(s, c, from_below, from_above):
            whole = pl.BlockSpec(piece.shape, lambda i, at: (0, 0))
            taken = pl.BlockSpec(piece.shape, lambda i, at: (c if s == 2 + LAG else 0, 0))
            spec = pltpu.PrefetchScalarGridSpec(
                num_scalar_prefetch=1,
                grid=(1,),
                in_specs=[
                    taken,
                    taken,
                    pl.BlockSpec(piece.shape, lambda i, at: (c, jnp.clip(at[0] + 1 + depth + LAG - s, 0, depth - 1))),
                    pl.BlockSpec(piece.shape, lambda i, at: (c, jnp.clip(at[0] - 1 - depth - LAG + s, 0, depth - 1))),
                ],
                out_specs=[whole, whole],
            )

            def body(at_ref, *refs):
                combine(depth, s, *refs)

            return pl.pallas_call(
                body,
                grid_spec=spec,
                out_shape=[piece] * 2,
                name="combine",
                cost_estimate=FREE,
                compiler_params=pltpu.CompilerParams(vmem_limit_bytes=8 * 2**20),
            )(z[None], from_below, from_above, parts, parts)

        half = b1 // 2
        for s in range(1, depth + LAG):
            taken, chunks = from_below + from_above, len(from_below)
            blocks = range(1 if s <= LAG else CHUNKS)
            if s <= LAG:
                go = [(from_below[0], from_above[0])]
            else:
                go = [combined(s + 1, c, from_below[c % chunks], from_above[c % chunks]) for c in blocks]
            if s == depth - 1 and OPT["gram"] == 1:
                y1, go = tie(y1, go)
            if s == depth - 1 and OPT["gram"] == 2:
                y1, go[0] = tie(y1, go[0])
            from_below = [send(go[c][0], up) for c in blocks]
            from_above = [send(go[c][1], down) for c in blocks]
            if s == 1:
                (y1,) = call(own_product, [array(b1, span)], [high, low, w1], name="own_product", room=20)
            if s < depth - 1:
                (y1,) = call(
                    functools.partial(next_product, depth, s, chunks),
                    [array(b1, span)],
                    [high, low, y1] + taken,
                    name="next_product",
                    room=20,
                )
                if OPT["early"]:
                    y1, go = tie(y1, go)
            if s == depth - 1:
                y1, mine, theirs = call(
                    functools.partial(gram_products, depth, s, chunks),
                    [array(b1, span)] + [array(half + 8, 3 * half)] * 2,
                    [high, low, y1] + taken + [w1, w2],
                    scratch=[pltpu.VMEM((b1, span), F32)],
                    name="gram_products",
                    room=20,
                )

        def swap(value, step):
            return send(value, pairs(lambda z, y, x, k: (z ^ step, y, x, k)))

        def deliver(same, give, other):
            return [same, send(give, to_home), send(other, across)]

        grams = mine + swap(theirs, 1)
        if OPT["ztwo"]:
            grams, from_below[0], from_above[0] = tie(grams, from_below[0], from_above[0])
        step = 2
        while 2 * step < depth:
            grams = grams + swap(grams, step)
            step *= 2
        arrived = swap(grams, step)

        def last_part():
            whole = pl.BlockSpec((b1, span), lambda i, at: (0, 0))
            part = pl.BlockSpec(piece.shape, lambda i, at: (0, 0))
            small = pl.BlockSpec((2 * b1, rows), lambda i, at: (0, 0))
            spec = pltpu.PrefetchScalarGridSpec(
                num_scalar_prefetch=1,
                grid=(1,),
                in_specs=[pl.BlockSpec((b1, span), lambda i, at: (0, at[0]))] + [part] * (2 * CHUNKS) + [whole, whole],
                out_specs=[small] * 3 + [pl.BlockSpec((b2 + 8, b2), lambda i, at: (0, 0))],
            )

            def body(at_ref, *refs):
                energy_products(CHUNKS, *refs)

            return pl.pallas_call(
                body,
                grid_spec=spec,
                out_shape=[array(2 * b1, rows)] * 3 + [array(b2 + 8, b2)],
                name="energy",
                cost_estimate=FREE,
                compiler_params=pltpu.CompilerParams(vmem_limit_bytes=12 * 2**20),
            )(z[None], parts, *from_below, *from_above, w2, y1)

        same, other, give, energy = last_part()
        home = deliver(same, give, other)
        if OPT["zone"] == 2:
            arrived, energy = tie(arrived, energy)
        step = 1
        while 2 * step < depth:
            energy = energy + swap(energy, step)
            step *= 2
        if OPT["zone"] == 1:
            arrived, energy = tie(arrived, energy)
        grams = grams + arrived
        grams_too = swap(grams, 1)
        energies = [energy, swap(energy, step)]
        if OPT["home"] == 1:
            grams_too, home = tie(grams_too, home)
        if OPT["home"] == 2:
            grams, home = tie(grams, home)
        (sums,) = call(
            functools.partial(collect, depth), [array(half + 8, 7 * half)], [grams, grams_too] + energies, name="collect"
        )
        sums = deliver(sums, sums, sums)
        inverse_one, inverse_two = call(
            finish_rows,
            [array(rows, 2 * b1), array(rows, 4 * b2)],
            home + [factor_link] + scalars,
            scalars=5,
            name="finish_rows",
            room=16,
        )

        diagonal_one, inverse_link, diagonal_two = call(
            finish_blocks,
            [array(*pivot_one.shape), array(*factor_link.shape), array(*pivot_two.shape)],
            sums + [pivot_one, factor_link, pivot_two] + scalars[2:],
            scratch=[pltpu.VMEM((b1, b1), F32)],
            scalars=3,
            name="finish_blocks",
            room=16,
        )
        return inverse_one, diagonal_one, inverse_two, inverse_link, diagonal_two

    return jax.shard_map(
        on_device,
        mesh=mesh,
        in_specs=(
            P("prow", "pcol"),
            P("prow", "pcol"),
            P("pcol", None, None),
            P("prow", "pcol"),
            P("pcol", None, None),
            P("pcol", None, None),
            P(),
            P(),
            P(),
            P(),
            P(),
        ),
        out_specs=(
            P("prow", "pcol"),
            P("pcol", None, None),
            P("prow", "pcol"),
            P("pcol", None, None),
            P("pcol", None, None),
        ),
        check_vma=False,
    )
```

time: 160 us -> 138 us (0.86)
  Pallas kernels: 27.3 us -> 14.8 us
  local copies, waits for them, and re-layouts: 17.5 us -> 5.5 us
  starting transfers between devices: 58.4 us -> 66.1 us
  waiting for transfers between devices: 53.9 us -> 49.9 us
    unnamed x60 -> x30, local copies, waits for them, and re-layouts: 17.5 us -> 5.46 us
    pallas_call x4 -> x7, Pallas kernels: 10.3 us -> 1.13 us  [the longest x1 0.59 us: last_part(): pl.pallas_call(body, grid_spec=spec, out_shape=[array(2 * b1, rows)] * 3...]
    ppermute x34, starting transfers between devices: 58.4 us -> 66.1 us  [send(): return lax.ppermute(value, AXES, perm)]
    ppermute x34, waiting for transfers between devices: 53.9 us -> 49.9 us  [send(): return lax.ppermute(value, AXES, perm)]
    pallas_call x8 -> x10, Pallas kernels: 16.9 us -> 13.7 us  [call(): pl.pallas_call(body, out_shape=outs, in_specs=specs, out_specs=[VMEM] * l...]
  transfers between devices with their start and end apart: 34 -> 34, of which waited for: 14 -> 15; matrix products, arithmetic and copies ran while one was open for 1% -> 0% of each run, Pallas kernels for 10% -> 6%
where the time goes in v3:
time: 138 us; the launch traced here: 137 us
  starting transfers between devices  66.1 us (48%)
  waiting for transfers between devices  49.9 us (36%)
  Pallas kernels  14.8 us (11%)
  local copies, waits for them, and re-layouts  5.5 us (4%)
    ppermute x34, starting transfers between devices, send(): return lax.ppermute(value, AXES, perm)  66.1 us
    ppermute x34, waiting for transfers between devices, send(): return lax.ppermute(value, AXES, perm)  49.9 us
    pallas_call x10, Pallas kernels, call(): pl.pallas_call(body, out_shape=outs, in_specs=specs, out_specs=[VMEM] * l...  13.7 us
    unnamed x30, local copies, waits for them, and re-layouts  5.46 us
  transfers between devices with their start and end apart: 34, of which 15 were waited for; matrix products, arithmetic and copies ran while one was open for 0% of the time, Pallas kernels for 6%

profile of v3, /device:TPU:1, one launch (start us, length us, event | category | flops | bytes accessed | tf_op | source)
XLA Modules:
  0.0 137.5 jit_solution(9928507733490061533)
XLA Ops:
  0.6 2.1 %collective-permute-start.2 = (f32[256,512]{1,0:T(8,128)}, f32[256,512]{1,0:T(8,128)S(1)}, u32[]{:S(2)}, u32[]{:S(2)}) collective-permute-start(f32[256,512]{1,0:T(8,128)} %refs_0_.1), channel_id=1, source_target_pairs={{0,4},{1,5},{2,6},{3,7},{4,0},{5,1},{6,2},{7,3},{8,12},{9,13},{10,... | collective-permute-start | bytes 1572872 | tf_op jit(solution)/shard_map/ppermute | solution.py:382
  2.8 1.0 copy-done.1
  3.8 1.0 copy-done.2
  4.9 0.7 copy-done.5
  8.2 1.0 pack.1
  9.3 4.5 %collective-permute-start.1 = (f32[512,256]{1,0:T(8,128)S(1)}, f32[512,256]{1,0:T(8,128)S(1)}, u32[]{:S(2)}, u32[]{:S(2)}) collective-permute-start(f32[512,256]{1,0:T(8,128)S(1)} %get-tuple-element.52.kept_ref), channel_id=1, source_target_pairs={{1,4},{3,6},{4,1},{6,3},{9,12},{11,14},{12,9},{14,11},{17,20},{19,... | collective-permute-start | bytes 1572872 | tf_op jit(solution)/shard_map/ppermute | solution.py:382
  13.7 1.3 collective-permute-start.3
  15.0 5.3 %collective-permute-done.near_ref = f32[512,256]{1,0:T(8,128)S(1)} collective-permute-done((f32[512,256]{1,0:T(8,128)S(1)}, f32[512,256]{1,0:T(8,128)S(1)}, u32[]{:S(2)}, u32[]{:S(2)}) %collective-permute-start) | collective-permute-done | bytes 524320 | tf_op jit(solution)/shard_map/ppermute | solution.py:382
  20.3 6.1 %collective-permute-done.1.far_ref = f32[512,256]{1,0:T(8,128)S(1)} collective-permute-done((f32[512,256]{1,0:T(8,128)S(1)}, f32[512,256]{1,0:T(8,128)S(1)}, u32[]{:S(2)}, u32[]{:S(2)}) %collective-permute-start.1) | collective-permute-done | bytes 524320 | tf_op jit(solution)/shard_map/ppermute | solution.py:382
  26.5 1.3 collective-permute-start.5
  27.8 4.1 %collective-permute-start.4 = (f32[256,512]{1,0:T(8,128)S(1)}, f32[256,512]{1,0:T(8,128)S(1)}, u32[]{:S(2)}, u32[]{:S(2)}) collective-permute-start(f32[256,512]{1,0:T(8,128)S(1)} %get-tuple-element.59.refs_0_.refs_4_), channel_id=1, source_target_pairs={{0,8},{1,9},{2,10},{3,11},{4,12},{5,13},{6,14},{7,15},{8,16},{9,17... | collective-permute-start | bytes 1572872 | tf_op jit(solution)/shard_map/ppermute | solution.py:382
  32.0 1.4 %collective-permute-start.8 = (f32[128,512]{1,0:T(8,128)S(1)}, f32[128,512]{1,0:T(8,128)}, u32[]{:S(2)}, u32[]{:S(2)}) collective-permute-start(f32[128,512]{1,0:T(8,128)S(1)} %slice.6), channel_id=1, source_target_pairs={{0,2},{1,3},{2,0},{3,1},{4,6},{5,7},{6,4},{7,5},{8,10},{9,11},{10,... | collective-permute-start | bytes 786440 | tf_op jit(solution)/shard_map/ppermute | solution.py:382
  33.4 3.0 %collective-permute-start.6 = (f32[256,512]{1,0:T(8,128)}, f32[256,512]{1,0:T(8,128)}, u32[]{:S(2)}, u32[]{:S(2)}) collective-permute-start(f32[256,512]{1,0:T(8,128)} %refs_0_.1), channel_id=1, source_target_pairs={{0,1},{1,0},{2,3},{3,2},{4,5},{5,4},{6,7},{7,6},{8,9},{9,8},{10,11... | collective-permute-start | bytes 1572872 | tf_op jit(solution)/shard_map/ppermute | solution.py:382
  36.5 2.5 %collective-permute-done.9.refs_6_ = f32[128,512]{1,0:T(8,128)S(1)} collective-permute-done((f32[128,512]{1,0:T(8,128)S(1)}, f32[128,512]{1,0:T(8,128)S(1)}, u32[]{:S(2)}, u32[]{:S(2)}) %collective-permute-start.9) | collective-permute-done | bytes 262176 | tf_op jit(solution)/shard_map/ppermute | solution.py:382
  39.0 1.7 %collective-permute-start.10 = (f32[256,512]{1,0:T(8,128)S(1)}, f32[256,512]{1,0:T(8,128)}, u32[]{:S(2)}, u32[]{:S(2)}) collective-permute-start(f32[256,512]{1,0:T(8,128)S(1)} %collective-permute-done.3.refs_4_), channel_id=1, source_target_pairs={{0,1},{1,0},{2,3},{3,2},{4,5},{5,4},{6,7},{7,6},{8,9},{9,8},{10,11... | collective-permute-start | bytes 1572872 | tf_op jit(solution)/shard_map/ppermute | solution.py:382
  40.7 0.8 collective-permute-start.7
  42.0 1.9 %collective-permute-done.12.refs_9_ = f32[128,512]{1,0:T(8,128)} collective-permute-done((f32[128,512]{1,0:T(8,128)S(1)}, f32[128,512]{1,0:T(8,128)}, u32[]{:S(2)}, u32[]{:S(2)}) %collective-permute-start.12) | collective-permute-done | bytes 262176 | tf_op jit(solution)/shard_map/ppermute | solution.py:382
  44.1 4.1 %partial_products.1 = (f32[256,2048]{1,0:T(8,128)S(1)}, bf16[512,2048]{1,0:T(8,128)(2,1)S(1)}, bf16[512,2048]{1,0:T(8,128)(2,1)S(1)}) custom-call(f32[256,512]{1,0:T(8,128)S(1)} %get-tuple-element.60.w2_ref.refs_5_, f32[256,512]{1,0:T(8,128)} %refs_0_.1, f32[256,512]{1,0:T(8,128)S(1)} %collective-permute-done.2.refs_1_, ...), custom_call_target="tpu_custom_call" | custom-call | tf_op jit(solution)/shard_map/partial_products/pallas_call | solution.py:341
  48.3 3.3 %collective-permute-start.13 = (f32[128,512]{1,0:T(8,128)S(1)}, f32[128,512]{1,0:T(8,128)S(1)}, u32[]{:S(2)}, u32[]{:S(2)}) collective-permute-start(f32[128,512]{1,0:T(8,128)S(1)} %get-tuple-element.68), channel_id=1, source_target_pairs={{0,8},{1,9},{2,10},{3,11},{4,12},{5,13},{6,14},{7,15},{8,16},{9,17... | collective-permute-start | bytes 786440 | tf_op jit(solution)/shard_map/ppermute | solution.py:382
  51.7 1.3 collective-permute-start.15
  53.1 4.0 %collective-permute-start.14 = (f32[128,512]{1,0:T(8,128)S(1)}, f32[128,512]{1,0:T(8,128)S(1)}, u32[]{:S(2)}, u32[]{:S(2)}) collective-permute-start(f32[128,512]{1,0:T(8,128)S(1)} %get-tuple-element.70), channel_id=1, source_target_pairs={{0,8},{1,9},{2,10},{3,11},{4,12},{5,13},{6,14},{7,15},{8,16},{9,17... | collective-permute-start | bytes 786440 | tf_op jit(solution)/shard_map/ppermute | solution.py:382
  57.1 1.3 collective-permute-start.16
  58.4 2.4 %collective-permute-done.15.refs_2_.refs_1_ = f32[128,512]{1,0:T(8,128)S(1)} collective-permute-done((f32[128,512]{1,0:T(8,128)S(1)}, f32[128,512]{1,0:T(8,128)S(1)}, u32[]{:S(2)}, u32[]{:S(2)}) %collective-permute-start.15) | collective-permute-done | bytes 262176 | tf_op jit(solution)/shard_map/ppermute | solution.py:382
  60.8 3.2 %collective-permute-start.17 = (f32[128,512]{1,0:T(8,128)S(1)}, f32[128,512]{1,0:T(8,128)S(1)}, u32[]{:S(2)}, u32[]{:S(2)}) collective-permute-start(f32[128,512]{1,0:T(8,128)S(1)} %get-tuple-element.73), channel_id=1, source_target_pairs={{0,8},{1,9},{2,10},{3,11},{4,12},{5,13},{6,14},{7,15},{8,16},{9,17... | collective-permute-start | bytes 786440 | tf_op jit(solution)/shard_map/ppermute | solution.py:382
  64.1 1.3 collective-permute-start.19
  66.1 3.4 %collective-permute-start.18 = (f32[128,512]{1,0:T(8,128)S(1)}, f32[128,512]{1,0:T(8,128)S(1)}, u32[]{:S(2)}, u32[]{:S(2)}) collective-permute-start(f32[128,512]{1,0:T(8,128)S(1)} %get-tuple-element.75), channel_id=1, source_target_pairs={{0,8},{1,9},{2,10},{3,11},{4,12},{5,13},{6,14},{7,15},{8,16},{9,17... | collective-permute-start | bytes 786440 | tf_op jit(solution)/shard_map/ppermute | solution.py:382
  69.5 1.3 collective-permute-start.20
  70.8 1.0 collective-permute-done.19.refs_2_.refs_1_
  71.9 3.4 %collective-permute-start.22 = (f32[128,512]{1,0:T(8,128)S(1)}, f32[128,512]{1,0:T(8,128)S(1)}, u32[]{:S(2)}, u32[]{:S(2)}) collective-permute-start(f32[128,512]{1,0:T(8,128)S(1)} %get-tuple-element.80), channel_id=1, source_target_pairs={{0,8},{1,9},{2,10},{3,11},{4,12},{5,13},{6,14},{7,15},{8,16},{9,17... | collective-permute-start | bytes 786440 | tf_op jit(solution)/shard_map/ppermute | solution.py:382
  75.2 1.3 collective-permute-start.23
  78.5 1.3 gram_products.1
  79.9 2.1 %collective-permute-start.21 = (f32[136,384]{1,0:T(8,128)S(1)}, f32[136,384]{1,0:T(8,128)S(1)}, u32[]{:S(2)}, u32[]{:S(2)}) collective-permute-start(f32[136,384]{1,0:T(8,128)S(1)} %get-tuple-element.79), channel_id=1, source_target_pairs={{0,8},{1,9},{2,10},{3,11},{4,12},{5,13},{6,14},{7,15},{8,0},{9,1},... | collective-permute-start | bytes 626696 | tf_op jit(solution)/shard_map/ppermute | solution.py:382
  82.1 2.0 %collective-permute-start.24 = (f32[128,512]{1,0:T(8,128)S(1)}, f32[128,512]{1,0:T(8,128)S(1)}, u32[]{:S(2)}, u32[]{:S(2)}) collective-permute-start(f32[128,512]{1,0:T(8,128)S(1)} %get-tuple-element.83), channel_id=1, source_target_pairs={{0,8},{1,9},{2,10},{3,11},{4,12},{5,13},{6,14},{7,15},{8,16},{9,17... | collective-permute-start | bytes 786440 | tf_op jit(solution)/shard_map/ppermute | solution.py:382
  84.1 1.3 collective-permute-start.25
  85.4 2.3 %collective-permute-done.21 = f32[136,384]{1,0:T(8,128)S(1)} collective-permute-done((f32[136,384]{1,0:T(8,128)S(1)}, f32[136,384]{1,0:T(8,128)S(1)}, u32[]{:S(2)}, u32[]{:S(2)}) %collective-permute-start.21) | collective-permute-done | bytes 208928 | tf_op jit(solution)/shard_map/ppermute | solution.py:382
  87.7 0.7 collective-permute-start.28
  88.8 7.2 %collective-permute-done.25.refs_4_ = f32[128,512]{1,0:T(8,128)S(1)} collective-permute-done((f32[128,512]{1,0:T(8,128)S(1)}, f32[128,512]{1,0:T(8,128)S(1)}, u32[]{:S(2)}, u32[]{:S(2)}) %collective-permute-start.25) | collective-permute-done | bytes 262176 | tf_op jit(solution)/shard_map/ppermute | solution.py:382
  96.7 0.8 collective-permute-done.28
  97.5 1.5 %collective-permute-start.29 = (f32[136,384]{1,0:T(8,128)S(1)}, f32[136,384]{1,0:T(8,128)S(1)}, u32[]{:S(2)}, u32[]{:S(2)}) collective-permute-start(f32[136,384]{1,0:T(8,128)S(1)} %add.11.grams_ref), channel_id=1, source_target_pairs={{0,8},{1,9},{2,10},{3,11},{4,12},{5,13},{6,14},{7,15},{8,0},{9,1},... | collective-permute-start | bytes 626696 | tf_op jit(solution)/shard_map/ppermute | solution.py:382
  99.1 6.1 %collective-permute-done.30 = f32[136,128]{1,0:T(8,128)S(1)} collective-permute-done((f32[136,128]{1,0:T(8,128)S(1)}, f32[136,128]{1,0:T(8,128)S(1)}, u32[]{:S(2)}, u32[]{:S(2)}) %collective-permute-start.30) | collective-permute-done | bytes 69664 | tf_op jit(solution)/shard_map/ppermute | solution.py:382
  105.2 1.1 collective-permute-start.31
  106.3 5.6 %collective-permute-start.26 = (f32[512,256]{1,0:T(8,128)S(1)}, f32[512,256]{1,0:T(8,128)S(1)}, u32[]{:S(2)}, u32[]{:S(2)}) collective-permute-start(f32[512,256]{1,0:T(8,128)S(1)} %get-tuple-element.88), channel_id=1, source_target_pairs={{0,4},{1,0},{2,6},{3,2},{4,5},{5,1},{6,7},{7,3},{8,12},{9,8},{10,1... | collective-permute-start | bytes 1572872 | tf_op jit(solution)/shard_map/ppermute | solution.py:382
  111.9 1.9 %collective-permute-start.27 = (f32[512,256]{1,0:T(8,128)S(1)}, f32[512,256]{1,0:T(8,128)S(1)}, u32[]{:S(2)}, u32[]{:S(2)}) collective-permute-start(f32[512,256]{1,0:T(8,128)S(1)} %get-tuple-element.89), channel_id=1, source_target_pairs={{1,4},{3,6},{4,1},{6,3},{9,12},{11,14},{12,9},{14,11},{17,20},{19,... | collective-permute-start | bytes 1572872 | tf_op jit(solution)/shard_map/ppermute | solution.py:382
  113.9 5.2 %collective-permute-start.33 = (f32[136,896]{1,0:T(8,128)S(1)}, f32[136,896]{1,0:T(8,128)S(1)}, u32[]{:S(2)}, u32[]{:S(2)}) collective-permute-start(f32[136,896]{1,0:T(8,128)S(1)} %collect.1.own), channel_id=1, source_target_pairs={{1,4},{3,6},{4,1},{6,3},{9,12},{11,14},{12,9},{14,11},{17,20},{19,... | collective-permute-start | bytes 1462280 | tf_op jit(solution)/shard_map/ppermute | solution.py:382
  119.1 6.4 %collective-permute-done.27.far = f32[512,256]{1,0:T(8,128)S(1)} collective-permute-done((f32[512,256]{1,0:T(8,128)S(1)}, f32[512,256]{1,0:T(8,128)S(1)}, u32[]{:S(2)}, u32[]{:S(2)}) %collective-permute-start.27) | collective-permute-done | bytes 524320 | tf_op jit(solution)/shard_map/ppermute | solution.py:382
  125.6 2.1 %finish_rows.1 = (f32[256,512]{1,0:T(8,128)}, f32[256,512]{1,0:T(8,128)}) custom-call(f32[512,256]{1,0:T(8,128)S(1)} %get-tuple-element.87.own, f32[512,256]{1,0:T(8,128)S(1)} %collective-permute-done.26.near, f32[512,256]{1,0:T(8,128)S(1)} %collective-permute-done.27.far, f32[4,256,128]{2,1,0:T(8,128)S(1)} %copy-done, s32[8,8]{1,0:T(8,128)S(1)} %copy-done.6, ...), custom_call_target="tpu_custom_call" | custom-call | tf_op jit(solution)/shard_map/finish_rows/pallas_call | solution.py:341
  127.8 6.7 %collective-permute-done.33.far = f32[136,896]{1,0:T(8,128)S(1)} collective-permute-done((f32[136,896]{1,0:T(8,128)S(1)}, f32[136,896]{1,0:T(8,128)S(1)}, u32[]{:S(2)}, u32[]{:S(2)}) %collective-permute-start.33) | collective-permute-done | bytes 487456 | tf_op jit(solution)/shard_map/ppermute | solution.py:382
  134.5 3.0 %finish_blocks.1 = (f32[2,256,256]{2,1,0:T(8,128)}, f32[4,256,128]{2,1,0:T(8,128)}, f32[4,128,128]{2,1,0:T(8,128)}) custom-call(f32[136,896]{1,0:T(8,128)S(1)} %collect.1.own, f32[136,896]{1,0:T(8,128)S(1)} %collective-permute-done.32.near, f32[136,896]{1,0:T(8,128)S(1)} %collective-permute-done.33.far, f32[2,256,256]{2,1,0:T(8,128)S(1)} %copy-done.3, ...), custom_call_target="tpu_custom_call" | custom-call | tf_op jit(solution)/shard_map/finish_blocks/pallas_call | solution.py:341
  (72 shorter events, 7.9 us)
Async XLA Ops:
  0.6 14.4 %collective-permute-start.2 = (f32[256,512]{1,0:T(8,128)}, f32[256,512]{1,0:T(8,128)S(1)}, u32[]{:S(2)}, u32[]{:S(2)}) collective-permute-start(f32[256,512]{1,0:T(8,128)} %refs_0_.1), channel_id=1, source_target_pairs={{0,4},{1,5},{2,6},{3,7},{4,0},{5,1},{6,2},{7,3},{8,12},{9,13},{10,... | collective-permute-start | bytes 1572872 | tf_op jit(solution)/shard_map/ppermute | solution.py:382
  2.8 1.0 copy-start.1
  3.8 1.0 copy-start.2
  4.8 0.7 copy-start.5
  5.5 0.7 copy-start.7
  6.2 0.7 copy-start.9
  6.9 0.7 copy-start.11
  9.2 11.1 %collective-permute-start = (f32[512,256]{1,0:T(8,128)S(1)}, f32[512,256]{1,0:T(8,128)S(1)}, u32[]{:S(2)}, u32[]{:S(2)}) collective-permute-start(f32[512,256]{1,0:T(8,128)S(1)} %get-tuple-element.53), channel_id=1, source_target_pairs={{0,1},{1,5},{2,3},{3,7},{4,0},{5,4},{6,2},{7,6},{8,9},{9,13},{10,1... | collective-permute-start | bytes 1572872 | tf_op jit(solution)/shard_map/ppermute | solution.py:382
  9.3 17.1 %collective-permute-start.1 = (f32[512,256]{1,0:T(8,128)S(1)}, f32[512,256]{1,0:T(8,128)S(1)}, u32[]{:S(2)}, u32[]{:S(2)}) collective-permute-start(f32[512,256]{1,0:T(8,128)S(1)} %get-tuple-element.52.kept_ref), channel_id=1, source_target_pairs={{1,4},{3,6},{4,1},{6,3},{9,12},{11,14},{12,9},{14,11},{17,20},{19,... | collective-permute-start | bytes 1572872 | tf_op jit(solution)/shard_map/ppermute | solution.py:382
  13.7 12.7 %collective-permute-start.3 = (f32[256,512]{1,0:T(8,128)}, f32[256,512]{1,0:T(8,128)S(1)}, u32[]{:S(2)}, u32[]{:S(2)}) collective-permute-start(f32[256,512]{1,0:T(8,128)} %refs_0_.1), channel_id=1, source_target_pairs={{0,2},{1,3},{2,0},{3,1},{4,6},{5,7},{6,4},{7,5},{8,10},{9,11},{10,... | collective-permute-start | bytes 1572872 | tf_op jit(solution)/shard_map/ppermute | solution.py:382
  26.5 15.0 %collective-permute-start.5 = (f32[256,512]{1,0:T(8,128)S(1)}, f32[256,512]{1,0:T(8,128)S(1)}, u32[]{:S(2)}, u32[]{:S(2)}) collective-permute-start(f32[256,512]{1,0:T(8,128)S(1)} %get-tuple-element.59.refs_0_.refs_4_), channel_id=1, source_target_pairs={{8,0},{9,1},{10,2},{11,3},{12,4},{13,5},{14,6},{15,7},{16,8},{17,9... | collective-permute-start | bytes 1572872 | tf_op jit(solution)/shard_map/ppermute | solution.py:382
  27.8 13.7 %collective-permute-start.4 = (f32[256,512]{1,0:T(8,128)S(1)}, f32[256,512]{1,0:T(8,128)S(1)}, u32[]{:S(2)}, u32[]{:S(2)}) collective-permute-start(f32[256,512]{1,0:T(8,128)S(1)} %get-tuple-element.59.refs_0_.refs_4_), channel_id=1, source_target_pairs={{0,8},{1,9},{2,10},{3,11},{4,12},{5,13},{6,14},{7,15},{8,16},{9,17... | collective-permute-start | bytes 1572872 | tf_op jit(solution)/shard_map/ppermute | solution.py:382
  31.9 7.1 %collective-permute-start.9 = (f32[128,512]{1,0:T(8,128)S(1)}, f32[128,512]{1,0:T(8,128)S(1)}, u32[]{:S(2)}, u32[]{:S(2)}) collective-permute-start(f32[128,512]{1,0:T(8,128)S(1)} %slice.7), channel_id=1, source_target_pairs={{0,4},{1,5},{2,6},{3,7},{4,0},{5,1},{6,2},{7,3},{8,12},{9,13},{10,... | collective-permute-start | bytes 786440 | tf_op jit(solution)/shard_map/ppermute | solution.py:382
  32.0 8.7 %collective-permute-start.8 = (f32[128,512]{1,0:T(8,128)S(1)}, f32[128,512]{1,0:T(8,128)}, u32[]{:S(2)}, u32[]{:S(2)}) collective-permute-start(f32[128,512]{1,0:T(8,128)S(1)} %slice.6), channel_id=1, source_target_pairs={{0,2},{1,3},{2,0},{3,1},{4,6},{5,7},{6,4},{7,5},{8,10},{9,11},{10,... | collective-permute-start | bytes 786440 | tf_op jit(solution)/shard_map/ppermute | solution.py:382
  33.4 8.5 %collective-permute-start.6 = (f32[256,512]{1,0:T(8,128)}, f32[256,512]{1,0:T(8,128)}, u32[]{:S(2)}, u32[]{:S(2)}) collective-permute-start(f32[256,512]{1,0:T(8,128)} %refs_0_.1), channel_id=1, source_target_pairs={{0,1},{1,0},{2,3},{3,2},{4,5},{5,4},{6,7},{7,6},{8,9},{9,8},{10,11... | collective-permute-start | bytes 1572872 | tf_op jit(solution)/shard_map/ppermute | solution.py:382
  39.0 5.1 %collective-permute-start.10 = (f32[256,512]{1,0:T(8,128)S(1)}, f32[256,512]{1,0:T(8,128)}, u32[]{:S(2)}, u32[]{:S(2)}) collective-permute-start(f32[256,512]{1,0:T(8,128)S(1)} %collective-permute-done.3.refs_4_), channel_id=1, source_target_pairs={{0,1},{1,0},{2,3},{3,2},{4,5},{5,4},{6,7},{7,6},{8,9},{9,8},{10,11... | collective-permute-start | bytes 1572872 | tf_op jit(solution)/shard_map/ppermute | solution.py:382
  40.7 3.4 %collective-permute-start.7 = (f32[256,512]{1,0:T(8,128)S(1)}, f32[256,512]{1,0:T(8,128)}, u32[]{:S(2)}, u32[]{:S(2)}) collective-permute-start(f32[256,512]{1,0:T(8,128)S(1)} %collective-permute-done.2.refs_1_), channel_id=1, source_target_pairs={{0,1},{1,0},{2,3},{3,2},{4,5},{5,4},{6,7},{7,6},{8,9},{9,8},{10,11... | collective-permute-start | bytes 1572872 | tf_op jit(solution)/shard_map/ppermute | solution.py:382
  41.5 2.4 %collective-permute-start.12 = (f32[128,512]{1,0:T(8,128)S(1)}, f32[128,512]{1,0:T(8,128)}, u32[]{:S(2)}, u32[]{:S(2)}) collective-permute-start(f32[128,512]{1,0:T(8,128)S(1)} %collective-permute-done.9.refs_6_), channel_id=1, source_target_pairs={{0,1},{1,0},{2,3},{3,2},{4,5},{5,4},{6,7},{7,6},{8,9},{9,8},{10,11... | collective-permute-start | bytes 786440 | tf_op jit(solution)/shard_map/ppermute | solution.py:382
  41.5 2.6 %collective-permute-start.11 = (f32[128,512]{1,0:T(8,128)}, f32[128,512]{1,0:T(8,128)}, u32[]{:S(2)}, u32[]{:S(2)}) collective-permute-start(f32[128,512]{1,0:T(8,128)} %collective-permute-done.8.refs_5_), channel_id=1, source_target_pairs={{0,1},{1,0},{2,3},{3,2},{4,5},{5,4},{6,7},{7,6},{8,9},{9,8},{10,11... | collective-permute-start | bytes 786440 | tf_op jit(solution)/shard_map/ppermute | solution.py:382
  48.3 10.0 %collective-permute-start.13 = (f32[128,512]{1,0:T(8,128)S(1)}, f32[128,512]{1,0:T(8,128)S(1)}, u32[]{:S(2)}, u32[]{:S(2)}) collective-permute-start(f32[128,512]{1,0:T(8,128)S(1)} %get-tuple-element.68), channel_id=1, source_target_pairs={{0,8},{1,9},{2,10},{3,11},{4,12},{5,13},{6,14},{7,15},{8,16},{9,17... | collective-permute-start | bytes 786440 | tf_op jit(solution)/shard_map/ppermute | solution.py:382
  51.7 9.1 %collective-permute-start.15 = (f32[128,512]{1,0:T(8,128)S(1)}, f32[128,512]{1,0:T(8,128)S(1)}, u32[]{:S(2)}, u32[]{:S(2)}) collective-permute-start(f32[128,512]{1,0:T(8,128)S(1)} %get-tuple-element.69), channel_id=1, source_target_pairs={{8,0},{9,1},{10,2},{11,3},{12,4},{13,5},{14,6},{15,7},{16,8},{17,9... | collective-permute-start | bytes 786440 | tf_op jit(solution)/shard_map/ppermute | solution.py:382
  53.1 12.3 %collective-permute-start.14 = (f32[128,512]{1,0:T(8,128)S(1)}, f32[128,512]{1,0:T(8,128)S(1)}, u32[]{:S(2)}, u32[]{:S(2)}) collective-permute-start(f32[128,512]{1,0:T(8,128)S(1)} %get-tuple-element.70), channel_id=1, source_target_pairs={{0,8},{1,9},{2,10},{3,11},{4,12},{5,13},{6,14},{7,15},{8,16},{9,17... | collective-permute-start | bytes 786440 | tf_op jit(solution)/shard_map/ppermute | solution.py:382
  57.1 8.9 %collective-permute-start.16 = (f32[128,512]{1,0:T(8,128)S(1)}, f32[128,512]{1,0:T(8,128)S(1)}, u32[]{:S(2)}, u32[]{:S(2)}) collective-permute-start(f32[128,512]{1,0:T(8,128)S(1)} %get-tuple-element.71), channel_id=1, source_target_pairs={{8,0},{9,1},{10,2},{11,3},{12,4},{13,5},{14,6},{15,7},{16,8},{17,9... | collective-permute-start | bytes 786440 | tf_op jit(solution)/shard_map/ppermute | solution.py:382
  60.8 10.0 %collective-permute-start.17 = (f32[128,512]{1,0:T(8,128)S(1)}, f32[128,512]{1,0:T(8,128)S(1)}, u32[]{:S(2)}, u32[]{:S(2)}) collective-permute-start(f32[128,512]{1,0:T(8,128)S(1)} %get-tuple-element.73), channel_id=1, source_target_pairs={{0,8},{1,9},{2,10},{3,11},{4,12},{5,13},{6,14},{7,15},{8,16},{9,17... | collective-permute-start | bytes 786440 | tf_op jit(solution)/shard_map/ppermute | solution.py:382
  64.1 7.7 %collective-permute-start.19 = (f32[128,512]{1,0:T(8,128)S(1)}, f32[128,512]{1,0:T(8,128)S(1)}, u32[]{:S(2)}, u32[]{:S(2)}) collective-permute-start(f32[128,512]{1,0:T(8,128)S(1)} %get-tuple-element.74), channel_id=1, source_target_pairs={{8,0},{9,1},{10,2},{11,3},{12,4},{13,5},{14,6},{15,7},{16,8},{17,9... | collective-permute-start | bytes 786440 | tf_op jit(solution)/shard_map/ppermute | solution.py:382
  66.1 12.5 %collective-permute-start.18 = (f32[128,512]{1,0:T(8,128)S(1)}, f32[128,512]{1,0:T(8,128)S(1)}, u32[]{:S(2)}, u32[]{:S(2)}) collective-permute-start(f32[128,512]{1,0:T(8,128)S(1)} %get-tuple-element.75), channel_id=1, source_target_pairs={{0,8},{1,9},{2,10},{3,11},{4,12},{5,13},{6,14},{7,15},{8,16},{9,17... | collective-permute-start | bytes 786440 | tf_op jit(solution)/shard_map/ppermute | solution.py:382
  69.5 9.0 %collective-permute-start.20 = (f32[128,512]{1,0:T(8,128)S(1)}, f32[128,512]{1,0:T(8,128)S(1)}, u32[]{:S(2)}, u32[]{:S(2)}) collective-permute-start(f32[128,512]{1,0:T(8,128)S(1)} %get-tuple-element.76), channel_id=1, source_target_pairs={{8,0},{9,1},{10,2},{11,3},{12,4},{13,5},{14,6},{15,7},{16,8},{17,9... | collective-permute-start | bytes 786440 | tf_op jit(solution)/shard_map/ppermute | solution.py:382
  71.9 15.9 %collective-permute-start.22 = (f32[128,512]{1,0:T(8,128)S(1)}, f32[128,512]{1,0:T(8,128)S(1)}, u32[]{:S(2)}, u32[]{:S(2)}) collective-permute-start(f32[128,512]{1,0:T(8,128)S(1)} %get-tuple-element.80), channel_id=1, source_target_pairs={{0,8},{1,9},{2,10},{3,11},{4,12},{5,13},{6,14},{7,15},{8,16},{9,17... | collective-permute-start | bytes 786440 | tf_op jit(solution)/shard_map/ppermute | solution.py:382
  75.2 12.5 %collective-permute-start.23 = (f32[128,512]{1,0:T(8,128)S(1)}, f32[128,512]{1,0:T(8,128)S(1)}, u32[]{:S(2)}, u32[]{:S(2)}) collective-permute-start(f32[128,512]{1,0:T(8,128)S(1)} %get-tuple-element.81), channel_id=1, source_target_pairs={{8,0},{9,1},{10,2},{11,3},{12,4},{13,5},{14,6},{15,7},{16,8},{17,9... | collective-permute-start | bytes 786440 | tf_op jit(solution)/shard_map/ppermute | solution.py:382
  79.9 7.8 %collective-permute-start.21 = (f32[136,384]{1,0:T(8,128)S(1)}, f32[136,384]{1,0:T(8,128)S(1)}, u32[]{:S(2)}, u32[]{:S(2)}) collective-permute-start(f32[136,384]{1,0:T(8,128)S(1)} %get-tuple-element.79), channel_id=1, source_target_pairs={{0,8},{1,9},{2,10},{3,11},{4,12},{5,13},{6,14},{7,15},{8,0},{9,1},... | collective-permute-start | bytes 626696 | tf_op jit(solution)/shard_map/ppermute | solution.py:382
  82.1 6.7 %collective-permute-start.24 = (f32[128,512]{1,0:T(8,128)S(1)}, f32[128,512]{1,0:T(8,128)S(1)}, u32[]{:S(2)}, u32[]{:S(2)}) collective-permute-start(f32[128,512]{1,0:T(8,128)S(1)} %get-tuple-element.83), channel_id=1, source_target_pairs={{0,8},{1,9},{2,10},{3,11},{4,12},{5,13},{6,14},{7,15},{8,16},{9,17... | collective-permute-start | bytes 786440 | tf_op jit(solution)/shard_map/ppermute | solution.py:382
  84.1 11.9 %collective-permute-start.25 = (f32[128,512]{1,0:T(8,128)S(1)}, f32[128,512]{1,0:T(8,128)S(1)}, u32[]{:S(2)}, u32[]{:S(2)}) collective-permute-start(f32[128,512]{1,0:T(8,128)S(1)} %get-tuple-element.85), channel_id=1, source_target_pairs={{8,0},{9,1},{10,2},{11,3},{12,4},{13,5},{14,6},{15,7},{16,8},{17,9... | collective-permute-start | bytes 786440 | tf_op jit(solution)/shard_map/ppermute | solution.py:382
  87.7 9.7 %collective-permute-start.28 = (f32[136,384]{1,0:T(8,128)S(1)}, f32[136,384]{1,0:T(8,128)S(1)}, u32[]{:S(2)}, u32[]{:S(2)}) collective-permute-start(f32[136,384]{1,0:T(8,128)S(1)} %add.10), channel_id=1, source_target_pairs={{0,16},{1,17},{2,18},{3,19},{4,20},{5,21},{6,22},{7,23},{8,24},{9,... | collective-permute-start | bytes 626696 | tf_op jit(solution)/shard_map/ppermute | solution.py:382
  96.0 29.6 %copy-start = (f32[4,256,128]{2,1,0:T(8,128)S(1)}, f32[4,256,128]{2,1,0:T(8,128)}, u32[]{:S(2)}) copy-start(f32[4,256,128]{2,1,0:T(8,128)} %link_ref.3) | copy-start | bytes 1572868
  96.0 29.6 %copy-start.6 = (s32[8,8]{1,0:T(8,128)S(1)}, s32[8,8]{1,0:T(8,128)}, u32[]{:S(2)}) copy-start(s32[8,8]{1,0:T(8,128)} %first_ref.3) | copy-start | bytes 772
  96.0 29.6 %copy-start.8 = (s32[8,16]{1,0:T(8,128)S(1)}, s32[8,16]{1,0:T(8,128)}, u32[]{:S(2)}) copy-start(s32[8,16]{1,0:T(8,128)} %second_ref.3) | copy-start | bytes 1540
  96.0 29.6 %copy-start.10 = (s32[16]{0:T(128)S(1)}, s32[16]{0:T(128)}, u32[]{:S(2)}) copy-start(s32[16]{0:T(128)} %parent_ref.5) | copy-start | bytes 196
  96.0 29.6 %copy-start.12 = (s32[8]{0:T(128)S(1)}, s32[8]{0:T(128)}, u32[]{:S(2)}) copy-start(s32[8]{0:T(128)} %one_ref.5) | copy-start | bytes 100
  96.0 29.6 %copy-start.14 = (s32[16]{0:T(128)S(1)}, s32[16]{0:T(128)}, u32[]{:S(2)}) copy-start(s32[16]{0:T(128)} %two_ref.5) | copy-start | bytes 196
  96.6 37.9 %copy-start.3 = (f32[2,256,256]{2,1,0:T(8,128)S(1)}, f32[2,256,256]{2,1,0:T(8,128)}, u32[]{:S(2)}) copy-start(f32[2,256,256]{2,1,0:T(8,128)} %pivot1_ref.1) | copy-start | bytes 1572868
  96.7 37.9 %copy-start.4 = (f32[4,128,128]{2,1,0:T(8,128)S(1)}, f32[4,128,128]{2,1,0:T(8,128)}, u32[]{:S(2)}) copy-start(f32[4,128,128]{2,1,0:T(8,128)} %pivot2_ref.1) | copy-start | bytes 786436
  97.5 16.3 %collective-permute-start.29 = (f32[136,384]{1,0:T(8,128)S(1)}, f32[136,384]{1,0:T(8,128)S(1)}, u32[]{:S(2)}, u32[]{:S(2)}) collective-permute-start(f32[136,384]{1,0:T(8,128)S(1)} %add.11.grams_ref), channel_id=1, source_target_pairs={{0,8},{1,9},{2,10},{3,11},{4,12},{5,13},{6,14},{7,15},{8,0},{9,1},... | collective-permute-start | bytes 626696 | tf_op jit(solution)/shard_map/ppermute | solution.py:382
  99.0 6.2 %collective-permute-start.30 = (f32[136,128]{1,0:T(8,128)S(1)}, f32[136,128]{1,0:T(8,128)S(1)}, u32[]{:S(2)}, u32[]{:S(2)}) collective-permute-start(f32[136,128]{1,0:T(8,128)S(1)} %get-tuple-element.94), channel_id=1, source_target_pairs={{0,8},{1,9},{2,10},{3,11},{4,12},{5,13},{6,14},{7,15},{8,0},{9,1},... | collective-permute-start | bytes 208904 | tf_op jit(solution)/shard_map/ppermute | solution.py:382
  105.2 8.6 %collective-permute-start.31 = (f32[136,128]{1,0:T(8,128)S(1)}, f32[136,128]{1,0:T(8,128)S(1)}, u32[]{:S(2)}, u32[]{:S(2)}) collective-permute-start(f32[136,128]{1,0:T(8,128)S(1)} %add.12.refs_0_), channel_id=1, source_target_pairs={{0,16},{1,17},{2,18},{3,19},{4,20},{5,21},{6,22},{7,23},{8,24},{9,... | collective-permute-start | bytes 208904 | tf_op jit(solution)/shard_map/ppermute | solution.py:382
  106.3 12.8 %collective-permute-start.26 = (f32[512,256]{1,0:T(8,128)S(1)}, f32[512,256]{1,0:T(8,128)S(1)}, u32[]{:S(2)}, u32[]{:S(2)}) collective-permute-start(f32[512,256]{1,0:T(8,128)S(1)} %get-tuple-element.88), channel_id=1, source_target_pairs={{0,4},{1,0},{2,6},{3,2},{4,5},{5,1},{6,7},{7,3},{8,12},{9,8},{10,1... | collective-permute-start | bytes 1572872 | tf_op jit(solution)/shard_map/ppermute | solution.py:382
  111.9 13.7 %collective-permute-start.27 = (f32[512,256]{1,0:T(8,128)S(1)}, f32[512,256]{1,0:T(8,128)S(1)}, u32[]{:S(2)}, u32[]{:S(2)}) collective-permute-start(f32[512,256]{1,0:T(8,128)S(1)} %get-tuple-element.89), channel_id=1, source_target_pairs={{1,4},{3,6},{4,1},{6,3},{9,12},{11,14},{12,9},{14,11},{17,20},{19,... | collective-permute-start | bytes 1572872 | tf_op jit(solution)/shard_map/ppermute | solution.py:382
  113.9 20.6 %collective-permute-start.33 = (f32[136,896]{1,0:T(8,128)S(1)}, f32[136,896]{1,0:T(8,128)S(1)}, u32[]{:S(2)}, u32[]{:S(2)}) collective-permute-start(f32[136,896]{1,0:T(8,128)S(1)} %collect.1.own), channel_id=1, source_target_pairs={{1,4},{3,6},{4,1},{6,3},{9,12},{11,14},{12,9},{14,11},{17,20},{19,... | collective-permute-start | bytes 1462280 | tf_op jit(solution)/shard_map/ppermute | solution.py:382
  119.1 15.4 %collective-permute-start.32 = (f32[136,896]{1,0:T(8,128)S(1)}, f32[136,896]{1,0:T(8,128)S(1)}, u32[]{:S(2)}, u32[]{:S(2)}) collective-permute-start(f32[136,896]{1,0:T(8,128)S(1)} %collect.1.own), channel_id=1, source_target_pairs={{0,4},{1,0},{2,6},{3,2},{4,5},{5,1},{6,7},{7,3},{8,12},{9,8},{10,1... | collective-permute-start | bytes 1462280 | tf_op jit(solution)/shard_map/ppermute | solution.py:382
  (1 other events, 0.7 us)

commit v4 on v3

--- a/solution.py
+++ b/solution.py
@@ -9,8 +9,6 @@
 
 AXES = ("prow", "pcol")
 CHUNKS = 2
-LAG = 0
-OPT = {'CHUNKS': 2, 'LAG': 0, 'merge': 1, 'w2': 3, 'wtie': 1, 'relay': 4, 'half': 1, 'one': 1, 'gram': 0, 'early': 1, 'ztwo': 1, 'zone': 2, 'home': 0}
 FREE = pl.CostEstimate(flops=0, bytes_accessed=0, transcendentals=0)
 F32 = jnp.float32
 VMEM = pl.BlockSpec(memory_space=pltpu.VMEM)
@@ -88,25 +86,6 @@
             on = first_ref[my_row, my_col * 2 + f] * second_ref[my_row, my_col * 4 + child]
             keep = below(size_ref[my_col * 4 + child], values.shape, 1) * on.astype(F32)
             out_ref[i * block : (i + 1) * block, :] = (values * keep).T
-
-
-def pack(one_ref, two_ref, first_ref, second_ref, parent_ref, size1_ref, size2_ref, kept_ref, give_ref):
-    my_row, my_col = lax.axis_index("prow"), lax.axis_index("pcol")
-    y = my_row % 2
-    order = family_order(parent_ref, my_col)
-    wide = kept_ref.shape[0] // 2
-    block = wide // 2
-    for out_ref, f in ((kept_ref, y), (give_ref, 1 - y)):
-        values = one_ref[:, pl.ds(pl.multiple_of(f * wide, 128), wide)]
-        on = first_ref[my_row, my_col * 2 + f]
-        keep = below(size1_ref[my_col * 2 + f], values.shape, 1) * on.astype(F32)
-        out_ref[:wide] = (values * keep).T
-        for i in range(2):
-            child = pick([order[i], order[2 + i]], f)
-            values = two_ref[:, pl.ds(pl.multiple_of(child * block, 128), block)]
-            both = (on * second_ref[my_row, my_col * 4 + child]).astype(F32)
-            keep = below(size2_ref[my_col * 4 + child], values.shape, 1) * both
-            out_ref[wide + i * block : wide + (i + 1) * block] = (values * keep).T
 
 
 def join(kept_ref, near_ref, far_ref, *outs):
@@ -158,19 +137,19 @@
 def combine(depth, s, up_ref, down_ref, part_up_ref, part_down_ref, go_up_ref, go_down_ref):
     z = lax.axis_index("prow") // 2
 
-    @pl.when(z <= s - 2 - LAG)
+    @pl.when(z <= s - 2)
     def _():
         go_up_ref[...] = up_ref[...] + part_up_ref[...]
 
-    @pl.when(z > s - 2 - LAG)
+    @pl.when(z > s - 2)
     def _():
         go_up_ref[...] = up_ref[...]
 
-    @pl.when(depth - 1 - z <= s - 2 - LAG)
+    @pl.when(depth - 1 - z <= s - 2)
     def _():
         go_down_ref[...] = down_ref[...] + part_down_ref[...]
 
-    @pl.when(depth - 1 - z > s - 2 - LAG)
+    @pl.when(depth - 1 - z > s - 2)
     def _():
         go_down_ref[...] = down_ref[...]
 
@@ -401,6 +380,7 @@
         z = lax.axis_index("prow") // 2
         block = array(b1, rows)
         scalars = [pattern_one, pattern_two, parent_two, size_one, size_two]
+
         def tie(*values):
             return lax.optimization_barrier(values)
 
@@ -408,65 +388,28 @@
         beside = send(anc_inverse, other_y)
         turns = [pairs(lambda z, y, x, k: (z, y, (x + s) % wide, k)) for s in range(1, wide)]
         tops = [send(anc_inverse, turn) for turn in turns]
-        if OPT["merge"]:
-            kept, give = call(
-                pack, [array(2 * b1, rows)] * 2, [factor_one, factor_two] + scalars, scalars=5, name="pack"
-            )
-            near, far = send(give, to_worker), send(kept, across)
-            if OPT["wtie"]:
-                near, far, beside = tie(near, far, beside)
-            w1, w2 = call(join, [array(b1, span)] * 2, [kept, near, far], name="join")
-            give1 = give
-        else:
-            kept1, give1 = call(pack_one, [block] * 2, [factor_one, pattern_one, size_one], scalars=2, name="pack_one")
-            near1, far1 = send(give1, to_worker), send(kept1, across)
-            if OPT["w2"] == 1:
-                factor_two, _ = tie(factor_two, give1)
-            if OPT["w2"] == 2:
-                factor_two, near1, far1 = tie(factor_two, near1, far1)
-            if OPT["w2"] == 3:
-                factor_two, near1, far1, beside = tie(factor_two, near1, far1, beside)
-            kept2, give2 = call(
-                pack_two,
-                [block] * 2,
-                [factor_two, pattern_one, pattern_two, parent_two, size_two],
-                scalars=4,
-                name="pack_two",
-            )
-            if OPT["wtie"] == 1:
-                near1, far1, kept2, give2 = tie(near1, far1, kept2, give2)
-            if OPT["wtie"] == 2:
-                near1, far1, beside = tie(near1, far1, beside)
-            (w1,) = call(join, [array(b1, span)], [kept1, near1, far1], name="join_one")
-            if OPT["wtie"] == 3:
-                w1, kept2, give2 = tie(w1, kept2, give2)
-            near2, far2 = send(give2, to_worker), send(kept2, across)
-            if OPT["wtie"] == 4:
-                near1, far1, near2, far2 = tie(near1, far1, near2, far2)
-            (w2,) = call(join, [array(b1, span)], [kept2, near2, far2], name="join_two")
-        passed = beside
-        if OPT["relay"] == 1:
-            passed, _ = tie(beside, give1)
-        if OPT["relay"] == 2:
-            passed, w1 = tie(beside, w1)
-        if OPT["relay"] == 3:
-            passed, _ = tie(beside, w1)
-        if OPT["relay"] == 4:
-            passed, w1, *tops = tie(beside, w1, *tops)
+        beside, *tops = tie(beside, *tops)
+        kept1, give1 = call(pack_one, [block] * 2, [factor_one, pattern_one, size_one], scalars=2, name="pack_one")
+        near1, far1 = send(give1, to_worker), send(kept1, across)
+        factor_two, near1, far1 = tie(factor_two, near1, far1)
+        kept2, give2 = call(
+            pack_two,
+            [block] * 2,
+            [factor_two, pattern_one, pattern_two, parent_two, size_two],
+            scalars=4,
+            name="pack_two",
+        )
+        near1, far1, kept2, give2 = tie(near1, far1, kept2, give2)
+        (w1,) = call(join, [array(b1, span)], [kept1, near1, far1], name="join_one")
+        near2, far2 = send(give2, to_worker), send(kept2, across)
+        (w2,) = call(join, [array(b1, span)], [kept2, near2, far2], name="join_two")
+        passed, _ = tie(beside, w1)
         middle = rows // 2
         tiles = [[anc_inverse, beside]]
         for turn, top in zip(turns, tops):
-            if OPT["half"]:
-                tiles.append([top, send(passed[:middle], turn), send(top[middle:], other_y)])
-            else:
-                tiles.append([top, send(passed, turn)])
+            tiles.append([top, send(passed[:middle], turn), send(top[middle:], other_y)])
         from_below, from_above = [send(w1, up)], [send(w1, down)]
-        if OPT["one"] == 1:
-            w2, from_below, from_above = tie(w2, from_below, from_above)
-        if OPT["one"] == 2:
-            tiles[1:], from_below, from_above = tie(tiles[1:], from_below, from_above)
-        if OPT["one"] == 3:
-            tiles[1][1], from_below, from_above = tie(tiles[1][1], from_below, from_above)
+        w2, from_below, from_above = tie(w2, from_below, from_above)
         panel = []
         for mine in tiles:
             panel += mine + [send(v, other_core) for v in mine]
@@ -480,15 +423,15 @@
 
         def combined(s, c, from_below, from_above):
             whole = pl.BlockSpec(piece.shape, lambda i, at: (0, 0))
-            taken = pl.BlockSpec(piece.shape, lambda i, at: (c if s == 2 + LAG else 0, 0))
+            taken = pl.BlockSpec(piece.shape, lambda i, at: (c if s == 2 else 0, 0))
             spec = pltpu.PrefetchScalarGridSpec(
                 num_scalar_prefetch=1,
                 grid=(1,),
                 in_specs=[
                     taken,
                     taken,
-                    pl.BlockSpec(piece.shape, lambda i, at: (c, jnp.clip(at[0] + 1 + depth + LAG - s, 0, depth - 1))),
-                    pl.BlockSpec(piece.shape, lambda i, at: (c, jnp.clip(at[0] - 1 - depth - LAG + s, 0, depth - 1))),
+                    pl.BlockSpec(piece.shape, lambda i, at: (c, jnp.clip(at[0] + 1 + depth - s, 0, depth - 1))),
+                    pl.BlockSpec(piece.shape, lambda i, at: (c, jnp.clip(at[0] - 1 - depth + s, 0, depth - 1))),
                 ],
                 out_specs=[whole, whole],
             )
@@ -506,17 +449,10 @@
             )(z[None], from_below, from_above, parts, parts)
 
         half = b1 // 2
-        for s in range(1, depth + LAG):
+        for s in range(1, depth):
             taken, chunks = from_below + from_above, len(from_below)
-            blocks = range(1 if s <= LAG else CHUNKS)
-            if s <= LAG:
-                go = [(from_below[0], from_above[0])]
-            else:
-                go = [combined(s + 1, c, from_below[c % chunks], from_above[c % chunks]) for c in blocks]
-            if s == depth - 1 and OPT["gram"] == 1:
-                y1, go = tie(y1, go)
-            if s == depth - 1 and OPT["gram"] == 2:
-                y1, go[0] = tie(y1, go[0])
+            blocks = range(CHUNKS)
+            go = [combined(s + 1, c, from_below[c % chunks], from_above[c % chunks]) for c in blocks]
             from_below = [send(go[c][0], up) for c in blocks]
             from_above = [send(go[c][1], down) for c in blocks]
             if s == 1:
@@ -529,8 +465,6 @@
                     name="next_product",
                     room=20,
                 )
-                if OPT["early"]:
-                    y1, go = tie(y1, go)
             if s == depth - 1:
                 y1, mine, theirs = call(
                     functools.partial(gram_products, depth, s, chunks),
@@ -548,8 +482,7 @@
             return [same, send(give, to_home), send(other, across)]
 
         grams = mine + swap(theirs, 1)
-        if OPT["ztwo"]:
-            grams, from_below[0], from_above[0] = tie(grams, from_below[0], from_above[0])
+        grams, from_below[0], from_above[0] = tie(grams, from_below[0], from_above[0])
         step = 2
         while 2 * step < depth:
             grams = grams + swap(grams, step)
@@ -581,21 +514,14 @@
 
         same, other, give, energy = last_part()
         home = deliver(same, give, other)
-        if OPT["zone"] == 2:
-            arrived, energy = tie(arrived, energy)
         step = 1
         while 2 * step < depth:
             energy = energy + swap(energy, step)
             step *= 2
-        if OPT["zone"] == 1:
-            arrived, energy = tie(arrived, energy)
+        arrived, energy = tie(arrived, energy)
         grams = grams + arrived
         grams_too = swap(grams, 1)
         energies = [energy, swap(energy, step)]
-        if OPT["home"] == 1:
-            grams_too, home = tie(grams_too, home)
-        if OPT["home"] == 2:
-            grams, home = tie(grams, home)
         (sums,) = call(
             functools.partial(collect, depth), [array(half + 8, 7 * half)], [grams, grams_too] + energies, name="collect"
         )

time: 138 us -> 134 us (0.971)
  waiting for transfers between devices: 49.9 us -> 40.4 us
  local copies, waits for them, and re-layouts: 5.5 us -> 9.54 us
    ppermute x34 -> x36, waiting for transfers between devices: 49.9 us -> 40.4 us  [send(): return lax.ppermute(value, AXES, perm)]
    unnamed x30 -> x42, local copies, waits for them, and re-layouts: 5.46 us -> 9.51 us
    pallas_call x10 -> x12, Pallas kernels: 13.7 us -> 14.4 us  [call(): pl.pallas_call(body, out_shape=outs, in_specs=specs, out_specs=[VMEM] * l...]
    ppermute x34 -> x36, starting transfers between devices: 66.1 us -> 66 us  [send(): return lax.ppermute(value, AXES, perm)]
  transfers between devices with their start and end apart: 34 -> 36, of which waited for: 15 -> 14; matrix products, arithmetic and copies ran while one was open for 0% -> 0% of each run, Pallas kernels for 6% -> 6%
where the time goes in v4:
time: 134 us; the launch traced here: 133 us
  starting transfers between devices  66 us (49%)
  waiting for transfers between devices  40.4 us (30%)
  Pallas kernels  15.6 us (12%)
  local copies, waits for them, and re-layouts  9.54 us (7%)
    ppermute x36, starting transfers between devices, send(): return lax.ppermute(value, AXES, perm)  66 us
    ppermute x36, waiting for transfers between devices, send(): return lax.ppermute(value, AXES, perm)  40.4 us
    pallas_call x12, Pallas kernels, call(): pl.pallas_call(body, out_shape=outs, in_specs=specs, out_specs=[VMEM] * l...  14.4 us
    unnamed x42, local copies, waits for them, and re-layouts  9.51 us
  transfers between devices with their start and end apart: 36, of which 14 were waited for; matrix products, arithmetic and copies ran while one was open for 0% of the time, Pallas kernels for 6%

profile of v4, /device:TPU:1, one launch (start us, length us, event | category | flops | bytes accessed | tf_op | source)
XLA Modules:
  0.0 132.8 jit_solution(15252143829549085436)
XLA Ops:
  0.7 1.1 copy-done.2
  3.1 0.8 pack_one.1
  3.9 2.1 %collective-permute-start = (f32[256,256]{1,0:T(8,128)S(1)}, f32[256,256]{1,0:T(8,128)S(1)}, u32[]{:S(2)}, u32[]{:S(2)}) collective-permute-start(f32[256,256]{1,0:T(8,128)S(1)} %get-tuple-element.54), channel_id=1, source_target_pairs={{0,1},{1,5},{2,3},{3,7},{4,0},{5,4},{6,2},{7,6},{8,9},{9,13},{10,1... | collective-permute-start | bytes 786440 | tf_op jit(solution)/shard_map/ppermute | solution.py:361
  6.0 2.5 %collective-permute-start.1 = (f32[256,256]{1,0:T(8,128)S(1)}, f32[256,256]{1,0:T(8,128)S(1)}, u32[]{:S(2)}, u32[]{:S(2)}) collective-permute-start(f32[256,256]{1,0:T(8,128)S(1)} %get-tuple-element.55.kept_ref), channel_id=1, source_target_pairs={{1,4},{3,6},{4,1},{6,3},{9,12},{11,14},{12,9},{14,11},{17,20},{19,... | collective-permute-start | bytes 786440 | tf_op jit(solution)/shard_map/ppermute | solution.py:361
  8.5 1.8 %collective-permute-start.7 = (f32[256,512]{1,0:T(8,128)}, f32[256,512]{1,0:T(8,128)S(1)}, u32[]{:S(2)}, u32[]{:S(2)}) collective-permute-start(f32[256,512]{1,0:T(8,128)} %refs_0_.1), channel_id=1, source_target_pairs={{0,2},{1,3},{2,0},{3,1},{4,6},{5,7},{6,4},{7,5},{8,10},{9,11},{10,... | collective-permute-start | bytes 1572872 | tf_op jit(solution)/shard_map/ppermute | solution.py:361
  10.2 4.5 %collective-permute-done.1.far_ref = f32[256,256]{1,0:T(8,128)S(1)} collective-permute-done((f32[256,256]{1,0:T(8,128)S(1)}, f32[256,256]{1,0:T(8,128)S(1)}, u32[]{:S(2)}, u32[]{:S(2)}) %collective-permute-start.1) | collective-permute-done | bytes 262176 | tf_op jit(solution)/shard_map/ppermute | solution.py:361
  14.7 1.0 copy-done.3
  18.4 0.9 pack_two.1
  19.4 1.3 collective-permute-start.5
  20.7 4.4 %collective-permute-start.4 = (f32[256,512]{1,0:T(8,128)S(1)}, f32[256,512]{1,0:T(8,128)S(1)}, u32[]{:S(2)}, u32[]{:S(2)}) collective-permute-start(f32[256,512]{1,0:T(8,128)S(1)} %join_one.1.refs_0_.refs_4_), channel_id=1, source_target_pairs={{0,8},{1,9},{2,10},{3,11},{4,12},{5,13},{6,14},{7,15},{8,16},{9,17... | collective-permute-start | bytes 1572872 | tf_op jit(solution)/shard_map/ppermute | solution.py:361
  25.1 2.0 %collective-permute-start.3 = (f32[256,256]{1,0:T(8,128)S(1)}, f32[256,256]{1,0:T(8,128)S(1)}, u32[]{:S(2)}, u32[]{:S(2)}) collective-permute-start(f32[256,256]{1,0:T(8,128)S(1)} %get-tuple-element.61.kept_ref), channel_id=1, source_target_pairs={{1,4},{3,6},{4,1},{6,3},{9,12},{11,14},{12,9},{14,11},{17,20},{19,... | collective-permute-start | bytes 786440 | tf_op jit(solution)/shard_map/ppermute | solution.py:361
  27.3 1.1 collective-permute-done.2.near_ref
  29.1 2.2 %collective-permute-start.11 = (f32[128,512]{1,0:T(8,128)S(1)}, f32[128,512]{1,0:T(8,128)}, u32[]{:S(2)}, u32[]{:S(2)}) collective-permute-start(f32[128,512]{1,0:T(8,128)S(1)} %slice.7), channel_id=1, source_target_pairs={{0,4},{1,5},{2,6},{3,7},{4,0},{5,1},{6,2},{7,3},{8,12},{9,13},{10,... | collective-permute-start | bytes 786440 | tf_op jit(solution)/shard_map/ppermute | solution.py:361
  31.3 2.0 %collective-permute-done.3.far_ref = f32[256,256]{1,0:T(8,128)S(1)} collective-permute-done((f32[256,256]{1,0:T(8,128)S(1)}, f32[256,256]{1,0:T(8,128)S(1)}, u32[]{:S(2)}, u32[]{:S(2)}) %collective-permute-start.3) | collective-permute-done | bytes 262176 | tf_op jit(solution)/shard_map/ppermute | solution.py:361
  33.3 0.7 copy-done.7
  34.0 2.6 %collective-permute-start.10 = (f32[128,512]{1,0:T(8,128)S(1)}, f32[128,512]{1,0:T(8,128)}, u32[]{:S(2)}, u32[]{:S(2)}) collective-permute-start(f32[128,512]{1,0:T(8,128)S(1)} %slice.6), channel_id=1, source_target_pairs={{0,2},{1,3},{2,0},{3,1},{4,6},{5,7},{6,4},{7,5},{8,10},{9,11},{10,... | collective-permute-start | bytes 786440 | tf_op jit(solution)/shard_map/ppermute | solution.py:361
  37.2 0.9 collective-permute-done.11.refs_6_
  38.1 1.2 collective-permute-start.14
  39.2 1.5 %collective-permute-done.10.refs_5_ = f32[128,512]{1,0:T(8,128)} collective-permute-done((f32[128,512]{1,0:T(8,128)S(1)}, f32[128,512]{1,0:T(8,128)}, u32[]{:S(2)}, u32[]{:S(2)}) %collective-permute-start.10) | collective-permute-done | bytes 262176 | tf_op jit(solution)/shard_map/ppermute | solution.py:361
  40.7 0.9 copy-done.6
  41.7 0.9 copy-done.8
  42.7 4.1 %partial_products.1 = (f32[256,2048]{1,0:T(8,128)S(1)}, bf16[512,2048]{1,0:T(8,128)(2,1)S(1)}, bf16[512,2048]{1,0:T(8,128)(2,1)S(1)}) custom-call(f32[256,512]{1,0:T(8,128)S(1)} %join_two.1.w2_ref.refs_5_, f32[256,512]{1,0:T(8,128)S(1)} %copy-done.1, f32[256,512]{1,0:T(8,128)S(1)} %collective-permute-done.6.refs_1_, ...), custom_call_target="tpu_custom_call" | custom-call | tf_op jit(solution)/shard_map/partial_products/pallas_call | solution.py:320
  46.9 3.0 %collective-permute-start.15 = (f32[128,512]{1,0:T(8,128)S(1)}, f32[128,512]{1,0:T(8,128)S(1)}, u32[]{:S(2)}, u32[]{:S(2)}) collective-permute-start(f32[128,512]{1,0:T(8,128)S(1)} %get-tuple-element.74), channel_id=1, source_target_pairs={{0,8},{1,9},{2,10},{3,11},{4,12},{5,13},{6,14},{7,15},{8,16},{9,17... | collective-permute-start | bytes 786440 | tf_op jit(solution)/shard_map/ppermute | solution.py:361
  49.9 1.3 collective-permute-start.17
  51.3 4.0 %collective-permute-start.16 = (f32[128,512]{1,0:T(8,128)S(1)}, f32[128,512]{1,0:T(8,128)S(1)}, u32[]{:S(2)}, u32[]{:S(2)}) collective-permute-start(f32[128,512]{1,0:T(8,128)S(1)} %get-tuple-element.75), channel_id=1, source_target_pairs={{0,8},{1,9},{2,10},{3,11},{4,12},{5,13},{6,14},{7,15},{8,16},{9,17... | collective-permute-start | bytes 786440 | tf_op jit(solution)/shard_map/ppermute | solution.py:361
  55.3 1.3 collective-permute-start.18
  56.6 2.2 %collective-permute-done.17.refs_2_.refs_1_ = f32[128,512]{1,0:T(8,128)S(1)} collective-permute-done((f32[128,512]{1,0:T(8,128)S(1)}, f32[128,512]{1,0:T(8,128)S(1)}, u32[]{:S(2)}, u32[]{:S(2)}) %collective-permute-start.17) | collective-permute-done | bytes 262176 | tf_op jit(solution)/shard_map/ppermute | solution.py:361
  58.9 3.2 %collective-permute-start.19 = (f32[128,512]{1,0:T(8,128)S(1)}, f32[128,512]{1,0:T(8,128)S(1)}, u32[]{:S(2)}, u32[]{:S(2)}) collective-permute-start(f32[128,512]{1,0:T(8,128)S(1)} %get-tuple-element.78), channel_id=1, source_target_pairs={{0,8},{1,9},{2,10},{3,11},{4,12},{5,13},{6,14},{7,15},{8,16},{9,17... | collective-permute-start | bytes 786440 | tf_op jit(solution)/shard_map/ppermute | solution.py:361
  62.2 1.3 collective-permute-start.21
  64.2 3.4 %collective-permute-start.20 = (f32[128,512]{1,0:T(8,128)S(1)}, f32[128,512]{1,0:T(8,128)S(1)}, u32[]{:S(2)}, u32[]{:S(2)}) collective-permute-start(f32[128,512]{1,0:T(8,128)S(1)} %get-tuple-element.79), channel_id=1, source_target_pairs={{0,8},{1,9},{2,10},{3,11},{4,12},{5,13},{6,14},{7,15},{8,16},{9,17... | collective-permute-start | bytes 786440 | tf_op jit(solution)/shard_map/ppermute | solution.py:361
  67.6 1.3 collective-permute-start.22
  68.9 0.8 collective-permute-done.21.refs_2_.refs_1_
  69.8 3.2 %collective-permute-start.24 = (f32[128,512]{1,0:T(8,128)S(1)}, f32[128,512]{1,0:T(8,128)S(1)}, u32[]{:S(2)}, u32[]{:S(2)}) collective-permute-start(f32[128,512]{1,0:T(8,128)S(1)} %get-tuple-element.84), channel_id=1, source_target_pairs={{0,8},{1,9},{2,10},{3,11},{4,12},{5,13},{6,14},{7,15},{8,16},{9,17... | collective-permute-start | bytes 786440 | tf_op jit(solution)/shard_map/ppermute | solution.py:361
  73.0 1.3 collective-permute-start.25
  76.4 1.4 %gram_products.1 = (f32[256,512]{1,0:T(8,128)S(1)}, f32[136,384]{1,0:T(8,128)S(1)}, f32[136,384]{1,0:T(8,128)S(1)}) custom-call(bf16[512,2048]{1,0:T(8,128)(2,1)S(1)} %get-tuple-element.70.high_ref, bf16[512,2048]{1,0:T(8,128)(2,1)S(1)} %get-tuple-element.71.low_ref, f32[256,512]{1,0:T(8,128)S(1)} %next_product.3.before_ref, ...), custom_call_target="tpu_custom_call" | custom-call | tf_op jit(solution)/shard_map/gram_products/pallas_call | solution.py:320
  77.7 2.1 %collective-permute-start.23 = (f32[136,384]{1,0:T(8,128)S(1)}, f32[136,384]{1,0:T(8,128)S(1)}, u32[]{:S(2)}, u32[]{:S(2)}) collective-permute-start(f32[136,384]{1,0:T(8,128)S(1)} %get-tuple-element.83), channel_id=1, source_target_pairs={{0,8},{1,9},{2,10},{3,11},{4,12},{5,13},{6,14},{7,15},{8,0},{9,1},... | collective-permute-start | bytes 626696 | tf_op jit(solution)/shard_map/ppermute | solution.py:361
  80.0 2.0 %collective-permute-start.26 = (f32[128,512]{1,0:T(8,128)S(1)}, f32[128,512]{1,0:T(8,128)S(1)}, u32[]{:S(2)}, u32[]{:S(2)}) collective-permute-start(f32[128,512]{1,0:T(8,128)S(1)} %get-tuple-element.87), channel_id=1, source_target_pairs={{0,8},{1,9},{2,10},{3,11},{4,12},{5,13},{6,14},{7,15},{8,16},{9,17... | collective-permute-start | bytes 786440 | tf_op jit(solution)/shard_map/ppermute | solution.py:361
  81.9 1.3 collective-permute-start.27
  83.2 2.1 %collective-permute-done.23 = f32[136,384]{1,0:T(8,128)S(1)} collective-permute-done((f32[136,384]{1,0:T(8,128)S(1)}, f32[136,384]{1,0:T(8,128)S(1)}, u32[]{:S(2)}, u32[]{:S(2)}) %collective-permute-start.23) | collective-permute-done | bytes 208928 | tf_op jit(solution)/shard_map/ppermute | solution.py:361
  86.4 7.8 %collective-permute-done.27.refs_4_ = f32[128,512]{1,0:T(8,128)S(1)} collective-permute-done((f32[128,512]{1,0:T(8,128)S(1)}, f32[128,512]{1,0:T(8,128)S(1)}, u32[]{:S(2)}, u32[]{:S(2)}) %collective-permute-start.27) | collective-permute-done | bytes 262176 | tf_op jit(solution)/shard_map/ppermute | solution.py:361
  94.9 3.4 %collective-permute-done.31 = f32[136,128]{1,0:T(8,128)S(1)} collective-permute-done((f32[136,128]{1,0:T(8,128)S(1)}, f32[136,128]{1,0:T(8,128)S(1)}, u32[]{:S(2)}, u32[]{:S(2)}) %collective-permute-start.31) | collective-permute-done | bytes 69664 | tf_op jit(solution)/shard_map/ppermute | solution.py:361
  98.5 5.4 %collective-permute-start.28 = (f32[512,256]{1,0:T(8,128)S(1)}, f32[512,256]{1,0:T(8,128)S(1)}, u32[]{:S(2)}, u32[]{:S(2)}) collective-permute-start(f32[512,256]{1,0:T(8,128)S(1)} %get-tuple-element.92), channel_id=1, source_target_pairs={{0,4},{1,0},{2,6},{3,2},{4,5},{5,1},{6,7},{7,3},{8,12},{9,8},{10,1... | collective-permute-start | bytes 1572872 | tf_op jit(solution)/shard_map/ppermute | solution.py:361
  104.0 5.0 %collective-permute-start.29 = (f32[512,256]{1,0:T(8,128)S(1)}, f32[512,256]{1,0:T(8,128)S(1)}, u32[]{:S(2)}, u32[]{:S(2)}) collective-permute-start(f32[512,256]{1,0:T(8,128)S(1)} %get-tuple-element.93), channel_id=1, source_target_pairs={{1,4},{3,6},{4,1},{6,3},{9,12},{11,14},{12,9},{14,11},{17,20},{19,... | collective-permute-start | bytes 1572872 | tf_op jit(solution)/shard_map/ppermute | solution.py:361
  109.0 5.7 %collective-permute-start.35 = (f32[136,896]{1,0:T(8,128)S(1)}, f32[136,896]{1,0:T(8,128)S(1)}, u32[]{:S(2)}, u32[]{:S(2)}) collective-permute-start(f32[136,896]{1,0:T(8,128)S(1)} %collect.1.own), channel_id=1, source_target_pairs={{1,4},{3,6},{4,1},{6,3},{9,12},{11,14},{12,9},{14,11},{17,20},{19,... | collective-permute-start | bytes 1462280 | tf_op jit(solution)/shard_map/ppermute | solution.py:361
  114.8 5.9 %collective-permute-done.29.far = f32[512,256]{1,0:T(8,128)S(1)} collective-permute-done((f32[512,256]{1,0:T(8,128)S(1)}, f32[512,256]{1,0:T(8,128)S(1)}, u32[]{:S(2)}, u32[]{:S(2)}) %collective-permute-start.29) | collective-permute-done | bytes 524320 | tf_op jit(solution)/shard_map/ppermute | solution.py:361
  120.7 2.2 %finish_rows.1 = (f32[256,512]{1,0:T(8,128)}, f32[256,512]{1,0:T(8,128)}) custom-call(f32[512,256]{1,0:T(8,128)S(1)} %get-tuple-element.91.own, f32[512,256]{1,0:T(8,128)S(1)} %collective-permute-done.28.near, f32[512,256]{1,0:T(8,128)S(1)} %collective-permute-done.29.far, f32[4,256,128]{2,1,0:T(8,128)S(1)} %copy-done, s32[8,8]{1,0:T(8,128)S(1)} %copy-done.12, ...), custom_call_target="tpu_custom_call" | custom-call | tf_op jit(solution)/shard_map/finish_rows/pallas_call | solution.py:320
  122.9 6.9 %collective-permute-done.35.far = f32[136,896]{1,0:T(8,128)S(1)} collective-permute-done((f32[136,896]{1,0:T(8,128)S(1)}, f32[136,896]{1,0:T(8,128)S(1)}, u32[]{:S(2)}, u32[]{:S(2)}) %collective-permute-start.35) | collective-permute-done | bytes 487456 | tf_op jit(solution)/shard_map/ppermute | solution.py:361
  129.8 3.0 %finish_blocks.1 = (f32[2,256,256]{2,1,0:T(8,128)}, f32[4,256,128]{2,1,0:T(8,128)}, f32[4,128,128]{2,1,0:T(8,128)}) custom-call(f32[136,896]{1,0:T(8,128)S(1)} %collect.1.own, f32[136,896]{1,0:T(8,128)S(1)} %collective-permute-done.34.near, f32[136,896]{1,0:T(8,128)S(1)} %collective-permute-done.35.far, f32[2,256,256]{2,1,0:T(8,128)S(1)} %copy-done.4, ...), custom_call_target="tpu_custom_call" | custom-call | tf_op jit(solution)/shard_map/finish_blocks/pallas_call | solution.py:320
  (90 shorter events, 10.6 us)
Async XLA Ops:
  0.6 26.5 %copy-start.1 = (f32[256,512]{1,0:T(8,128)S(1)}, f32[256,512]{1,0:T(8,128)}, u32[]{:S(2)}) copy-start(f32[256,512]{1,0:T(8,128)} %refs_0_.1) | copy-start | bytes 1572868
  0.6 1.1 copy-start.2
  3.9 6.3 %collective-permute-start = (f32[256,256]{1,0:T(8,128)S(1)}, f32[256,256]{1,0:T(8,128)S(1)}, u32[]{:S(2)}, u32[]{:S(2)}) collective-permute-start(f32[256,256]{1,0:T(8,128)S(1)} %get-tuple-element.54), channel_id=1, source_target_pairs={{0,1},{1,5},{2,3},{3,7},{4,0},{5,4},{6,2},{7,6},{8,9},{9,13},{10,1... | collective-permute-start | bytes 786440 | tf_op jit(solution)/shard_map/ppermute | solution.py:361
  6.0 8.7 %collective-permute-start.1 = (f32[256,256]{1,0:T(8,128)S(1)}, f32[256,256]{1,0:T(8,128)S(1)}, u32[]{:S(2)}, u32[]{:S(2)}) collective-permute-start(f32[256,256]{1,0:T(8,128)S(1)} %get-tuple-element.55.kept_ref), channel_id=1, source_target_pairs={{1,4},{3,6},{4,1},{6,3},{9,12},{11,14},{12,9},{14,11},{17,20},{19,... | collective-permute-start | bytes 786440 | tf_op jit(solution)/shard_map/ppermute | solution.py:361
  8.5 16.6 %collective-permute-start.7 = (f32[256,512]{1,0:T(8,128)}, f32[256,512]{1,0:T(8,128)S(1)}, u32[]{:S(2)}, u32[]{:S(2)}) collective-permute-start(f32[256,512]{1,0:T(8,128)} %refs_0_.1), channel_id=1, source_target_pairs={{0,2},{1,3},{2,0},{3,1},{4,6},{5,7},{6,4},{7,5},{8,10},{9,11},{10,... | collective-permute-start | bytes 1572872 | tf_op jit(solution)/shard_map/ppermute | solution.py:361
  10.2 16.9 %collective-permute-start.6 = (f32[256,512]{1,0:T(8,128)}, f32[256,512]{1,0:T(8,128)S(1)}, u32[]{:S(2)}, u32[]{:S(2)}) collective-permute-start(f32[256,512]{1,0:T(8,128)} %refs_0_.1), channel_id=1, source_target_pairs={{0,4},{1,5},{2,6},{3,7},{4,0},{5,1},{6,2},{7,3},{8,12},{9,13},{10,... | collective-permute-start | bytes 1572872 | tf_op jit(solution)/shard_map/ppermute | solution.py:361
  14.7 1.0 copy-start.3
  19.4 17.2 %collective-permute-start.5 = (f32[256,512]{1,0:T(8,128)S(1)}, f32[256,512]{1,0:T(8,128)S(1)}, u32[]{:S(2)}, u32[]{:S(2)}) collective-permute-start(f32[256,512]{1,0:T(8,128)S(1)} %join_one.1.refs_0_.refs_4_), channel_id=1, source_target_pairs={{8,0},{9,1},{10,2},{11,3},{12,4},{13,5},{14,6},{15,7},{16,8},{17,9... | collective-permute-start | bytes 1572872 | tf_op jit(solution)/shard_map/ppermute | solution.py:361
  20.7 15.9 %collective-permute-start.4 = (f32[256,512]{1,0:T(8,128)S(1)}, f32[256,512]{1,0:T(8,128)S(1)}, u32[]{:S(2)}, u32[]{:S(2)}) collective-permute-start(f32[256,512]{1,0:T(8,128)S(1)} %join_one.1.refs_0_.refs_4_), channel_id=1, source_target_pairs={{0,8},{1,9},{2,10},{3,11},{4,12},{5,13},{6,14},{7,15},{8,16},{9,17... | collective-permute-start | bytes 1572872 | tf_op jit(solution)/shard_map/ppermute | solution.py:361
  25.1 3.3 %collective-permute-start.2 = (f32[256,256]{1,0:T(8,128)S(1)}, f32[256,256]{1,0:T(8,128)S(1)}, u32[]{:S(2)}, u32[]{:S(2)}) collective-permute-start(f32[256,256]{1,0:T(8,128)S(1)} %get-tuple-element.62), channel_id=1, source_target_pairs={{0,1},{1,5},{2,3},{3,7},{4,0},{5,4},{6,2},{7,6},{8,9},{9,13},{10,1... | collective-permute-start | bytes 786440 | tf_op jit(solution)/shard_map/ppermute | solution.py:361
  25.1 8.2 %collective-permute-start.3 = (f32[256,256]{1,0:T(8,128)S(1)}, f32[256,256]{1,0:T(8,128)S(1)}, u32[]{:S(2)}, u32[]{:S(2)}) collective-permute-start(f32[256,256]{1,0:T(8,128)S(1)} %get-tuple-element.61.kept_ref), channel_id=1, source_target_pairs={{1,4},{3,6},{4,1},{6,3},{9,12},{11,14},{12,9},{14,11},{17,20},{19,... | collective-permute-start | bytes 786440 | tf_op jit(solution)/shard_map/ppermute | solution.py:361
  27.2 15.5 %collective-permute-start.8 = (f32[256,512]{1,0:T(8,128)S(1)}, f32[256,512]{1,0:T(8,128)}, u32[]{:S(2)}, u32[]{:S(2)}) collective-permute-start(f32[256,512]{1,0:T(8,128)S(1)} %copy-done.1), channel_id=1, source_target_pairs={{0,1},{1,0},{2,3},{3,2},{4,5},{5,4},{6,7},{7,6},{8,9},{9,8},{10,11... | collective-permute-start | bytes 1572872 | tf_op jit(solution)/shard_map/ppermute | solution.py:361
  29.1 8.9 %collective-permute-start.11 = (f32[128,512]{1,0:T(8,128)S(1)}, f32[128,512]{1,0:T(8,128)}, u32[]{:S(2)}, u32[]{:S(2)}) collective-permute-start(f32[128,512]{1,0:T(8,128)S(1)} %slice.7), channel_id=1, source_target_pairs={{0,4},{1,5},{2,6},{3,7},{4,0},{5,1},{6,2},{7,3},{8,12},{9,13},{10,... | collective-permute-start | bytes 786440 | tf_op jit(solution)/shard_map/ppermute | solution.py:361
  34.0 6.7 %collective-permute-start.10 = (f32[128,512]{1,0:T(8,128)S(1)}, f32[128,512]{1,0:T(8,128)}, u32[]{:S(2)}, u32[]{:S(2)}) collective-permute-start(f32[128,512]{1,0:T(8,128)S(1)} %slice.6), channel_id=1, source_target_pairs={{0,2},{1,3},{2,0},{3,1},{4,6},{5,7},{6,4},{7,5},{8,10},{9,11},{10,... | collective-permute-start | bytes 786440 | tf_op jit(solution)/shard_map/ppermute | solution.py:361
  36.6 6.1 %collective-permute-start.9 = (f32[256,512]{1,0:T(8,128)S(1)}, f32[256,512]{1,0:T(8,128)}, u32[]{:S(2)}, u32[]{:S(2)}) collective-permute-start(f32[256,512]{1,0:T(8,128)S(1)} %collective-permute-done.6.refs_1_), channel_id=1, source_target_pairs={{0,1},{1,0},{2,3},{3,2},{4,5},{5,4},{6,7},{7,6},{8,9},{9,8},{10,11... | collective-permute-start | bytes 1572872 | tf_op jit(solution)/shard_map/ppermute | solution.py:361
  36.7 6.1 %collective-permute-start.12 = (f32[256,512]{1,0:T(8,128)S(1)}, f32[256,512]{1,0:T(8,128)}, u32[]{:S(2)}, u32[]{:S(2)}) collective-permute-start(f32[256,512]{1,0:T(8,128)S(1)} %collective-permute-done.7.refs_4_), channel_id=1, source_target_pairs={{0,1},{1,0},{2,3},{3,2},{4,5},{5,4},{6,7},{7,6},{8,9},{9,8},{10,11... | collective-permute-start | bytes 1572872 | tf_op jit(solution)/shard_map/ppermute | solution.py:361
  38.1 4.6 %collective-permute-start.14 = (f32[128,512]{1,0:T(8,128)}, f32[128,512]{1,0:T(8,128)}, u32[]{:S(2)}, u32[]{:S(2)}) collective-permute-start(f32[128,512]{1,0:T(8,128)} %collective-permute-done.11.refs_6_), channel_id=1, source_target_pairs={{0,1},{1,0},{2,3},{3,2},{4,5},{5,4},{6,7},{7,6},{8,9},{9,8},{10,11... | collective-permute-start | bytes 786440 | tf_op jit(solution)/shard_map/ppermute | solution.py:361
  40.7 2.0 %collective-permute-start.13 = (f32[128,512]{1,0:T(8,128)}, f32[128,512]{1,0:T(8,128)}, u32[]{:S(2)}, u32[]{:S(2)}) collective-permute-start(f32[128,512]{1,0:T(8,128)} %collective-permute-done.10.refs_5_), channel_id=1, source_target_pairs={{0,1},{1,0},{2,3},{3,2},{4,5},{5,4},{6,7},{7,6},{8,9},{9,8},{10,11... | collective-permute-start | bytes 786440 | tf_op jit(solution)/shard_map/ppermute | solution.py:361
  40.7 1.0 copy-start.6
  46.9 9.7 %collective-permute-start.15 = (f32[128,512]{1,0:T(8,128)S(1)}, f32[128,512]{1,0:T(8,128)S(1)}, u32[]{:S(2)}, u32[]{:S(2)}) collective-permute-start(f32[128,512]{1,0:T(8,128)S(1)} %get-tuple-element.74), channel_id=1, source_target_pairs={{0,8},{1,9},{2,10},{3,11},{4,12},{5,13},{6,14},{7,15},{8,16},{9,17... | collective-permute-start | bytes 786440 | tf_op jit(solution)/shard_map/ppermute | solution.py:361
  49.9 8.9 %collective-permute-start.17 = (f32[128,512]{1,0:T(8,128)S(1)}, f32[128,512]{1,0:T(8,128)S(1)}, u32[]{:S(2)}, u32[]{:S(2)}) collective-permute-start(f32[128,512]{1,0:T(8,128)S(1)} %get-tuple-element.76), channel_id=1, source_target_pairs={{8,0},{9,1},{10,2},{11,3},{12,4},{13,5},{14,6},{15,7},{16,8},{17,9... | collective-permute-start | bytes 786440 | tf_op jit(solution)/shard_map/ppermute | solution.py:361
  51.3 12.1 %collective-permute-start.16 = (f32[128,512]{1,0:T(8,128)S(1)}, f32[128,512]{1,0:T(8,128)S(1)}, u32[]{:S(2)}, u32[]{:S(2)}) collective-permute-start(f32[128,512]{1,0:T(8,128)S(1)} %get-tuple-element.75), channel_id=1, source_target_pairs={{0,8},{1,9},{2,10},{3,11},{4,12},{5,13},{6,14},{7,15},{8,16},{9,17... | collective-permute-start | bytes 786440 | tf_op jit(solution)/shard_map/ppermute | solution.py:361
  55.3 8.8 %collective-permute-start.18 = (f32[128,512]{1,0:T(8,128)S(1)}, f32[128,512]{1,0:T(8,128)S(1)}, u32[]{:S(2)}, u32[]{:S(2)}) collective-permute-start(f32[128,512]{1,0:T(8,128)S(1)} %get-tuple-element.77), channel_id=1, source_target_pairs={{8,0},{9,1},{10,2},{11,3},{12,4},{13,5},{14,6},{15,7},{16,8},{17,9... | collective-permute-start | bytes 786440 | tf_op jit(solution)/shard_map/ppermute | solution.py:361
  58.9 10.0 %collective-permute-start.19 = (f32[128,512]{1,0:T(8,128)S(1)}, f32[128,512]{1,0:T(8,128)S(1)}, u32[]{:S(2)}, u32[]{:S(2)}) collective-permute-start(f32[128,512]{1,0:T(8,128)S(1)} %get-tuple-element.78), channel_id=1, source_target_pairs={{0,8},{1,9},{2,10},{3,11},{4,12},{5,13},{6,14},{7,15},{8,16},{9,17... | collective-permute-start | bytes 786440 | tf_op jit(solution)/shard_map/ppermute | solution.py:361
  62.2 7.6 %collective-permute-start.21 = (f32[128,512]{1,0:T(8,128)S(1)}, f32[128,512]{1,0:T(8,128)S(1)}, u32[]{:S(2)}, u32[]{:S(2)}) collective-permute-start(f32[128,512]{1,0:T(8,128)S(1)} %get-tuple-element.80), channel_id=1, source_target_pairs={{8,0},{9,1},{10,2},{11,3},{12,4},{13,5},{14,6},{15,7},{16,8},{17,9... | collective-permute-start | bytes 786440 | tf_op jit(solution)/shard_map/ppermute | solution.py:361
  64.2 12.2 %collective-permute-start.20 = (f32[128,512]{1,0:T(8,128)S(1)}, f32[128,512]{1,0:T(8,128)S(1)}, u32[]{:S(2)}, u32[]{:S(2)}) collective-permute-start(f32[128,512]{1,0:T(8,128)S(1)} %get-tuple-element.79), channel_id=1, source_target_pairs={{0,8},{1,9},{2,10},{3,11},{4,12},{5,13},{6,14},{7,15},{8,16},{9,17... | collective-permute-start | bytes 786440 | tf_op jit(solution)/shard_map/ppermute | solution.py:361
  67.6 8.7 %collective-permute-start.22 = (f32[128,512]{1,0:T(8,128)S(1)}, f32[128,512]{1,0:T(8,128)S(1)}, u32[]{:S(2)}, u32[]{:S(2)}) collective-permute-start(f32[128,512]{1,0:T(8,128)S(1)} %get-tuple-element.81), channel_id=1, source_target_pairs={{8,0},{9,1},{10,2},{11,3},{12,4},{13,5},{14,6},{15,7},{16,8},{17,9... | collective-permute-start | bytes 786440 | tf_op jit(solution)/shard_map/ppermute | solution.py:361
  69.8 15.6 %collective-permute-start.24 = (f32[128,512]{1,0:T(8,128)S(1)}, f32[128,512]{1,0:T(8,128)S(1)}, u32[]{:S(2)}, u32[]{:S(2)}) collective-permute-start(f32[128,512]{1,0:T(8,128)S(1)} %get-tuple-element.84), channel_id=1, source_target_pairs={{0,8},{1,9},{2,10},{3,11},{4,12},{5,13},{6,14},{7,15},{8,16},{9,17... | collective-permute-start | bytes 786440 | tf_op jit(solution)/shard_map/ppermute | solution.py:361
  73.0 12.3 %collective-permute-start.25 = (f32[128,512]{1,0:T(8,128)S(1)}, f32[128,512]{1,0:T(8,128)S(1)}, u32[]{:S(2)}, u32[]{:S(2)}) collective-permute-start(f32[128,512]{1,0:T(8,128)S(1)} %get-tuple-element.85), channel_id=1, source_target_pairs={{8,0},{9,1},{10,2},{11,3},{12,4},{13,5},{14,6},{15,7},{16,8},{17,9... | collective-permute-start | bytes 786440 | tf_op jit(solution)/shard_map/ppermute | solution.py:361
  77.7 7.6 %collective-permute-start.23 = (f32[136,384]{1,0:T(8,128)S(1)}, f32[136,384]{1,0:T(8,128)S(1)}, u32[]{:S(2)}, u32[]{:S(2)}) collective-permute-start(f32[136,384]{1,0:T(8,128)S(1)} %get-tuple-element.83), channel_id=1, source_target_pairs={{0,8},{1,9},{2,10},{3,11},{4,12},{5,13},{6,14},{7,15},{8,0},{9,1},... | collective-permute-start | bytes 626696 | tf_op jit(solution)/shard_map/ppermute | solution.py:361
  80.0 6.4 %collective-permute-start.26 = (f32[128,512]{1,0:T(8,128)S(1)}, f32[128,512]{1,0:T(8,128)S(1)}, u32[]{:S(2)}, u32[]{:S(2)}) collective-permute-start(f32[128,512]{1,0:T(8,128)S(1)} %get-tuple-element.87), channel_id=1, source_target_pairs={{0,8},{1,9},{2,10},{3,11},{4,12},{5,13},{6,14},{7,15},{8,16},{9,17... | collective-permute-start | bytes 786440 | tf_op jit(solution)/shard_map/ppermute | solution.py:361
  81.9 12.2 %collective-permute-start.27 = (f32[128,512]{1,0:T(8,128)S(1)}, f32[128,512]{1,0:T(8,128)S(1)}, u32[]{:S(2)}, u32[]{:S(2)}) collective-permute-start(f32[128,512]{1,0:T(8,128)S(1)} %get-tuple-element.89), channel_id=1, source_target_pairs={{8,0},{9,1},{10,2},{11,3},{12,4},{13,5},{14,6},{15,7},{16,8},{17,9... | collective-permute-start | bytes 786440 | tf_op jit(solution)/shard_map/ppermute | solution.py:361
  85.4 13.0 %collective-permute-start.30 = (f32[136,384]{1,0:T(8,128)S(1)}, f32[136,384]{1,0:T(8,128)S(1)}, u32[]{:S(2)}, u32[]{:S(2)}) collective-permute-start(f32[136,384]{1,0:T(8,128)S(1)} %add.10), channel_id=1, source_target_pairs={{0,16},{1,17},{2,18},{3,19},{4,20},{5,21},{6,22},{7,23},{8,24},{9,... | collective-permute-start | bytes 626696 | tf_op jit(solution)/shard_map/ppermute | solution.py:361
  94.1 26.6 %copy-start = (f32[4,256,128]{2,1,0:T(8,128)S(1)}, f32[4,256,128]{2,1,0:T(8,128)}, u32[]{:S(2)}) copy-start(f32[4,256,128]{2,1,0:T(8,128)} %link_ref.3) | copy-start | bytes 1572868
  94.1 26.6 %copy-start.12 = (s32[8,8]{1,0:T(8,128)S(1)}, s32[8,8]{1,0:T(8,128)}, u32[]{:S(2)}) copy-start(s32[8,8]{1,0:T(8,128)} %first_ref.5) | copy-start | bytes 772
  94.1 26.6 %copy-start.14 = (s32[8,16]{1,0:T(8,128)S(1)}, s32[8,16]{1,0:T(8,128)}, u32[]{:S(2)}) copy-start(s32[8,16]{1,0:T(8,128)} %second_ref.3) | copy-start | bytes 1540
  94.1 26.6 %copy-start.16 = (s32[8]{0:T(128)S(1)}, s32[8]{0:T(128)}, u32[]{:S(2)}) copy-start(s32[8]{0:T(128)} %one_ref.3) | copy-start | bytes 100
  94.2 26.6 %copy-start.18 = (s32[16]{0:T(128)S(1)}, s32[16]{0:T(128)}, u32[]{:S(2)}) copy-start(s32[16]{0:T(128)} %parent_ref.5) | copy-start | bytes 196
  94.2 26.6 %copy-start.20 = (s32[16]{0:T(128)S(1)}, s32[16]{0:T(128)}, u32[]{:S(2)}) copy-start(s32[16]{0:T(128)} %two_ref.3) | copy-start | bytes 196
  94.8 35.0 %copy-start.4 = (f32[2,256,256]{2,1,0:T(8,128)S(1)}, f32[2,256,256]{2,1,0:T(8,128)}, u32[]{:S(2)}) copy-start(f32[2,256,256]{2,1,0:T(8,128)} %pivot1_ref.1) | copy-start | bytes 1572868
  94.8 35.0 %copy-start.9 = (f32[4,128,128]{2,1,0:T(8,128)S(1)}, f32[4,128,128]{2,1,0:T(8,128)}, u32[]{:S(2)}) copy-start(f32[4,128,128]{2,1,0:T(8,128)} %pivot2_ref.1) | copy-start | bytes 786436
  94.8 3.5 %collective-permute-start.31 = (f32[136,128]{1,0:T(8,128)S(1)}, f32[136,128]{1,0:T(8,128)S(1)}, u32[]{:S(2)}, u32[]{:S(2)}) collective-permute-start(f32[136,128]{1,0:T(8,128)S(1)} %get-tuple-element.96), channel_id=1, source_target_pairs={{0,8},{1,9},{2,10},{3,11},{4,12},{5,13},{6,14},{7,15},{8,0},{9,1},... | collective-permute-start | bytes 208904 | tf_op jit(solution)/shard_map/ppermute | solution.py:361
  98.4 10.6 %collective-permute-start.32 = (f32[136,384]{1,0:T(8,128)S(1)}, f32[136,384]{1,0:T(8,128)S(1)}, u32[]{:S(2)}, u32[]{:S(2)}) collective-permute-start(f32[136,384]{1,0:T(8,128)S(1)} %add.12.grams_ref), channel_id=1, source_target_pairs={{0,8},{1,9},{2,10},{3,11},{4,12},{5,13},{6,14},{7,15},{8,0},{9,1},... | collective-permute-start | bytes 626696 | tf_op jit(solution)/shard_map/ppermute | solution.py:361
  98.5 10.5 %collective-permute-start.33 = (f32[136,128]{1,0:T(8,128)S(1)}, f32[136,128]{1,0:T(8,128)S(1)}, u32[]{:S(2)}, u32[]{:S(2)}) collective-permute-start(f32[136,128]{1,0:T(8,128)S(1)} %add.11.refs_0_), channel_id=1, source_target_pairs={{0,16},{1,17},{2,18},{3,19},{4,20},{5,21},{6,22},{7,23},{8,24},{9,... | collective-permute-start | bytes 208904 | tf_op jit(solution)/shard_map/ppermute | solution.py:361
  98.5 16.3 %collective-permute-start.28 = (f32[512,256]{1,0:T(8,128)S(1)}, f32[512,256]{1,0:T(8,128)S(1)}, u32[]{:S(2)}, u32[]{:S(2)}) collective-permute-start(f32[512,256]{1,0:T(8,128)S(1)} %get-tuple-element.92), channel_id=1, source_target_pairs={{0,4},{1,0},{2,6},{3,2},{4,5},{5,1},{6,7},{7,3},{8,12},{9,8},{10,1... | collective-permute-start | bytes 1572872 | tf_op jit(solution)/shard_map/ppermute | solution.py:361
  104.0 16.7 %collective-permute-start.29 = (f32[512,256]{1,0:T(8,128)S(1)}, f32[512,256]{1,0:T(8,128)S(1)}, u32[]{:S(2)}, u32[]{:S(2)}) collective-permute-start(f32[512,256]{1,0:T(8,128)S(1)} %get-tuple-element.93), channel_id=1, source_target_pairs={{1,4},{3,6},{4,1},{6,3},{9,12},{11,14},{12,9},{14,11},{17,20},{19,... | collective-permute-start | bytes 1572872 | tf_op jit(solution)/shard_map/ppermute | solution.py:361
  109.0 20.8 %collective-permute-start.35 = (f32[136,896]{1,0:T(8,128)S(1)}, f32[136,896]{1,0:T(8,128)S(1)}, u32[]{:S(2)}, u32[]{:S(2)}) collective-permute-start(f32[136,896]{1,0:T(8,128)S(1)} %collect.1.own), channel_id=1, source_target_pairs={{1,4},{3,6},{4,1},{6,3},{9,12},{11,14},{12,9},{14,11},{17,20},{19,... | collective-permute-start | bytes 1462280 | tf_op jit(solution)/shard_map/ppermute | solution.py:361
  114.8 15.0 %collective-permute-start.34 = (f32[136,896]{1,0:T(8,128)S(1)}, f32[136,896]{1,0:T(8,128)S(1)}, u32[]{:S(2)}, u32[]{:S(2)}) collective-permute-start(f32[136,896]{1,0:T(8,128)S(1)} %collect.1.own), channel_id=1, source_target_pairs={{0,4},{1,0},{2,6},{3,2},{4,5},{5,1},{6,7},{7,3},{8,12},{9,8},{10,1... | collective-permute-start | bytes 1462280 | tf_op jit(solution)/shard_map/ppermute | solution.py:361
  (9 other events, 6.4 us)

commit v5 on v4

--- a/solution.py
+++ b/solution.py
@@ -385,9 +385,9 @@
             return lax.optimization_barrier(values)
 
         piece = array(b1 // CHUNKS, span)
-        beside = send(anc_inverse, other_y)
         turns = [pairs(lambda z, y, x, k: (z, y, (x + s) % wide, k)) for s in range(1, wide)]
         tops = [send(anc_inverse, turn) for turn in turns]
+        beside = send(anc_inverse, other_y)
         beside, *tops = tie(beside, *tops)
         kept1, give1 = call(pack_one, [block] * 2, [factor_one, pattern_one, size_one], scalars=2, name="pack_one")
         near1, far1 = send(give1, to_worker), send(kept1, across)
@@ -404,7 +404,7 @@
         near2, far2 = send(give2, to_worker), send(kept2, across)
         (w2,) = call(join, [array(b1, span)], [kept2, near2, far2], name="join_two")
         passed, _ = tie(beside, w1)
-        middle = rows // 2
+        middle = rows * 5 // 64 * 8
         tiles = [[anc_inverse, beside]]
         for turn, top in zip(turns, tops):
             tiles.append([top, send(passed[:middle], turn), send(top[middle:], other_y)])
@@ -518,7 +518,7 @@
         while 2 * step < depth:
             energy = energy + swap(energy, step)
             step *= 2
-        arrived, energy = tie(arrived, energy)
+        arrived, _ = tie(arrived, energy)
         grams = grams + arrived
         grams_too = swap(grams, 1)
         energies = [energy, swap(energy, step)]

time: 134 us -> 133 us (level)
  the two profiles are of different devices: /device:TPU:1 before, /device:TPU:22 now
where the time goes in v5:
time: 133 us
  starting transfers between devices  64.3 us (48%)
  waiting for transfers between devices  41 us (31%)
  Pallas kernels  15.4 us (12%)
  local copies, waits for them, and re-layouts  10.5 us (8%)
    ppermute x36, starting transfers between devices, send(): return lax.ppermute(value, AXES, perm)  64.3 us
    ppermute x36, waiting for transfers between devices, send(): return lax.ppermute(value, AXES, perm)  41 us
    pallas_call x12, Pallas kernels, call(): pl.pallas_call(body, out_shape=outs, in_specs=specs, out_specs=[VMEM] * l...  14.3 us
    unnamed x46, local copies, waits for them, and re-layouts  10.5 us
  transfers between devices with their start and end apart: 36, of which 13 were waited for; matrix products, arithmetic and copies ran while one was open for 0% of the time, Pallas kernels for 6%

profile of v5, /device:TPU:22, one launch (start us, length us, event | category | flops | bytes accessed | tf_op | source)
XLA Modules:
  0.0 132.6 jit_solution(123976143143133023)
XLA Ops:
  0.7 1.1 copy-done.2
  1.7 0.7 copy-done.12
  3.1 0.8 pack_one.1
  4.4 2.6 %collective-permute-start.1 = (f32[256,256]{1,0:T(8,128)S(1)}, f32[256,256]{1,0:T(8,128)S(1)}, u32[]{:S(2)}, u32[]{:S(2)}) collective-permute-start(f32[256,256]{1,0:T(8,128)S(1)} %get-tuple-element.54.kept_ref), channel_id=1, source_target_pairs={{1,4},{3,6},{4,1},{6,3},{9,12},{11,14},{12,9},{14,11},{17,20},{19,... | collective-permute-start | bytes 786440 | tf_op jit(solution)/shard_map/ppermute | solution.py:361
  7.6 0.7 collective-permute-done.near_ref
  8.3 4.8 %collective-permute-done.1.far_ref = f32[256,256]{1,0:T(8,128)S(1)} collective-permute-done((f32[256,256]{1,0:T(8,128)S(1)}, f32[256,256]{1,0:T(8,128)S(1)}, u32[]{:S(2)}, u32[]{:S(2)}) %collective-permute-start.1) | collective-permute-done | bytes 262176 | tf_op jit(solution)/shard_map/ppermute | solution.py:361
  13.1 1.0 copy-done.3
  14.1 0.7 copy-done.13
  16.8 0.9 pack_two.1
  17.8 2.4 %collective-permute-start.5 = (f32[256,512]{1,0:T(8,128)S(1)}, f32[256,512]{1,0:T(8,128)S(1)}, u32[]{:S(2)}, u32[]{:S(2)}) collective-permute-start(f32[256,512]{1,0:T(8,128)S(1)} %join_one.1.refs_0_.refs_4_), channel_id=1, source_target_pairs={{8,0},{9,1},{10,2},{11,3},{12,4},{13,5},{14,6},{15,7},{16,8},{17,9... | collective-permute-start | bytes 1572872 | tf_op jit(solution)/shard_map/ppermute | solution.py:361
  20.2 3.8 %collective-permute-start.3 = (f32[256,256]{1,0:T(8,128)S(1)}, f32[256,256]{1,0:T(8,128)S(1)}, u32[]{:S(2)}, u32[]{:S(2)}) collective-permute-start(f32[256,256]{1,0:T(8,128)S(1)} %get-tuple-element.60.kept_ref), channel_id=1, source_target_pairs={{1,4},{3,6},{4,1},{6,3},{9,12},{11,14},{12,9},{14,11},{17,20},{19,... | collective-permute-start | bytes 786440 | tf_op jit(solution)/shard_map/ppermute | solution.py:361
  24.1 3.5 %collective-permute-start.4 = (f32[256,512]{1,0:T(8,128)S(1)}, f32[256,512]{1,0:T(8,128)S(1)}, u32[]{:S(2)}, u32[]{:S(2)}) collective-permute-start(f32[256,512]{1,0:T(8,128)S(1)} %join_one.1.refs_0_.refs_4_), channel_id=1, source_target_pairs={{0,8},{1,9},{2,10},{3,11},{4,12},{5,13},{6,14},{7,15},{8,16},{9,17... | collective-permute-start | bytes 1572872 | tf_op jit(solution)/shard_map/ppermute | solution.py:361
  27.7 0.7 copy-done.7
  29.0 0.7 copy-done.9
  29.7 3.8 %collective-permute-done.11.refs_6_ = f32[96,512]{1,0:T(8,128)} collective-permute-done((f32[96,512]{1,0:T(8,128)S(1)}, f32[96,512]{1,0:T(8,128)}, u32[]{:S(2)}, u32[]{:S(2)}) %collective-permute-start.11) | collective-permute-done | bytes 196640 | tf_op jit(solution)/shard_map/ppermute | solution.py:361
  34.0 3.9 %collective-permute-done.10.refs_5_ = f32[160,512]{1,0:T(8,128)S(1)} collective-permute-done((f32[160,512]{1,0:T(8,128)S(1)}, f32[160,512]{1,0:T(8,128)S(1)}, u32[]{:S(2)}, u32[]{:S(2)}) %collective-permute-start.10) | collective-permute-done | bytes 327712 | tf_op jit(solution)/shard_map/ppermute | solution.py:361
  38.4 0.9 copy-done.6
  39.3 0.9 copy-done.8
  40.3 0.9 copy-done.10
  41.3 4.0 %partial_products.1 = (f32[256,2048]{1,0:T(8,128)S(1)}, bf16[512,2048]{1,0:T(8,128)(2,1)S(1)}, bf16[512,2048]{1,0:T(8,128)(2,1)S(1)}) custom-call(f32[256,512]{1,0:T(8,128)S(1)} %join_two.1.w2_ref.refs_5_, f32[256,512]{1,0:T(8,128)S(1)} %copy-done.1, f32[256,512]{1,0:T(8,128)S(1)} %collective-permute-done.6.refs_1_, ...), custom_call_target="tpu_custom_call" | custom-call | tf_op jit(solution)/shard_map/partial_products/pallas_call | solution.py:320
  45.4 2.2 %collective-permute-start.15 = (f32[128,512]{1,0:T(8,128)S(1)}, f32[128,512]{1,0:T(8,128)S(1)}, u32[]{:S(2)}, u32[]{:S(2)}) collective-permute-start(f32[128,512]{1,0:T(8,128)S(1)} %get-tuple-element.73), channel_id=1, source_target_pairs={{0,8},{1,9},{2,10},{3,11},{4,12},{5,13},{6,14},{7,15},{8,16},{9,17... | collective-permute-start | bytes 786440 | tf_op jit(solution)/shard_map/ppermute | solution.py:361
  47.6 3.6 %collective-permute-start.17 = (f32[128,512]{1,0:T(8,128)S(1)}, f32[128,512]{1,0:T(8,128)S(1)}, u32[]{:S(2)}, u32[]{:S(2)}) collective-permute-start(f32[128,512]{1,0:T(8,128)S(1)} %get-tuple-element.75), channel_id=1, source_target_pairs={{8,0},{9,1},{10,2},{11,3},{12,4},{13,5},{14,6},{15,7},{16,8},{17,9... | collective-permute-start | bytes 786440 | tf_op jit(solution)/shard_map/ppermute | solution.py:361
  51.3 2.3 %collective-permute-start.16 = (f32[128,512]{1,0:T(8,128)S(1)}, f32[128,512]{1,0:T(8,128)S(1)}, u32[]{:S(2)}, u32[]{:S(2)}) collective-permute-start(f32[128,512]{1,0:T(8,128)S(1)} %get-tuple-element.74), channel_id=1, source_target_pairs={{0,8},{1,9},{2,10},{3,11},{4,12},{5,13},{6,14},{7,15},{8,16},{9,17... | collective-permute-start | bytes 786440 | tf_op jit(solution)/shard_map/ppermute | solution.py:361
  53.6 3.6 %collective-permute-start.18 = (f32[128,512]{1,0:T(8,128)S(1)}, f32[128,512]{1,0:T(8,128)S(1)}, u32[]{:S(2)}, u32[]{:S(2)}) collective-permute-start(f32[128,512]{1,0:T(8,128)S(1)} %get-tuple-element.76), channel_id=1, source_target_pairs={{8,0},{9,1},{10,2},{11,3},{12,4},{13,5},{14,6},{15,7},{16,8},{17,9... | collective-permute-start | bytes 786440 | tf_op jit(solution)/shard_map/ppermute | solution.py:361
  57.2 0.9 collective-permute-done.17.refs_2_.refs_1_
  58.2 1.9 %collective-permute-start.19 = (f32[128,512]{1,0:T(8,128)S(1)}, f32[128,512]{1,0:T(8,128)S(1)}, u32[]{:S(2)}, u32[]{:S(2)}) collective-permute-start(f32[128,512]{1,0:T(8,128)S(1)} %get-tuple-element.77), channel_id=1, source_target_pairs={{0,8},{1,9},{2,10},{3,11},{4,12},{5,13},{6,14},{7,15},{8,16},{9,17... | collective-permute-start | bytes 786440 | tf_op jit(solution)/shard_map/ppermute | solution.py:361
  60.1 3.9 %collective-permute-start.21 = (f32[128,512]{1,0:T(8,128)S(1)}, f32[128,512]{1,0:T(8,128)S(1)}, u32[]{:S(2)}, u32[]{:S(2)}) collective-permute-start(f32[128,512]{1,0:T(8,128)S(1)} %get-tuple-element.79), channel_id=1, source_target_pairs={{8,0},{9,1},{10,2},{11,3},{12,4},{13,5},{14,6},{15,7},{16,8},{17,9... | collective-permute-start | bytes 786440 | tf_op jit(solution)/shard_map/ppermute | solution.py:361
  64.2 1.9 %collective-permute-start.20 = (f32[128,512]{1,0:T(8,128)S(1)}, f32[128,512]{1,0:T(8,128)S(1)}, u32[]{:S(2)}, u32[]{:S(2)}) collective-permute-start(f32[128,512]{1,0:T(8,128)S(1)} %get-tuple-element.78), channel_id=1, source_target_pairs={{0,8},{1,9},{2,10},{3,11},{4,12},{5,13},{6,14},{7,15},{8,16},{9,17... | collective-permute-start | bytes 786440 | tf_op jit(solution)/shard_map/ppermute | solution.py:361
  66.1 3.9 %collective-permute-start.22 = (f32[128,512]{1,0:T(8,128)S(1)}, f32[128,512]{1,0:T(8,128)S(1)}, u32[]{:S(2)}, u32[]{:S(2)}) collective-permute-start(f32[128,512]{1,0:T(8,128)S(1)} %get-tuple-element.80), channel_id=1, source_target_pairs={{8,0},{9,1},{10,2},{11,3},{12,4},{13,5},{14,6},{15,7},{16,8},{17,9... | collective-permute-start | bytes 786440 | tf_op jit(solution)/shard_map/ppermute | solution.py:361
  70.2 1.9 %collective-permute-start.24 = (f32[128,512]{1,0:T(8,128)S(1)}, f32[128,512]{1,0:T(8,128)S(1)}, u32[]{:S(2)}, u32[]{:S(2)}) collective-permute-start(f32[128,512]{1,0:T(8,128)S(1)} %get-tuple-element.83), channel_id=1, source_target_pairs={{0,8},{1,9},{2,10},{3,11},{4,12},{5,13},{6,14},{7,15},{8,16},{9,17... | collective-permute-start | bytes 786440 | tf_op jit(solution)/shard_map/ppermute | solution.py:361
  72.1 3.9 %collective-permute-start.25 = (f32[128,512]{1,0:T(8,128)S(1)}, f32[128,512]{1,0:T(8,128)S(1)}, u32[]{:S(2)}, u32[]{:S(2)}) collective-permute-start(f32[128,512]{1,0:T(8,128)S(1)} %get-tuple-element.84), channel_id=1, source_target_pairs={{8,0},{9,1},{10,2},{11,3},{12,4},{13,5},{14,6},{15,7},{16,8},{17,9... | collective-permute-start | bytes 786440 | tf_op jit(solution)/shard_map/ppermute | solution.py:361
  76.7 1.3 next_product.2.total_ref
  78.7 0.8 gram_products.1
  79.6 3.9 %collective-permute-start.26 = (f32[128,512]{1,0:T(8,128)S(1)}, f32[128,512]{1,0:T(8,128)S(1)}, u32[]{:S(2)}, u32[]{:S(2)}) collective-permute-start(f32[128,512]{1,0:T(8,128)S(1)} %get-tuple-element.86), channel_id=1, source_target_pairs={{0,8},{1,9},{2,10},{3,11},{4,12},{5,13},{6,14},{7,15},{8,16},{9,17... | collective-permute-start | bytes 786440 | tf_op jit(solution)/shard_map/ppermute | solution.py:361
  83.5 2.0 %collective-permute-start.27 = (f32[128,512]{1,0:T(8,128)S(1)}, f32[128,512]{1,0:T(8,128)S(1)}, u32[]{:S(2)}, u32[]{:S(2)}) collective-permute-start(f32[128,512]{1,0:T(8,128)S(1)} %get-tuple-element.88), channel_id=1, source_target_pairs={{8,0},{9,1},{10,2},{11,3},{12,4},{13,5},{14,6},{15,7},{16,8},{17,9... | collective-permute-start | bytes 786440 | tf_op jit(solution)/shard_map/ppermute | solution.py:361
  85.6 4.9 %collective-permute-start.30 = (f32[136,384]{1,0:T(8,128)S(1)}, f32[136,384]{1,0:T(8,128)S(1)}, u32[]{:S(2)}, u32[]{:S(2)}) collective-permute-start(f32[136,384]{1,0:T(8,128)S(1)} %add.10), channel_id=1, source_target_pairs={{0,16},{1,17},{2,18},{3,19},{4,20},{5,21},{6,22},{7,23},{8,24},{9,... | collective-permute-start | bytes 626696 | tf_op jit(solution)/shard_map/ppermute | solution.py:361
  90.5 1.2 collective-permute-done.26.refs_2_
  91.6 2.3 %collective-permute-done.27.refs_4_ = f32[128,512]{1,0:T(8,128)S(1)} collective-permute-done((f32[128,512]{1,0:T(8,128)S(1)}, f32[128,512]{1,0:T(8,128)S(1)}, u32[]{:S(2)}, u32[]{:S(2)}) %collective-permute-start.27) | collective-permute-done | bytes 262176 | tf_op jit(solution)/shard_map/ppermute | solution.py:361
  94.7 5.0 %collective-permute-done.31 = f32[136,128]{1,0:T(8,128)S(1)} collective-permute-done((f32[136,128]{1,0:T(8,128)S(1)}, f32[136,128]{1,0:T(8,128)S(1)}, u32[]{:S(2)}, u32[]{:S(2)}) %collective-permute-start.31) | collective-permute-done | bytes 69664 | tf_op jit(solution)/shard_map/ppermute | solution.py:361
  99.8 4.5 %collective-permute-start.33 = (f32[136,128]{1,0:T(8,128)S(1)}, f32[136,128]{1,0:T(8,128)S(1)}, u32[]{:S(2)}, u32[]{:S(2)}) collective-permute-start(f32[136,128]{1,0:T(8,128)S(1)} %add.11.refs_0_), channel_id=1, source_target_pairs={{0,16},{1,17},{2,18},{3,19},{4,20},{5,21},{6,22},{7,23},{8,24},{9,... | collective-permute-start | bytes 208904 | tf_op jit(solution)/shard_map/ppermute | solution.py:361
  104.4 3.1 %collective-permute-start.29 = (f32[512,256]{1,0:T(8,128)S(1)}, f32[512,256]{1,0:T(8,128)S(1)}, u32[]{:S(2)}, u32[]{:S(2)}) collective-permute-start(f32[512,256]{1,0:T(8,128)S(1)} %get-tuple-element.92), channel_id=1, source_target_pairs={{1,4},{3,6},{4,1},{6,3},{9,12},{11,14},{12,9},{14,11},{17,20},{19,... | collective-permute-start | bytes 1572872 | tf_op jit(solution)/shard_map/ppermute | solution.py:361
  107.5 1.4 %collective-permute-done.33.refs_1_ = f32[136,128]{1,0:T(8,128)S(1)} collective-permute-done((f32[136,128]{1,0:T(8,128)S(1)}, f32[136,128]{1,0:T(8,128)S(1)}, u32[]{:S(2)}, u32[]{:S(2)}) %collective-permute-start.33) | collective-permute-done | bytes 69664 | tf_op jit(solution)/shard_map/ppermute | solution.py:361
  108.9 1.9 %collective-permute-start.35 = (f32[136,896]{1,0:T(8,128)S(1)}, f32[136,896]{1,0:T(8,128)S(1)}, u32[]{:S(2)}, u32[]{:S(2)}) collective-permute-start(f32[136,896]{1,0:T(8,128)S(1)} %collect.1.own), channel_id=1, source_target_pairs={{1,4},{3,6},{4,1},{6,3},{9,12},{11,14},{12,9},{14,11},{17,20},{19,... | collective-permute-start | bytes 1462280 | tf_op jit(solution)/shard_map/ppermute | solution.py:361
  110.9 6.9 %collective-permute-done.28.near = f32[512,256]{1,0:T(8,128)S(1)} collective-permute-done((f32[512,256]{1,0:T(8,128)S(1)}, f32[512,256]{1,0:T(8,128)S(1)}, u32[]{:S(2)}, u32[]{:S(2)}) %collective-permute-start.28) | collective-permute-done | bytes 524320 | tf_op jit(solution)/shard_map/ppermute | solution.py:361
  117.8 2.7 %collective-permute-done.29.far = f32[512,256]{1,0:T(8,128)S(1)} collective-permute-done((f32[512,256]{1,0:T(8,128)S(1)}, f32[512,256]{1,0:T(8,128)S(1)}, u32[]{:S(2)}, u32[]{:S(2)}) %collective-permute-start.29) | collective-permute-done | bytes 524320 | tf_op jit(solution)/shard_map/ppermute | solution.py:361
  120.5 2.2 %finish_rows.1 = (f32[256,512]{1,0:T(8,128)}, f32[256,512]{1,0:T(8,128)}) custom-call(f32[512,256]{1,0:T(8,128)S(1)} %get-tuple-element.90.own, f32[512,256]{1,0:T(8,128)S(1)} %collective-permute-done.28.near, f32[512,256]{1,0:T(8,128)S(1)} %collective-permute-done.29.far, f32[4,256,128]{2,1,0:T(8,128)S(1)} %copy-done, s32[8,8]{1,0:T(8,128)S(1)} %copy-done.14, ...), custom_call_target="tpu_custom_call" | custom-call | tf_op jit(solution)/shard_map/finish_rows/pallas_call | solution.py:320
  122.7 6.9 %collective-permute-done.35.far = f32[136,896]{1,0:T(8,128)S(1)} collective-permute-done((f32[136,896]{1,0:T(8,128)S(1)}, f32[136,896]{1,0:T(8,128)S(1)}, u32[]{:S(2)}, u32[]{:S(2)}) %collective-permute-start.35) | collective-permute-done | bytes 487456 | tf_op jit(solution)/shard_map/ppermute | solution.py:361
  129.6 3.0 %finish_blocks.1 = (f32[2,256,256]{2,1,0:T(8,128)}, f32[4,256,128]{2,1,0:T(8,128)}, f32[4,128,128]{2,1,0:T(8,128)}) custom-call(f32[136,896]{1,0:T(8,128)S(1)} %collect.1.own, f32[136,896]{1,0:T(8,128)S(1)} %collective-permute-done.34.near, f32[136,896]{1,0:T(8,128)S(1)} %collective-permute-done.35.far, f32[2,256,256]{2,1,0:T(8,128)S(1)} %copy-done.4, ...), custom_call_target="tpu_custom_call" | custom-call | tf_op jit(solution)/shard_map/finish_blocks/pallas_call | solution.py:320
  (94 shorter events, 8.5 us)
Async XLA Ops:
  0.6 29.1 %copy-start.1 = (f32[256,512]{1,0:T(8,128)S(1)}, f32[256,512]{1,0:T(8,128)}, u32[]{:S(2)}) copy-start(f32[256,512]{1,0:T(8,128)} %refs_0_.1) | copy-start | bytes 1572868
  0.6 1.1 copy-start.2
  3.9 4.4 %collective-permute-start = (f32[256,256]{1,0:T(8,128)S(1)}, f32[256,256]{1,0:T(8,128)S(1)}, u32[]{:S(2)}, u32[]{:S(2)}) collective-permute-start(f32[256,256]{1,0:T(8,128)S(1)} %get-tuple-element.53), channel_id=1, source_target_pairs={{0,1},{1,5},{2,3},{3,7},{4,0},{5,4},{6,2},{7,6},{8,9},{9,13},{10,1... | collective-permute-start | bytes 786440 | tf_op jit(solution)/shard_map/ppermute | solution.py:361
  4.4 8.6 %collective-permute-start.1 = (f32[256,256]{1,0:T(8,128)S(1)}, f32[256,256]{1,0:T(8,128)S(1)}, u32[]{:S(2)}, u32[]{:S(2)}) collective-permute-start(f32[256,256]{1,0:T(8,128)S(1)} %get-tuple-element.54.kept_ref), channel_id=1, source_target_pairs={{1,4},{3,6},{4,1},{6,3},{9,12},{11,14},{12,9},{14,11},{17,20},{19,... | collective-permute-start | bytes 786440 | tf_op jit(solution)/shard_map/ppermute | solution.py:361
  7.0 17.0 %collective-permute-start.7 = (f32[256,512]{1,0:T(8,128)}, f32[256,512]{1,0:T(8,128)S(1)}, u32[]{:S(2)}, u32[]{:S(2)}) collective-permute-start(f32[256,512]{1,0:T(8,128)} %refs_0_.1), channel_id=1, source_target_pairs={{0,2},{1,3},{2,0},{3,1},{4,6},{5,7},{6,4},{7,5},{8,10},{9,11},{10,... | collective-permute-start | bytes 1572872 | tf_op jit(solution)/shard_map/ppermute | solution.py:361
  7.6 20.0 %collective-permute-start.6 = (f32[256,512]{1,0:T(8,128)}, f32[256,512]{1,0:T(8,128)S(1)}, u32[]{:S(2)}, u32[]{:S(2)}) collective-permute-start(f32[256,512]{1,0:T(8,128)} %refs_0_.1), channel_id=1, source_target_pairs={{0,4},{1,5},{2,6},{3,7},{4,0},{5,1},{6,2},{7,3},{8,12},{9,13},{10,... | collective-permute-start | bytes 1572872 | tf_op jit(solution)/shard_map/ppermute | solution.py:361
  13.1 1.0 copy-start.3
  17.7 20.2 %copy-start.5 = (f32[256,256]{1,0:T(8,128)}, f32[256,256]{1,0:T(8,128)S(1)}, u32[]{:S(2)}) copy-start(f32[256,256]{1,0:T(8,128)S(1)} %get-tuple-element.60.kept_ref) | copy-start | bytes 786436
  17.8 15.6 %collective-permute-start.5 = (f32[256,512]{1,0:T(8,128)S(1)}, f32[256,512]{1,0:T(8,128)S(1)}, u32[]{:S(2)}, u32[]{:S(2)}) collective-permute-start(f32[256,512]{1,0:T(8,128)S(1)} %join_one.1.refs_0_.refs_4_), channel_id=1, source_target_pairs={{8,0},{9,1},{10,2},{11,3},{12,4},{13,5},{14,6},{15,7},{16,8},{17,9... | collective-permute-start | bytes 1572872 | tf_op jit(solution)/shard_map/ppermute | solution.py:361
  20.2 7.5 %collective-permute-start.2 = (f32[256,256]{1,0:T(8,128)S(1)}, f32[256,256]{1,0:T(8,128)S(1)}, u32[]{:S(2)}, u32[]{:S(2)}) collective-permute-start(f32[256,256]{1,0:T(8,128)S(1)} %get-tuple-element.61), channel_id=1, source_target_pairs={{0,1},{1,5},{2,3},{3,7},{4,0},{5,4},{6,2},{7,6},{8,9},{9,13},{10,1... | collective-permute-start | bytes 786440 | tf_op jit(solution)/shard_map/ppermute | solution.py:361
  20.2 8.8 %collective-permute-start.3 = (f32[256,256]{1,0:T(8,128)S(1)}, f32[256,256]{1,0:T(8,128)S(1)}, u32[]{:S(2)}, u32[]{:S(2)}) collective-permute-start(f32[256,256]{1,0:T(8,128)S(1)} %get-tuple-element.60.kept_ref), channel_id=1, source_target_pairs={{1,4},{3,6},{4,1},{6,3},{9,12},{11,14},{12,9},{14,11},{17,20},{19,... | collective-permute-start | bytes 786440 | tf_op jit(solution)/shard_map/ppermute | solution.py:361
  24.1 13.8 %collective-permute-start.4 = (f32[256,512]{1,0:T(8,128)S(1)}, f32[256,512]{1,0:T(8,128)S(1)}, u32[]{:S(2)}, u32[]{:S(2)}) collective-permute-start(f32[256,512]{1,0:T(8,128)S(1)} %join_one.1.refs_0_.refs_4_), channel_id=1, source_target_pairs={{0,8},{1,9},{2,10},{3,11},{4,12},{5,13},{6,14},{7,15},{8,16},{9,17... | collective-permute-start | bytes 1572872 | tf_op jit(solution)/shard_map/ppermute | solution.py:361
  27.6 5.8 %collective-permute-start.11 = (f32[96,512]{1,0:T(8,128)S(1)}, f32[96,512]{1,0:T(8,128)}, u32[]{:S(2)}, u32[]{:S(2)}) collective-permute-start(f32[96,512]{1,0:T(8,128)S(1)} %slice.7), channel_id=1, source_target_pairs={{0,4},{1,5},{2,6},{3,7},{4,0},{5,1},{6,2},{7,3},{8,12},{9,13},{10,... | collective-permute-start | bytes 589832 | tf_op jit(solution)/shard_map/ppermute | solution.py:361
  28.4 9.4 %collective-permute-start.10 = (f32[160,512]{1,0:T(8,128)S(1)}, f32[160,512]{1,0:T(8,128)S(1)}, u32[]{:S(2)}, u32[]{:S(2)}) collective-permute-start(f32[160,512]{1,0:T(8,128)S(1)} %slice.6), channel_id=1, source_target_pairs={{0,2},{1,3},{2,0},{3,1},{4,6},{5,7},{6,4},{7,5},{8,10},{9,11},{10,... | collective-permute-start | bytes 983048 | tf_op jit(solution)/shard_map/ppermute | solution.py:361
  29.7 11.6 %collective-permute-start.8 = (f32[256,512]{1,0:T(8,128)S(1)}, f32[256,512]{1,0:T(8,128)}, u32[]{:S(2)}, u32[]{:S(2)}) collective-permute-start(f32[256,512]{1,0:T(8,128)S(1)} %copy-done.1), channel_id=1, source_target_pairs={{0,1},{1,0},{2,3},{3,2},{4,5},{5,4},{6,7},{7,6},{8,9},{9,8},{10,11... | collective-permute-start | bytes 1572872 | tf_op jit(solution)/shard_map/ppermute | solution.py:361
  33.4 7.9 %collective-permute-start.9 = (f32[256,512]{1,0:T(8,128)S(1)}, f32[256,512]{1,0:T(8,128)}, u32[]{:S(2)}, u32[]{:S(2)}) collective-permute-start(f32[256,512]{1,0:T(8,128)S(1)} %collective-permute-done.6.refs_1_), channel_id=1, source_target_pairs={{0,1},{1,0},{2,3},{3,2},{4,5},{5,4},{6,7},{7,6},{8,9},{9,8},{10,11... | collective-permute-start | bytes 1572872 | tf_op jit(solution)/shard_map/ppermute | solution.py:361
  33.5 7.9 %collective-permute-start.12 = (f32[256,512]{1,0:T(8,128)S(1)}, f32[256,512]{1,0:T(8,128)}, u32[]{:S(2)}, u32[]{:S(2)}) collective-permute-start(f32[256,512]{1,0:T(8,128)S(1)} %collective-permute-done.7.refs_4_), channel_id=1, source_target_pairs={{0,1},{1,0},{2,3},{3,2},{4,5},{5,4},{6,7},{7,6},{8,9},{9,8},{10,11... | collective-permute-start | bytes 1572872 | tf_op jit(solution)/shard_map/ppermute | solution.py:361
  37.9 3.5 %collective-permute-start.13 = (f32[160,512]{1,0:T(8,128)S(1)}, f32[160,512]{1,0:T(8,128)}, u32[]{:S(2)}, u32[]{:S(2)}) collective-permute-start(f32[160,512]{1,0:T(8,128)S(1)} %collective-permute-done.10.refs_5_), channel_id=1, source_target_pairs={{0,1},{1,0},{2,3},{3,2},{4,5},{5,4},{6,7},{7,6},{8,9},{9,8},{10,11... | collective-permute-start | bytes 983048 | tf_op jit(solution)/shard_map/ppermute | solution.py:361
  37.9 3.4 %collective-permute-start.14 = (f32[96,512]{1,0:T(8,128)}, f32[96,512]{1,0:T(8,128)}, u32[]{:S(2)}, u32[]{:S(2)}) collective-permute-start(f32[96,512]{1,0:T(8,128)} %collective-permute-done.11.refs_6_), channel_id=1, source_target_pairs={{0,1},{1,0},{2,3},{3,2},{4,5},{5,4},{6,7},{7,6},{8,9},{9,8},{10,11... | collective-permute-start | bytes 589832 | tf_op jit(solution)/shard_map/ppermute | solution.py:361
  45.4 11.8 %collective-permute-start.15 = (f32[128,512]{1,0:T(8,128)S(1)}, f32[128,512]{1,0:T(8,128)S(1)}, u32[]{:S(2)}, u32[]{:S(2)}) collective-permute-start(f32[128,512]{1,0:T(8,128)S(1)} %get-tuple-element.73), channel_id=1, source_target_pairs={{0,8},{1,9},{2,10},{3,11},{4,12},{5,13},{6,14},{7,15},{8,16},{9,17... | collective-permute-start | bytes 786440 | tf_op jit(solution)/shard_map/ppermute | solution.py:361
  47.6 10.5 %collective-permute-start.17 = (f32[128,512]{1,0:T(8,128)S(1)}, f32[128,512]{1,0:T(8,128)S(1)}, u32[]{:S(2)}, u32[]{:S(2)}) collective-permute-start(f32[128,512]{1,0:T(8,128)S(1)} %get-tuple-element.75), channel_id=1, source_target_pairs={{8,0},{9,1},{10,2},{11,3},{12,4},{13,5},{14,6},{15,7},{16,8},{17,9... | collective-permute-start | bytes 786440 | tf_op jit(solution)/shard_map/ppermute | solution.py:361
  51.3 12.7 %collective-permute-start.16 = (f32[128,512]{1,0:T(8,128)S(1)}, f32[128,512]{1,0:T(8,128)S(1)}, u32[]{:S(2)}, u32[]{:S(2)}) collective-permute-start(f32[128,512]{1,0:T(8,128)S(1)} %get-tuple-element.74), channel_id=1, source_target_pairs={{0,8},{1,9},{2,10},{3,11},{4,12},{5,13},{6,14},{7,15},{8,16},{9,17... | collective-permute-start | bytes 786440 | tf_op jit(solution)/shard_map/ppermute | solution.py:361
  53.6 10.5 %collective-permute-start.18 = (f32[128,512]{1,0:T(8,128)S(1)}, f32[128,512]{1,0:T(8,128)S(1)}, u32[]{:S(2)}, u32[]{:S(2)}) collective-permute-start(f32[128,512]{1,0:T(8,128)S(1)} %get-tuple-element.76), channel_id=1, source_target_pairs={{8,0},{9,1},{10,2},{11,3},{12,4},{13,5},{14,6},{15,7},{16,8},{17,9... | collective-permute-start | bytes 786440 | tf_op jit(solution)/shard_map/ppermute | solution.py:361
  58.2 11.8 %collective-permute-start.19 = (f32[128,512]{1,0:T(8,128)S(1)}, f32[128,512]{1,0:T(8,128)S(1)}, u32[]{:S(2)}, u32[]{:S(2)}) collective-permute-start(f32[128,512]{1,0:T(8,128)S(1)} %get-tuple-element.77), channel_id=1, source_target_pairs={{0,8},{1,9},{2,10},{3,11},{4,12},{5,13},{6,14},{7,15},{8,16},{9,17... | collective-permute-start | bytes 786440 | tf_op jit(solution)/shard_map/ppermute | solution.py:361
  60.1 9.9 %collective-permute-start.21 = (f32[128,512]{1,0:T(8,128)S(1)}, f32[128,512]{1,0:T(8,128)S(1)}, u32[]{:S(2)}, u32[]{:S(2)}) collective-permute-start(f32[128,512]{1,0:T(8,128)S(1)} %get-tuple-element.79), channel_id=1, source_target_pairs={{8,0},{9,1},{10,2},{11,3},{12,4},{13,5},{14,6},{15,7},{16,8},{17,9... | collective-permute-start | bytes 786440 | tf_op jit(solution)/shard_map/ppermute | solution.py:361
  64.2 14.4 %collective-permute-start.20 = (f32[128,512]{1,0:T(8,128)S(1)}, f32[128,512]{1,0:T(8,128)S(1)}, u32[]{:S(2)}, u32[]{:S(2)}) collective-permute-start(f32[128,512]{1,0:T(8,128)S(1)} %get-tuple-element.78), channel_id=1, source_target_pairs={{0,8},{1,9},{2,10},{3,11},{4,12},{5,13},{6,14},{7,15},{8,16},{9,17... | collective-permute-start | bytes 786440 | tf_op jit(solution)/shard_map/ppermute | solution.py:361
  66.1 12.5 %collective-permute-start.22 = (f32[128,512]{1,0:T(8,128)S(1)}, f32[128,512]{1,0:T(8,128)S(1)}, u32[]{:S(2)}, u32[]{:S(2)}) collective-permute-start(f32[128,512]{1,0:T(8,128)S(1)} %get-tuple-element.80), channel_id=1, source_target_pairs={{8,0},{9,1},{10,2},{11,3},{12,4},{13,5},{14,6},{15,7},{16,8},{17,9... | collective-permute-start | bytes 786440 | tf_op jit(solution)/shard_map/ppermute | solution.py:361
  70.2 15.4 %collective-permute-start.24 = (f32[128,512]{1,0:T(8,128)S(1)}, f32[128,512]{1,0:T(8,128)S(1)}, u32[]{:S(2)}, u32[]{:S(2)}) collective-permute-start(f32[128,512]{1,0:T(8,128)S(1)} %get-tuple-element.83), channel_id=1, source_target_pairs={{0,8},{1,9},{2,10},{3,11},{4,12},{5,13},{6,14},{7,15},{8,16},{9,17... | collective-permute-start | bytes 786440 | tf_op jit(solution)/shard_map/ppermute | solution.py:361
  72.1 13.4 %collective-permute-start.25 = (f32[128,512]{1,0:T(8,128)S(1)}, f32[128,512]{1,0:T(8,128)S(1)}, u32[]{:S(2)}, u32[]{:S(2)}) collective-permute-start(f32[128,512]{1,0:T(8,128)S(1)} %get-tuple-element.84), channel_id=1, source_target_pairs={{8,0},{9,1},{10,2},{11,3},{12,4},{13,5},{14,6},{15,7},{16,8},{17,9... | collective-permute-start | bytes 786440 | tf_op jit(solution)/shard_map/ppermute | solution.py:361
  79.4 6.1 %collective-permute-start.23 = (f32[136,384]{1,0:T(8,128)S(1)}, f32[136,384]{1,0:T(8,128)S(1)}, u32[]{:S(2)}, u32[]{:S(2)}) collective-permute-start(f32[136,384]{1,0:T(8,128)S(1)} %get-tuple-element.82), channel_id=1, source_target_pairs={{0,8},{1,9},{2,10},{3,11},{4,12},{5,13},{6,14},{7,15},{8,0},{9,1},... | collective-permute-start | bytes 626696 | tf_op jit(solution)/shard_map/ppermute | solution.py:361
  79.6 12.0 %collective-permute-start.26 = (f32[128,512]{1,0:T(8,128)S(1)}, f32[128,512]{1,0:T(8,128)S(1)}, u32[]{:S(2)}, u32[]{:S(2)}) collective-permute-start(f32[128,512]{1,0:T(8,128)S(1)} %get-tuple-element.86), channel_id=1, source_target_pairs={{0,8},{1,9},{2,10},{3,11},{4,12},{5,13},{6,14},{7,15},{8,16},{9,17... | collective-permute-start | bytes 786440 | tf_op jit(solution)/shard_map/ppermute | solution.py:361
  83.5 10.4 %collective-permute-start.27 = (f32[128,512]{1,0:T(8,128)S(1)}, f32[128,512]{1,0:T(8,128)S(1)}, u32[]{:S(2)}, u32[]{:S(2)}) collective-permute-start(f32[128,512]{1,0:T(8,128)S(1)} %get-tuple-element.88), channel_id=1, source_target_pairs={{8,0},{9,1},{10,2},{11,3},{12,4},{13,5},{14,6},{15,7},{16,8},{17,9... | collective-permute-start | bytes 786440 | tf_op jit(solution)/shard_map/ppermute | solution.py:361
  85.6 14.2 %collective-permute-start.30 = (f32[136,384]{1,0:T(8,128)S(1)}, f32[136,384]{1,0:T(8,128)S(1)}, u32[]{:S(2)}, u32[]{:S(2)}) collective-permute-start(f32[136,384]{1,0:T(8,128)S(1)} %add.10), channel_id=1, source_target_pairs={{0,16},{1,17},{2,18},{3,19},{4,20},{5,21},{6,22},{7,23},{8,24},{9,... | collective-permute-start | bytes 626696 | tf_op jit(solution)/shard_map/ppermute | solution.py:361
  93.9 26.6 %copy-start = (f32[4,256,128]{2,1,0:T(8,128)S(1)}, f32[4,256,128]{2,1,0:T(8,128)}, u32[]{:S(2)}) copy-start(f32[4,256,128]{2,1,0:T(8,128)} %link_ref.3) | copy-start | bytes 1572868
  93.9 26.6 %copy-start.14 = (s32[8,8]{1,0:T(8,128)S(1)}, s32[8,8]{1,0:T(8,128)}, u32[]{:S(2)}) copy-start(s32[8,8]{1,0:T(8,128)} %first_ref.5) | copy-start | bytes 772
  93.9 26.6 %copy-start.16 = (s32[8,16]{1,0:T(8,128)S(1)}, s32[8,16]{1,0:T(8,128)}, u32[]{:S(2)}) copy-start(s32[8,16]{1,0:T(8,128)} %second_ref.3) | copy-start | bytes 1540
  93.9 26.6 %copy-start.18 = (s32[8]{0:T(128)S(1)}, s32[8]{0:T(128)}, u32[]{:S(2)}) copy-start(s32[8]{0:T(128)} %one_ref.3) | copy-start | bytes 100
  93.9 26.6 %copy-start.20 = (s32[16]{0:T(128)S(1)}, s32[16]{0:T(128)}, u32[]{:S(2)}) copy-start(s32[16]{0:T(128)} %parent_ref.5) | copy-start | bytes 196
  93.9 26.6 %copy-start.22 = (s32[16]{0:T(128)S(1)}, s32[16]{0:T(128)}, u32[]{:S(2)}) copy-start(s32[16]{0:T(128)} %two_ref.3) | copy-start | bytes 196
  94.6 35.0 %copy-start.4 = (f32[2,256,256]{2,1,0:T(8,128)S(1)}, f32[2,256,256]{2,1,0:T(8,128)}, u32[]{:S(2)}) copy-start(f32[2,256,256]{2,1,0:T(8,128)} %pivot1_ref.1) | copy-start | bytes 1572868
  94.6 35.0 %copy-start.11 = (f32[4,128,128]{2,1,0:T(8,128)S(1)}, f32[4,128,128]{2,1,0:T(8,128)}, u32[]{:S(2)}) copy-start(f32[4,128,128]{2,1,0:T(8,128)} %pivot2_ref.1) | copy-start | bytes 786436
  94.6 5.1 %collective-permute-start.31 = (f32[136,128]{1,0:T(8,128)S(1)}, f32[136,128]{1,0:T(8,128)S(1)}, u32[]{:S(2)}, u32[]{:S(2)}) collective-permute-start(f32[136,128]{1,0:T(8,128)S(1)} %get-tuple-element.95), channel_id=1, source_target_pairs={{0,8},{1,9},{2,10},{3,11},{4,12},{5,13},{6,14},{7,15},{8,0},{9,1},... | collective-permute-start | bytes 208904 | tf_op jit(solution)/shard_map/ppermute | solution.py:361
  99.8 9.1 %collective-permute-start.32 = (f32[136,384]{1,0:T(8,128)S(1)}, f32[136,384]{1,0:T(8,128)S(1)}, u32[]{:S(2)}, u32[]{:S(2)}) collective-permute-start(f32[136,384]{1,0:T(8,128)S(1)} %add.12.grams_ref), channel_id=1, source_target_pairs={{0,8},{1,9},{2,10},{3,11},{4,12},{5,13},{6,14},{7,15},{8,0},{9,1},... | collective-permute-start | bytes 626696 | tf_op jit(solution)/shard_map/ppermute | solution.py:361
  99.8 9.0 %collective-permute-start.33 = (f32[136,128]{1,0:T(8,128)S(1)}, f32[136,128]{1,0:T(8,128)S(1)}, u32[]{:S(2)}, u32[]{:S(2)}) collective-permute-start(f32[136,128]{1,0:T(8,128)S(1)} %add.11.refs_0_), channel_id=1, source_target_pairs={{0,16},{1,17},{2,18},{3,19},{4,20},{5,21},{6,22},{7,23},{8,24},{9,... | collective-permute-start | bytes 208904 | tf_op jit(solution)/shard_map/ppermute | solution.py:361
  104.4 13.4 %collective-permute-start.28 = (f32[512,256]{1,0:T(8,128)S(1)}, f32[512,256]{1,0:T(8,128)S(1)}, u32[]{:S(2)}, u32[]{:S(2)}) collective-permute-start(f32[512,256]{1,0:T(8,128)S(1)} %get-tuple-element.91), channel_id=1, source_target_pairs={{0,4},{1,0},{2,6},{3,2},{4,5},{5,1},{6,7},{7,3},{8,12},{9,8},{10,1... | collective-permute-start | bytes 1572872 | tf_op jit(solution)/shard_map/ppermute | solution.py:361
  104.4 16.1 %collective-permute-start.29 = (f32[512,256]{1,0:T(8,128)S(1)}, f32[512,256]{1,0:T(8,128)S(1)}, u32[]{:S(2)}, u32[]{:S(2)}) collective-permute-start(f32[512,256]{1,0:T(8,128)S(1)} %get-tuple-element.92), channel_id=1, source_target_pairs={{1,4},{3,6},{4,1},{6,3},{9,12},{11,14},{12,9},{14,11},{17,20},{19,... | collective-permute-start | bytes 1572872 | tf_op jit(solution)/shard_map/ppermute | solution.py:361
  108.9 20.7 %collective-permute-start.35 = (f32[136,896]{1,0:T(8,128)S(1)}, f32[136,896]{1,0:T(8,128)S(1)}, u32[]{:S(2)}, u32[]{:S(2)}) collective-permute-start(f32[136,896]{1,0:T(8,128)S(1)} %collect.1.own), channel_id=1, source_target_pairs={{1,4},{3,6},{4,1},{6,3},{9,12},{11,14},{12,9},{14,11},{17,20},{19,... | collective-permute-start | bytes 1462280 | tf_op jit(solution)/shard_map/ppermute | solution.py:361
  110.9 18.7 %collective-permute-start.34 = (f32[136,896]{1,0:T(8,128)S(1)}, f32[136,896]{1,0:T(8,128)S(1)}, u32[]{:S(2)}, u32[]{:S(2)}) collective-permute-start(f32[136,896]{1,0:T(8,128)S(1)} %collect.1.own), channel_id=1, source_target_pairs={{0,4},{1,0},{2,6},{3,2},{4,5},{5,1},{6,7},{7,3},{8,12},{9,8},{10,1... | collective-permute-start | bytes 1462280 | tf_op jit(solution)/shard_map/ppermute | solution.py:361
  (11 other events, 8.3 us)

commit v6 on v5

--- a/solution.py
+++ b/solution.py
@@ -391,7 +391,7 @@
         beside, *tops = tie(beside, *tops)
         kept1, give1 = call(pack_one, [block] * 2, [factor_one, pattern_one, size_one], scalars=2, name="pack_one")
         near1, far1 = send(give1, to_worker), send(kept1, across)
-        factor_two, near1, far1 = tie(factor_two, near1, far1)
+        factor_two, _ = tie(factor_two, give1)
         kept2, give2 = call(
             pack_two,
             [block] * 2,

time: 133 us -> 132 us (level)
  the two profiles are of different devices: /device:TPU:22 before, /device:TPU:1 now
where the time goes in v6:
time: 132 us; the launch traced here: 131 us
  starting transfers between devices  69.1 us (52%)
  waiting for transfers between devices  34.5 us (26%)
  Pallas kernels  15.4 us (12%)
  local copies, waits for them, and re-layouts  10.5 us (8%)
    ppermute x36, starting transfers between devices, send(): return lax.ppermute(value, AXES, perm)  69.1 us
    ppermute x36, waiting for transfers between devices, send(): return lax.ppermute(value, AXES, perm)  34.5 us
    pallas_call x12, Pallas kernels, call(): pl.pallas_call(body, out_shape=outs, in_specs=specs, out_specs=[VMEM] * l...  14.3 us
    unnamed x46, local copies, waits for them, and re-layouts  10.5 us
  transfers between devices with their start and end apart: 36, of which 10 were waited for; matrix products, arithmetic and copies ran while one was open for 0% of the time, Pallas kernels for 6%

profile of v6, /device:TPU:1, one launch (start us, length us, event | category | flops | bytes accessed | tf_op | source)
XLA Modules:
  0.0 130.9 jit_solution(3682815507477423225)
XLA Ops:
  0.7 1.1 copy-done.2
  3.1 0.8 pack_one.1
  3.9 2.1 %collective-permute-start = (f32[256,256]{1,0:T(8,128)S(1)}, f32[256,256]{1,0:T(8,128)S(1)}, u32[]{:S(2)}, u32[]{:S(2)}) collective-permute-start(f32[256,256]{1,0:T(8,128)S(1)} %get-tuple-element.51), channel_id=1, source_target_pairs={{0,1},{1,5},{2,3},{3,7},{4,0},{5,4},{6,2},{7,6},{8,9},{9,13},{10,1... | collective-permute-start | bytes 786440 | tf_op jit(solution)/shard_map/ppermute | solution.py:361
  6.0 2.5 %collective-permute-start.1 = (f32[256,256]{1,0:T(8,128)S(1)}, f32[256,256]{1,0:T(8,128)S(1)}, u32[]{:S(2)}, u32[]{:S(2)}) collective-permute-start(f32[256,256]{1,0:T(8,128)S(1)} %get-tuple-element.52.kept_ref), channel_id=1, source_target_pairs={{1,4},{3,6},{4,1},{6,3},{9,12},{11,14},{12,9},{14,11},{17,20},{19,... | collective-permute-start | bytes 786440 | tf_op jit(solution)/shard_map/ppermute | solution.py:361
  8.5 1.8 %collective-permute-start.7 = (f32[256,512]{1,0:T(8,128)}, f32[256,512]{1,0:T(8,128)S(1)}, u32[]{:S(2)}, u32[]{:S(2)}) collective-permute-start(f32[256,512]{1,0:T(8,128)} %refs_0_.1), channel_id=1, source_target_pairs={{0,2},{1,3},{2,0},{3,1},{4,6},{5,7},{6,4},{7,5},{8,10},{9,11},{10,... | collective-permute-start | bytes 1572872 | tf_op jit(solution)/shard_map/ppermute | solution.py:361
  10.2 1.0 copy-done.3
  14.0 0.9 pack_two.1
  15.0 1.3 collective-permute-start.5
  16.3 1.5 %collective-permute-start.2 = (f32[256,256]{1,0:T(8,128)S(1)}, f32[256,256]{1,0:T(8,128)S(1)}, u32[]{:S(2)}, u32[]{:S(2)}) collective-permute-start(f32[256,256]{1,0:T(8,128)S(1)} %get-tuple-element.57), channel_id=1, source_target_pairs={{0,1},{1,5},{2,3},{3,7},{4,0},{5,4},{6,2},{7,6},{8,9},{9,13},{10,1... | collective-permute-start | bytes 786440 | tf_op jit(solution)/shard_map/ppermute | solution.py:361
  17.8 3.4 %collective-permute-start.3 = (f32[256,256]{1,0:T(8,128)S(1)}, f32[256,256]{1,0:T(8,128)S(1)}, u32[]{:S(2)}, u32[]{:S(2)}) collective-permute-start(f32[256,256]{1,0:T(8,128)S(1)} %get-tuple-element.56.kept_ref), channel_id=1, source_target_pairs={{1,4},{3,6},{4,1},{6,3},{9,12},{11,14},{12,9},{14,11},{17,20},{19,... | collective-permute-start | bytes 786440 | tf_op jit(solution)/shard_map/ppermute | solution.py:361
  21.2 4.3 %collective-permute-start.4 = (f32[256,512]{1,0:T(8,128)S(1)}, f32[256,512]{1,0:T(8,128)S(1)}, u32[]{:S(2)}, u32[]{:S(2)}) collective-permute-start(f32[256,512]{1,0:T(8,128)S(1)} %join_one.1.refs_0_.refs_4_), channel_id=1, source_target_pairs={{0,8},{1,9},{2,10},{3,11},{4,12},{5,13},{6,14},{7,15},{8,16},{9,17... | collective-permute-start | bytes 1572872 | tf_op jit(solution)/shard_map/ppermute | solution.py:361
  26.9 1.4 %collective-permute-start.10 = (f32[160,512]{1,0:T(8,128)S(1)}, f32[160,512]{1,0:T(8,128)S(1)}, u32[]{:S(2)}, u32[]{:S(2)}) collective-permute-start(f32[160,512]{1,0:T(8,128)S(1)} %slice.6), channel_id=1, source_target_pairs={{0,2},{1,3},{2,0},{3,1},{4,6},{5,7},{6,4},{7,5},{8,10},{9,11},{10,... | collective-permute-start | bytes 983048 | tf_op jit(solution)/shard_map/ppermute | solution.py:361
  28.2 4.7 %collective-permute-done.3.far_ref = f32[256,256]{1,0:T(8,128)S(1)} collective-permute-done((f32[256,256]{1,0:T(8,128)S(1)}, f32[256,256]{1,0:T(8,128)S(1)}, u32[]{:S(2)}, u32[]{:S(2)}) %collective-permute-start.3) | collective-permute-done | bytes 262176 | tf_op jit(solution)/shard_map/ppermute | solution.py:361
  32.9 0.7 copy-done.9
  33.6 1.9 %collective-permute-start.9 = (f32[256,512]{1,0:T(8,128)S(1)}, f32[256,512]{1,0:T(8,128)}, u32[]{:S(2)}, u32[]{:S(2)}) collective-permute-start(f32[256,512]{1,0:T(8,128)S(1)} %collective-permute-done.6.refs_1_), channel_id=1, source_target_pairs={{0,1},{1,0},{2,3},{3,2},{4,5},{5,4},{6,7},{7,6},{8,9},{9,8},{10,11... | collective-permute-start | bytes 1572872 | tf_op jit(solution)/shard_map/ppermute | solution.py:361
  35.5 1.4 %collective-permute-start.13 = (f32[160,512]{1,0:T(8,128)S(1)}, f32[160,512]{1,0:T(8,128)}, u32[]{:S(2)}, u32[]{:S(2)}) collective-permute-start(f32[160,512]{1,0:T(8,128)S(1)} %collective-permute-done.10.refs_5_), channel_id=1, source_target_pairs={{0,1},{1,0},{2,3},{3,2},{4,5},{5,4},{6,7},{7,6},{8,9},{9,8},{10,11... | collective-permute-start | bytes 983048 | tf_op jit(solution)/shard_map/ppermute | solution.py:361
  37.1 0.9 copy-done.6
  38.0 0.9 copy-done.8
  39.0 0.9 copy-done.10
  40.0 3.9 %partial_products.1 = (f32[256,2048]{1,0:T(8,128)S(1)}, bf16[512,2048]{1,0:T(8,128)(2,1)S(1)}, bf16[512,2048]{1,0:T(8,128)(2,1)S(1)}) custom-call(f32[256,512]{1,0:T(8,128)S(1)} %join_two.1.w2_ref.refs_5_, f32[256,512]{1,0:T(8,128)S(1)} %copy-done.1, f32[256,512]{1,0:T(8,128)S(1)} %collective-permute-done.6.refs_1_, ...), custom_call_target="tpu_custom_call" | custom-call | tf_op jit(solution)/shard_map/partial_products/pallas_call | solution.py:320
  44.1 3.3 %collective-permute-start.15 = (f32[128,512]{1,0:T(8,128)S(1)}, f32[128,512]{1,0:T(8,128)S(1)}, u32[]{:S(2)}, u32[]{:S(2)}) collective-permute-start(f32[128,512]{1,0:T(8,128)S(1)} %get-tuple-element.69), channel_id=1, source_target_pairs={{0,8},{1,9},{2,10},{3,11},{4,12},{5,13},{6,14},{7,15},{8,16},{9,17... | collective-permute-start | bytes 786440 | tf_op jit(solution)/shard_map/ppermute | solution.py:361
  47.4 1.3 collective-permute-start.17
  48.8 4.0 %collective-permute-start.16 = (f32[128,512]{1,0:T(8,128)S(1)}, f32[128,512]{1,0:T(8,128)S(1)}, u32[]{:S(2)}, u32[]{:S(2)}) collective-permute-start(f32[128,512]{1,0:T(8,128)S(1)} %get-tuple-element.70), channel_id=1, source_target_pairs={{0,8},{1,9},{2,10},{3,11},{4,12},{5,13},{6,14},{7,15},{8,16},{9,17... | collective-permute-start | bytes 786440 | tf_op jit(solution)/shard_map/ppermute | solution.py:361
  52.8 1.3 collective-permute-start.18
  54.1 2.3 %collective-permute-done.17.refs_2_.refs_1_ = f32[128,512]{1,0:T(8,128)S(1)} collective-permute-done((f32[128,512]{1,0:T(8,128)S(1)}, f32[128,512]{1,0:T(8,128)S(1)}, u32[]{:S(2)}, u32[]{:S(2)}) %collective-permute-start.17) | collective-permute-done | bytes 262176 | tf_op jit(solution)/shard_map/ppermute | solution.py:361
  56.5 3.4 %collective-permute-start.19 = (f32[128,512]{1,0:T(8,128)S(1)}, f32[128,512]{1,0:T(8,128)S(1)}, u32[]{:S(2)}, u32[]{:S(2)}) collective-permute-start(f32[128,512]{1,0:T(8,128)S(1)} %get-tuple-element.73), channel_id=1, source_target_pairs={{0,8},{1,9},{2,10},{3,11},{4,12},{5,13},{6,14},{7,15},{8,16},{9,17... | collective-permute-start | bytes 786440 | tf_op jit(solution)/shard_map/ppermute | solution.py:361
  59.9 1.3 collective-permute-start.21
  61.7 3.6 %collective-permute-start.20 = (f32[128,512]{1,0:T(8,128)S(1)}, f32[128,512]{1,0:T(8,128)S(1)}, u32[]{:S(2)}, u32[]{:S(2)}) collective-permute-start(f32[128,512]{1,0:T(8,128)S(1)} %get-tuple-element.74), channel_id=1, source_target_pairs={{0,8},{1,9},{2,10},{3,11},{4,12},{5,13},{6,14},{7,15},{8,16},{9,17... | collective-permute-start | bytes 786440 | tf_op jit(solution)/shard_map/ppermute | solution.py:361
  65.3 1.3 collective-permute-start.22
  66.6 1.0 collective-permute-done.21.refs_2_.refs_1_
  67.7 3.1 %collective-permute-start.24 = (f32[128,512]{1,0:T(8,128)S(1)}, f32[128,512]{1,0:T(8,128)S(1)}, u32[]{:S(2)}, u32[]{:S(2)}) collective-permute-start(f32[128,512]{1,0:T(8,128)S(1)} %get-tuple-element.79), channel_id=1, source_target_pairs={{0,8},{1,9},{2,10},{3,11},{4,12},{5,13},{6,14},{7,15},{8,16},{9,17... | collective-permute-start | bytes 786440 | tf_op jit(solution)/shard_map/ppermute | solution.py:361
  70.8 1.3 collective-permute-start.25
  74.1 1.4 %gram_products.1 = (f32[256,512]{1,0:T(8,128)S(1)}, f32[136,384]{1,0:T(8,128)S(1)}, f32[136,384]{1,0:T(8,128)S(1)}) custom-call(bf16[512,2048]{1,0:T(8,128)(2,1)S(1)} %get-tuple-element.65.high_ref, bf16[512,2048]{1,0:T(8,128)(2,1)S(1)} %get-tuple-element.66.low_ref, f32[256,512]{1,0:T(8,128)S(1)} %next_product.3.before_ref, ...), custom_call_target="tpu_custom_call" | custom-call | tf_op jit(solution)/shard_map/gram_products/pallas_call | solution.py:320
  75.5 2.1 %collective-permute-start.23 = (f32[136,384]{1,0:T(8,128)S(1)}, f32[136,384]{1,0:T(8,128)S(1)}, u32[]{:S(2)}, u32[]{:S(2)}) collective-permute-start(f32[136,384]{1,0:T(8,128)S(1)} %get-tuple-element.78), channel_id=1, source_target_pairs={{0,8},{1,9},{2,10},{3,11},{4,12},{5,13},{6,14},{7,15},{8,0},{9,1},... | collective-permute-start | bytes 626696 | tf_op jit(solution)/shard_map/ppermute | solution.py:361
  77.8 2.0 %collective-permute-start.26 = (f32[128,512]{1,0:T(8,128)S(1)}, f32[128,512]{1,0:T(8,128)S(1)}, u32[]{:S(2)}, u32[]{:S(2)}) collective-permute-start(f32[128,512]{1,0:T(8,128)S(1)} %get-tuple-element.82), channel_id=1, source_target_pairs={{0,8},{1,9},{2,10},{3,11},{4,12},{5,13},{6,14},{7,15},{8,16},{9,17... | collective-permute-start | bytes 786440 | tf_op jit(solution)/shard_map/ppermute | solution.py:361
  79.7 1.3 collective-permute-start.27
  81.0 2.1 %collective-permute-done.23 = f32[136,384]{1,0:T(8,128)S(1)} collective-permute-done((f32[136,384]{1,0:T(8,128)S(1)}, f32[136,384]{1,0:T(8,128)S(1)}, u32[]{:S(2)}, u32[]{:S(2)}) %collective-permute-start.23) | collective-permute-done | bytes 208928 | tf_op jit(solution)/shard_map/ppermute | solution.py:361
  83.1 1.6 %collective-permute-start.30 = (f32[136,384]{1,0:T(8,128)S(1)}, f32[136,384]{1,0:T(8,128)S(1)}, u32[]{:S(2)}, u32[]{:S(2)}) collective-permute-start(f32[136,384]{1,0:T(8,128)S(1)} %add.10), channel_id=1, source_target_pairs={{0,16},{1,17},{2,18},{3,19},{4,20},{5,21},{6,22},{7,23},{8,24},{9,... | collective-permute-start | bytes 626696 | tf_op jit(solution)/shard_map/ppermute | solution.py:361
  84.7 6.9 %collective-permute-done.27.refs_4_ = f32[128,512]{1,0:T(8,128)S(1)} collective-permute-done((f32[128,512]{1,0:T(8,128)S(1)}, f32[128,512]{1,0:T(8,128)S(1)}, u32[]{:S(2)}, u32[]{:S(2)}) %collective-permute-start.27) | collective-permute-done | bytes 262176 | tf_op jit(solution)/shard_map/ppermute | solution.py:361
  92.4 4.0 %collective-permute-done.31 = f32[136,128]{1,0:T(8,128)S(1)} collective-permute-done((f32[136,128]{1,0:T(8,128)S(1)}, f32[136,128]{1,0:T(8,128)S(1)}, u32[]{:S(2)}, u32[]{:S(2)}) %collective-permute-start.31) | collective-permute-done | bytes 69664 | tf_op jit(solution)/shard_map/ppermute | solution.py:361
  96.5 1.7 %collective-permute-start.33 = (f32[136,128]{1,0:T(8,128)S(1)}, f32[136,128]{1,0:T(8,128)S(1)}, u32[]{:S(2)}, u32[]{:S(2)}) collective-permute-start(f32[136,128]{1,0:T(8,128)S(1)} %add.11.refs_0_), channel_id=1, source_target_pairs={{0,16},{1,17},{2,18},{3,19},{4,20},{5,21},{6,22},{7,23},{8,24},{9,... | collective-permute-start | bytes 208904 | tf_op jit(solution)/shard_map/ppermute | solution.py:361
  98.2 5.6 %collective-permute-start.28 = (f32[512,256]{1,0:T(8,128)S(1)}, f32[512,256]{1,0:T(8,128)S(1)}, u32[]{:S(2)}, u32[]{:S(2)}) collective-permute-start(f32[512,256]{1,0:T(8,128)S(1)} %get-tuple-element.87), channel_id=1, source_target_pairs={{0,4},{1,0},{2,6},{3,2},{4,5},{5,1},{6,7},{7,3},{8,12},{9,8},{10,1... | collective-permute-start | bytes 1572872 | tf_op jit(solution)/shard_map/ppermute | solution.py:361
  103.9 3.2 %collective-permute-start.29 = (f32[512,256]{1,0:T(8,128)S(1)}, f32[512,256]{1,0:T(8,128)S(1)}, u32[]{:S(2)}, u32[]{:S(2)}) collective-permute-start(f32[512,256]{1,0:T(8,128)S(1)} %get-tuple-element.88), channel_id=1, source_target_pairs={{1,4},{3,6},{4,1},{6,3},{9,12},{11,14},{12,9},{14,11},{17,20},{19,... | collective-permute-start | bytes 1572872 | tf_op jit(solution)/shard_map/ppermute | solution.py:361
  107.1 5.9 %collective-permute-start.35 = (f32[136,896]{1,0:T(8,128)S(1)}, f32[136,896]{1,0:T(8,128)S(1)}, u32[]{:S(2)}, u32[]{:S(2)}) collective-permute-start(f32[136,896]{1,0:T(8,128)S(1)} %collect.1.own), channel_id=1, source_target_pairs={{1,4},{3,6},{4,1},{6,3},{9,12},{11,14},{12,9},{14,11},{17,20},{19,... | collective-permute-start | bytes 1462280 | tf_op jit(solution)/shard_map/ppermute | solution.py:361
  113.1 5.7 %collective-permute-done.29.far = f32[512,256]{1,0:T(8,128)S(1)} collective-permute-done((f32[512,256]{1,0:T(8,128)S(1)}, f32[512,256]{1,0:T(8,128)S(1)}, u32[]{:S(2)}, u32[]{:S(2)}) %collective-permute-start.29) | collective-permute-done | bytes 524320 | tf_op jit(solution)/shard_map/ppermute | solution.py:361
  118.8 2.2 %finish_rows.1 = (f32[256,512]{1,0:T(8,128)}, f32[256,512]{1,0:T(8,128)}) custom-call(f32[512,256]{1,0:T(8,128)S(1)} %get-tuple-element.86.own, f32[512,256]{1,0:T(8,128)S(1)} %collective-permute-done.28.near, f32[512,256]{1,0:T(8,128)S(1)} %collective-permute-done.29.far, f32[4,256,128]{2,1,0:T(8,128)S(1)} %copy-done, s32[8,8]{1,0:T(8,128)S(1)} %copy-done.14, ...), custom_call_target="tpu_custom_call" | custom-call | tf_op jit(solution)/shard_map/finish_rows/pallas_call | solution.py:320
  121.0 6.9 %collective-permute-done.35.far = f32[136,896]{1,0:T(8,128)S(1)} collective-permute-done((f32[136,896]{1,0:T(8,128)S(1)}, f32[136,896]{1,0:T(8,128)S(1)}, u32[]{:S(2)}, u32[]{:S(2)}) %collective-permute-start.35) | collective-permute-done | bytes 487456 | tf_op jit(solution)/shard_map/ppermute | solution.py:361
  127.9 3.0 %finish_blocks.1 = (f32[2,256,256]{2,1,0:T(8,128)}, f32[4,256,128]{2,1,0:T(8,128)}, f32[4,128,128]{2,1,0:T(8,128)}) custom-call(f32[136,896]{1,0:T(8,128)S(1)} %collect.1.own, f32[136,896]{1,0:T(8,128)S(1)} %collective-permute-done.34.near, f32[136,896]{1,0:T(8,128)S(1)} %collective-permute-done.35.far, f32[2,256,256]{2,1,0:T(8,128)S(1)} %copy-done.4, ...), custom_call_target="tpu_custom_call" | custom-call | tf_op jit(solution)/shard_map/finish_blocks/pallas_call | solution.py:320
  (94 shorter events, 9.5 us)
Async XLA Ops:
  0.6 33.0 %copy-start.1 = (f32[256,512]{1,0:T(8,128)S(1)}, f32[256,512]{1,0:T(8,128)}, u32[]{:S(2)}) copy-start(f32[256,512]{1,0:T(8,128)} %refs_0_.1) | copy-start | bytes 1572868
  0.6 1.1 copy-start.2
  3.9 11.0 %collective-permute-start = (f32[256,256]{1,0:T(8,128)S(1)}, f32[256,256]{1,0:T(8,128)S(1)}, u32[]{:S(2)}, u32[]{:S(2)}) collective-permute-start(f32[256,256]{1,0:T(8,128)S(1)} %get-tuple-element.51), channel_id=1, source_target_pairs={{0,1},{1,5},{2,3},{3,7},{4,0},{5,4},{6,2},{7,6},{8,9},{9,13},{10,1... | collective-permute-start | bytes 786440 | tf_op jit(solution)/shard_map/ppermute | solution.py:361
  6.0 8.9 %collective-permute-start.1 = (f32[256,256]{1,0:T(8,128)S(1)}, f32[256,256]{1,0:T(8,128)S(1)}, u32[]{:S(2)}, u32[]{:S(2)}) collective-permute-start(f32[256,256]{1,0:T(8,128)S(1)} %get-tuple-element.52.kept_ref), channel_id=1, source_target_pairs={{1,4},{3,6},{4,1},{6,3},{9,12},{11,14},{12,9},{14,11},{17,20},{19,... | collective-permute-start | bytes 786440 | tf_op jit(solution)/shard_map/ppermute | solution.py:361
  8.5 12.7 %collective-permute-start.7 = (f32[256,512]{1,0:T(8,128)}, f32[256,512]{1,0:T(8,128)S(1)}, u32[]{:S(2)}, u32[]{:S(2)}) collective-permute-start(f32[256,512]{1,0:T(8,128)} %refs_0_.1), channel_id=1, source_target_pairs={{0,2},{1,3},{2,0},{3,1},{4,6},{5,7},{6,4},{7,5},{8,10},{9,11},{10,... | collective-permute-start | bytes 1572872 | tf_op jit(solution)/shard_map/ppermute | solution.py:361
  10.2 15.3 %collective-permute-start.6 = (f32[256,512]{1,0:T(8,128)}, f32[256,512]{1,0:T(8,128)S(1)}, u32[]{:S(2)}, u32[]{:S(2)}) collective-permute-start(f32[256,512]{1,0:T(8,128)} %refs_0_.1), channel_id=1, source_target_pairs={{0,4},{1,5},{2,6},{3,7},{4,0},{5,1},{6,2},{7,3},{8,12},{9,13},{10,... | collective-permute-start | bytes 1572872 | tf_op jit(solution)/shard_map/ppermute | solution.py:361
  10.2 1.0 copy-start.3
  14.9 22.1 %copy-start.5 = (f32[256,256]{1,0:T(8,128)}, f32[256,256]{1,0:T(8,128)S(1)}, u32[]{:S(2)}) copy-start(f32[256,256]{1,0:T(8,128)S(1)} %get-tuple-element.56.kept_ref) | copy-start | bytes 786436
  15.0 20.5 %collective-permute-start.5 = (f32[256,512]{1,0:T(8,128)S(1)}, f32[256,512]{1,0:T(8,128)S(1)}, u32[]{:S(2)}, u32[]{:S(2)}) collective-permute-start(f32[256,512]{1,0:T(8,128)S(1)} %join_one.1.refs_0_.refs_4_), channel_id=1, source_target_pairs={{8,0},{9,1},{10,2},{11,3},{12,4},{13,5},{14,6},{15,7},{16,8},{17,9... | collective-permute-start | bytes 1572872 | tf_op jit(solution)/shard_map/ppermute | solution.py:361
  16.3 9.9 %collective-permute-start.2 = (f32[256,256]{1,0:T(8,128)S(1)}, f32[256,256]{1,0:T(8,128)S(1)}, u32[]{:S(2)}, u32[]{:S(2)}) collective-permute-start(f32[256,256]{1,0:T(8,128)S(1)} %get-tuple-element.57), channel_id=1, source_target_pairs={{0,1},{1,5},{2,3},{3,7},{4,0},{5,4},{6,2},{7,6},{8,9},{9,13},{10,1... | collective-permute-start | bytes 786440 | tf_op jit(solution)/shard_map/ppermute | solution.py:361
  17.8 15.1 %collective-permute-start.3 = (f32[256,256]{1,0:T(8,128)S(1)}, f32[256,256]{1,0:T(8,128)S(1)}, u32[]{:S(2)}, u32[]{:S(2)}) collective-permute-start(f32[256,256]{1,0:T(8,128)S(1)} %get-tuple-element.56.kept_ref), channel_id=1, source_target_pairs={{1,4},{3,6},{4,1},{6,3},{9,12},{11,14},{12,9},{14,11},{17,20},{19,... | collective-permute-start | bytes 786440 | tf_op jit(solution)/shard_map/ppermute | solution.py:361
  21.2 15.8 %collective-permute-start.4 = (f32[256,512]{1,0:T(8,128)S(1)}, f32[256,512]{1,0:T(8,128)S(1)}, u32[]{:S(2)}, u32[]{:S(2)}) collective-permute-start(f32[256,512]{1,0:T(8,128)S(1)} %join_one.1.refs_0_.refs_4_), channel_id=1, source_target_pairs={{0,8},{1,9},{2,10},{3,11},{4,12},{5,13},{6,14},{7,15},{8,16},{9,17... | collective-permute-start | bytes 1572872 | tf_op jit(solution)/shard_map/ppermute | solution.py:361
  25.6 8.1 %collective-permute-start.11 = (f32[96,512]{1,0:T(8,128)S(1)}, f32[96,512]{1,0:T(8,128)}, u32[]{:S(2)}, u32[]{:S(2)}) collective-permute-start(f32[96,512]{1,0:T(8,128)S(1)} %slice.7), channel_id=1, source_target_pairs={{0,4},{1,5},{2,6},{3,7},{4,0},{5,1},{6,2},{7,3},{8,12},{9,13},{10,... | collective-permute-start | bytes 589832 | tf_op jit(solution)/shard_map/ppermute | solution.py:361
  26.9 8.7 %collective-permute-start.10 = (f32[160,512]{1,0:T(8,128)S(1)}, f32[160,512]{1,0:T(8,128)S(1)}, u32[]{:S(2)}, u32[]{:S(2)}) collective-permute-start(f32[160,512]{1,0:T(8,128)S(1)} %slice.6), channel_id=1, source_target_pairs={{0,2},{1,3},{2,0},{3,1},{4,6},{5,7},{6,4},{7,5},{8,10},{9,11},{10,... | collective-permute-start | bytes 983048 | tf_op jit(solution)/shard_map/ppermute | solution.py:361
  33.6 6.3 %collective-permute-start.8 = (f32[256,512]{1,0:T(8,128)S(1)}, f32[256,512]{1,0:T(8,128)}, u32[]{:S(2)}, u32[]{:S(2)}) collective-permute-start(f32[256,512]{1,0:T(8,128)S(1)} %copy-done.1), channel_id=1, source_target_pairs={{0,1},{1,0},{2,3},{3,2},{4,5},{5,4},{6,7},{7,6},{8,9},{9,8},{10,11... | collective-permute-start | bytes 1572872 | tf_op jit(solution)/shard_map/ppermute | solution.py:361
  33.6 6.3 %collective-permute-start.9 = (f32[256,512]{1,0:T(8,128)S(1)}, f32[256,512]{1,0:T(8,128)}, u32[]{:S(2)}, u32[]{:S(2)}) collective-permute-start(f32[256,512]{1,0:T(8,128)S(1)} %collective-permute-done.6.refs_1_), channel_id=1, source_target_pairs={{0,1},{1,0},{2,3},{3,2},{4,5},{5,4},{6,7},{7,6},{8,9},{9,8},{10,11... | collective-permute-start | bytes 1572872 | tf_op jit(solution)/shard_map/ppermute | solution.py:361
  35.5 4.5 %collective-permute-start.12 = (f32[256,512]{1,0:T(8,128)S(1)}, f32[256,512]{1,0:T(8,128)}, u32[]{:S(2)}, u32[]{:S(2)}) collective-permute-start(f32[256,512]{1,0:T(8,128)S(1)} %collective-permute-done.7.refs_4_), channel_id=1, source_target_pairs={{0,1},{1,0},{2,3},{3,2},{4,5},{5,4},{6,7},{7,6},{8,9},{9,8},{10,11... | collective-permute-start | bytes 1572872 | tf_op jit(solution)/shard_map/ppermute | solution.py:361
  35.5 4.5 %collective-permute-start.13 = (f32[160,512]{1,0:T(8,128)S(1)}, f32[160,512]{1,0:T(8,128)}, u32[]{:S(2)}, u32[]{:S(2)}) collective-permute-start(f32[160,512]{1,0:T(8,128)S(1)} %collective-permute-done.10.refs_5_), channel_id=1, source_target_pairs={{0,1},{1,0},{2,3},{3,2},{4,5},{5,4},{6,7},{7,6},{8,9},{9,8},{10,11... | collective-permute-start | bytes 983048 | tf_op jit(solution)/shard_map/ppermute | solution.py:361
  37.0 3.0 %collective-permute-start.14 = (f32[96,512]{1,0:T(8,128)}, f32[96,512]{1,0:T(8,128)}, u32[]{:S(2)}, u32[]{:S(2)}) collective-permute-start(f32[96,512]{1,0:T(8,128)} %collective-permute-done.11.refs_6_), channel_id=1, source_target_pairs={{0,1},{1,0},{2,3},{3,2},{4,5},{5,4},{6,7},{7,6},{8,9},{9,8},{10,11... | collective-permute-start | bytes 589832 | tf_op jit(solution)/shard_map/ppermute | solution.py:361
  44.1 10.1 %collective-permute-start.15 = (f32[128,512]{1,0:T(8,128)S(1)}, f32[128,512]{1,0:T(8,128)S(1)}, u32[]{:S(2)}, u32[]{:S(2)}) collective-permute-start(f32[128,512]{1,0:T(8,128)S(1)} %get-tuple-element.69), channel_id=1, source_target_pairs={{0,8},{1,9},{2,10},{3,11},{4,12},{5,13},{6,14},{7,15},{8,16},{9,17... | collective-permute-start | bytes 786440 | tf_op jit(solution)/shard_map/ppermute | solution.py:361
  47.4 9.0 %collective-permute-start.17 = (f32[128,512]{1,0:T(8,128)S(1)}, f32[128,512]{1,0:T(8,128)S(1)}, u32[]{:S(2)}, u32[]{:S(2)}) collective-permute-start(f32[128,512]{1,0:T(8,128)S(1)} %get-tuple-element.71), channel_id=1, source_target_pairs={{8,0},{9,1},{10,2},{11,3},{12,4},{13,5},{14,6},{15,7},{16,8},{17,9... | collective-permute-start | bytes 786440 | tf_op jit(solution)/shard_map/ppermute | solution.py:361
  48.8 12.4 %collective-permute-start.16 = (f32[128,512]{1,0:T(8,128)S(1)}, f32[128,512]{1,0:T(8,128)S(1)}, u32[]{:S(2)}, u32[]{:S(2)}) collective-permute-start(f32[128,512]{1,0:T(8,128)S(1)} %get-tuple-element.70), channel_id=1, source_target_pairs={{0,8},{1,9},{2,10},{3,11},{4,12},{5,13},{6,14},{7,15},{8,16},{9,17... | collective-permute-start | bytes 786440 | tf_op jit(solution)/shard_map/ppermute | solution.py:361
  52.8 8.8 %collective-permute-start.18 = (f32[128,512]{1,0:T(8,128)S(1)}, f32[128,512]{1,0:T(8,128)S(1)}, u32[]{:S(2)}, u32[]{:S(2)}) collective-permute-start(f32[128,512]{1,0:T(8,128)S(1)} %get-tuple-element.72), channel_id=1, source_target_pairs={{8,0},{9,1},{10,2},{11,3},{12,4},{13,5},{14,6},{15,7},{16,8},{17,9... | collective-permute-start | bytes 786440 | tf_op jit(solution)/shard_map/ppermute | solution.py:361
  56.5 10.1 %collective-permute-start.19 = (f32[128,512]{1,0:T(8,128)S(1)}, f32[128,512]{1,0:T(8,128)S(1)}, u32[]{:S(2)}, u32[]{:S(2)}) collective-permute-start(f32[128,512]{1,0:T(8,128)S(1)} %get-tuple-element.73), channel_id=1, source_target_pairs={{0,8},{1,9},{2,10},{3,11},{4,12},{5,13},{6,14},{7,15},{8,16},{9,17... | collective-permute-start | bytes 786440 | tf_op jit(solution)/shard_map/ppermute | solution.py:361
  59.9 7.7 %collective-permute-start.21 = (f32[128,512]{1,0:T(8,128)S(1)}, f32[128,512]{1,0:T(8,128)S(1)}, u32[]{:S(2)}, u32[]{:S(2)}) collective-permute-start(f32[128,512]{1,0:T(8,128)S(1)} %get-tuple-element.75), channel_id=1, source_target_pairs={{8,0},{9,1},{10,2},{11,3},{12,4},{13,5},{14,6},{15,7},{16,8},{17,9... | collective-permute-start | bytes 786440 | tf_op jit(solution)/shard_map/ppermute | solution.py:361
  61.7 12.4 %collective-permute-start.20 = (f32[128,512]{1,0:T(8,128)S(1)}, f32[128,512]{1,0:T(8,128)S(1)}, u32[]{:S(2)}, u32[]{:S(2)}) collective-permute-start(f32[128,512]{1,0:T(8,128)S(1)} %get-tuple-element.74), channel_id=1, source_target_pairs={{0,8},{1,9},{2,10},{3,11},{4,12},{5,13},{6,14},{7,15},{8,16},{9,17... | collective-permute-start | bytes 786440 | tf_op jit(solution)/shard_map/ppermute | solution.py:361
  65.3 8.8 %collective-permute-start.22 = (f32[128,512]{1,0:T(8,128)S(1)}, f32[128,512]{1,0:T(8,128)S(1)}, u32[]{:S(2)}, u32[]{:S(2)}) collective-permute-start(f32[128,512]{1,0:T(8,128)S(1)} %get-tuple-element.76), channel_id=1, source_target_pairs={{8,0},{9,1},{10,2},{11,3},{12,4},{13,5},{14,6},{15,7},{16,8},{17,9... | collective-permute-start | bytes 786440 | tf_op jit(solution)/shard_map/ppermute | solution.py:361
  67.7 15.4 %collective-permute-start.24 = (f32[128,512]{1,0:T(8,128)S(1)}, f32[128,512]{1,0:T(8,128)S(1)}, u32[]{:S(2)}, u32[]{:S(2)}) collective-permute-start(f32[128,512]{1,0:T(8,128)S(1)} %get-tuple-element.79), channel_id=1, source_target_pairs={{0,8},{1,9},{2,10},{3,11},{4,12},{5,13},{6,14},{7,15},{8,16},{9,17... | collective-permute-start | bytes 786440 | tf_op jit(solution)/shard_map/ppermute | solution.py:361
  70.8 12.3 %collective-permute-start.25 = (f32[128,512]{1,0:T(8,128)S(1)}, f32[128,512]{1,0:T(8,128)S(1)}, u32[]{:S(2)}, u32[]{:S(2)}) collective-permute-start(f32[128,512]{1,0:T(8,128)S(1)} %get-tuple-element.80), channel_id=1, source_target_pairs={{8,0},{9,1},{10,2},{11,3},{12,4},{13,5},{14,6},{15,7},{16,8},{17,9... | collective-permute-start | bytes 786440 | tf_op jit(solution)/shard_map/ppermute | solution.py:361
  75.5 7.6 %collective-permute-start.23 = (f32[136,384]{1,0:T(8,128)S(1)}, f32[136,384]{1,0:T(8,128)S(1)}, u32[]{:S(2)}, u32[]{:S(2)}) collective-permute-start(f32[136,384]{1,0:T(8,128)S(1)} %get-tuple-element.78), channel_id=1, source_target_pairs={{0,8},{1,9},{2,10},{3,11},{4,12},{5,13},{6,14},{7,15},{8,0},{9,1},... | collective-permute-start | bytes 626696 | tf_op jit(solution)/shard_map/ppermute | solution.py:361
  77.8 7.0 %collective-permute-start.26 = (f32[128,512]{1,0:T(8,128)S(1)}, f32[128,512]{1,0:T(8,128)S(1)}, u32[]{:S(2)}, u32[]{:S(2)}) collective-permute-start(f32[128,512]{1,0:T(8,128)S(1)} %get-tuple-element.82), channel_id=1, source_target_pairs={{0,8},{1,9},{2,10},{3,11},{4,12},{5,13},{6,14},{7,15},{8,16},{9,17... | collective-permute-start | bytes 786440 | tf_op jit(solution)/shard_map/ppermute | solution.py:361
  79.7 11.9 %collective-permute-start.27 = (f32[128,512]{1,0:T(8,128)S(1)}, f32[128,512]{1,0:T(8,128)S(1)}, u32[]{:S(2)}, u32[]{:S(2)}) collective-permute-start(f32[128,512]{1,0:T(8,128)S(1)} %get-tuple-element.84), channel_id=1, source_target_pairs={{8,0},{9,1},{10,2},{11,3},{12,4},{13,5},{14,6},{15,7},{16,8},{17,9... | collective-permute-start | bytes 786440 | tf_op jit(solution)/shard_map/ppermute | solution.py:361
  83.1 13.3 %collective-permute-start.30 = (f32[136,384]{1,0:T(8,128)S(1)}, f32[136,384]{1,0:T(8,128)S(1)}, u32[]{:S(2)}, u32[]{:S(2)}) collective-permute-start(f32[136,384]{1,0:T(8,128)S(1)} %add.10), channel_id=1, source_target_pairs={{0,16},{1,17},{2,18},{3,19},{4,20},{5,21},{6,22},{7,23},{8,24},{9,... | collective-permute-start | bytes 626696 | tf_op jit(solution)/shard_map/ppermute | solution.py:361
  91.6 27.2 %copy-start = (f32[4,256,128]{2,1,0:T(8,128)S(1)}, f32[4,256,128]{2,1,0:T(8,128)}, u32[]{:S(2)}) copy-start(f32[4,256,128]{2,1,0:T(8,128)} %link_ref.3) | copy-start | bytes 1572868
  91.6 27.2 %copy-start.14 = (s32[8,8]{1,0:T(8,128)S(1)}, s32[8,8]{1,0:T(8,128)}, u32[]{:S(2)}) copy-start(s32[8,8]{1,0:T(8,128)} %first_ref.5) | copy-start | bytes 772
  91.6 27.2 %copy-start.16 = (s32[8,16]{1,0:T(8,128)S(1)}, s32[8,16]{1,0:T(8,128)}, u32[]{:S(2)}) copy-start(s32[8,16]{1,0:T(8,128)} %second_ref.3) | copy-start | bytes 1540
  91.6 27.2 %copy-start.18 = (s32[8]{0:T(128)S(1)}, s32[8]{0:T(128)}, u32[]{:S(2)}) copy-start(s32[8]{0:T(128)} %one_ref.3) | copy-start | bytes 100
  91.6 27.2 %copy-start.20 = (s32[16]{0:T(128)S(1)}, s32[16]{0:T(128)}, u32[]{:S(2)}) copy-start(s32[16]{0:T(128)} %parent_ref.5) | copy-start | bytes 196
  91.6 27.2 %copy-start.22 = (s32[16]{0:T(128)S(1)}, s32[16]{0:T(128)}, u32[]{:S(2)}) copy-start(s32[16]{0:T(128)} %two_ref.3) | copy-start | bytes 196
  92.3 35.6 %copy-start.4 = (f32[2,256,256]{2,1,0:T(8,128)S(1)}, f32[2,256,256]{2,1,0:T(8,128)}, u32[]{:S(2)}) copy-start(f32[2,256,256]{2,1,0:T(8,128)} %pivot1_ref.1) | copy-start | bytes 1572868
  92.3 35.6 %copy-start.11 = (f32[4,128,128]{2,1,0:T(8,128)S(1)}, f32[4,128,128]{2,1,0:T(8,128)}, u32[]{:S(2)}) copy-start(f32[4,128,128]{2,1,0:T(8,128)} %pivot2_ref.1) | copy-start | bytes 786436
  92.3 4.1 %collective-permute-start.31 = (f32[136,128]{1,0:T(8,128)S(1)}, f32[136,128]{1,0:T(8,128)S(1)}, u32[]{:S(2)}, u32[]{:S(2)}) collective-permute-start(f32[136,128]{1,0:T(8,128)S(1)} %get-tuple-element.91), channel_id=1, source_target_pairs={{0,8},{1,9},{2,10},{3,11},{4,12},{5,13},{6,14},{7,15},{8,0},{9,1},... | collective-permute-start | bytes 208904 | tf_op jit(solution)/shard_map/ppermute | solution.py:361
  96.4 10.6 %collective-permute-start.32 = (f32[136,384]{1,0:T(8,128)S(1)}, f32[136,384]{1,0:T(8,128)S(1)}, u32[]{:S(2)}, u32[]{:S(2)}) collective-permute-start(f32[136,384]{1,0:T(8,128)S(1)} %add.12.grams_ref), channel_id=1, source_target_pairs={{0,8},{1,9},{2,10},{3,11},{4,12},{5,13},{6,14},{7,15},{8,0},{9,1},... | collective-permute-start | bytes 626696 | tf_op jit(solution)/shard_map/ppermute | solution.py:361
  96.5 10.5 %collective-permute-start.33 = (f32[136,128]{1,0:T(8,128)S(1)}, f32[136,128]{1,0:T(8,128)S(1)}, u32[]{:S(2)}, u32[]{:S(2)}) collective-permute-start(f32[136,128]{1,0:T(8,128)S(1)} %add.11.refs_0_), channel_id=1, source_target_pairs={{0,16},{1,17},{2,18},{3,19},{4,20},{5,21},{6,22},{7,23},{8,24},{9,... | collective-permute-start | bytes 208904 | tf_op jit(solution)/shard_map/ppermute | solution.py:361
  98.2 14.9 %collective-permute-start.28 = (f32[512,256]{1,0:T(8,128)S(1)}, f32[512,256]{1,0:T(8,128)S(1)}, u32[]{:S(2)}, u32[]{:S(2)}) collective-permute-start(f32[512,256]{1,0:T(8,128)S(1)} %get-tuple-element.87), channel_id=1, source_target_pairs={{0,4},{1,0},{2,6},{3,2},{4,5},{5,1},{6,7},{7,3},{8,12},{9,8},{10,1... | collective-permute-start | bytes 1572872 | tf_op jit(solution)/shard_map/ppermute | solution.py:361
  103.9 14.9 %collective-permute-start.29 = (f32[512,256]{1,0:T(8,128)S(1)}, f32[512,256]{1,0:T(8,128)S(1)}, u32[]{:S(2)}, u32[]{:S(2)}) collective-permute-start(f32[512,256]{1,0:T(8,128)S(1)} %get-tuple-element.88), channel_id=1, source_target_pairs={{1,4},{3,6},{4,1},{6,3},{9,12},{11,14},{12,9},{14,11},{17,20},{19,... | collective-permute-start | bytes 1572872 | tf_op jit(solution)/shard_map/ppermute | solution.py:361
  107.1 20.8 %collective-permute-start.35 = (f32[136,896]{1,0:T(8,128)S(1)}, f32[136,896]{1,0:T(8,128)S(1)}, u32[]{:S(2)}, u32[]{:S(2)}) collective-permute-start(f32[136,896]{1,0:T(8,128)S(1)} %collect.1.own), channel_id=1, source_target_pairs={{1,4},{3,6},{4,1},{6,3},{9,12},{11,14},{12,9},{14,11},{17,20},{19,... | collective-permute-start | bytes 1462280 | tf_op jit(solution)/shard_map/ppermute | solution.py:361
  113.1 14.8 %collective-permute-start.34 = (f32[136,896]{1,0:T(8,128)S(1)}, f32[136,896]{1,0:T(8,128)S(1)}, u32[]{:S(2)}, u32[]{:S(2)}) collective-permute-start(f32[136,896]{1,0:T(8,128)S(1)} %collect.1.own), channel_id=1, source_target_pairs={{0,4},{1,0},{2,6},{3,2},{4,5},{5,1},{6,7},{7,3},{8,12},{9,8},{10,1... | collective-permute-start | bytes 1462280 | tf_op jit(solution)/shard_map/ppermute | solution.py:361
  (11 other events, 8.3 us)
